TPU v7x, 32 devices: a whole 2x2x4 slice. The times are simulated.
32 devices in a mesh: blk: 16 (over z, y, core), shard: 2 (over x).
Axes of the slice: x: 2, y: 2, z: 4, core: 2. Of those that a mesh axis runs over, the one named last changes fastest.
Arguments:
- queries: bfloat16 [4096, 1536], P(('blk', 'shard')), may hold values from -16 to 16
- passages: bfloat16 [256, 1536], P(('blk', 'shard')), may hold values from -18 to 18
- neg_pool: bfloat16 [32768, 1536], P(('blk', 'shard')), may hold values from -18 to 18
- hard_ids: int32 [4096, 7], P(('blk', 'shard')), may hold values from 0 to 2047, as said below
- positives: int32 [4096], P(('blk', 'shard')), may hold values from 0 to 255
Outputs:
- query_grad: float32 [4096, 1536], P(('blk', 'shard'))
- passage_grad: float32 [256, 1536], P(('blk', 'shard'))
- pool_grad: float32 [32768, 1536], P(('blk', 'shard'))
Inputs may be any that keep to these rules, and one draw needn't show every extreme that they name: `hard_ids`: entry v names the pool row of the query's own blk index held by the shard index v // 1024. Among the 896 ids of one device's queries at most 597 fall on any one shard index; for every blk index one shard index receives exactly 597 ids from each of the 2 devices of that blk index.
All inputs are finite; a program needn't handle non-finite values.
Results may differ from a plain program's by a relative error of at most 0.0038.
Values may be sent and summed in bfloat16 or wider, within the bound.
No kernel may reach another device: no remote copies, remote signals or barrier semaphores. Data moves between devices by JAX's collectives and lax.ppermute only.
A program may use at most 128 MiB of HBM per device.

v0:
```python
import jax
import jax.numpy as jnp
from jax import lax
from jax.sharding import PartitionSpec as P


def body(queries, passages, neg_pool, hard_ids, positives):
    q_rows, features = queries.shape
    neg_count = hard_ids.shape[1]
    scaling = features ** (-0.5)
    owners = lax.axis_size("shard")
    pool_rows = neg_pool.shape[0]
    requests = q_rows * neg_count
    capacity = min(3 * requests // (2 * owners), 2 * requests // 3)
    my_tile = lax.all_gather(passages, "shard", axis=0, tiled=True)
    flat_ids = hard_ids.reshape(-1)
    owner_of = flat_ids // pool_rows
    row_of = flat_ids % pool_rows
    one_hot = (owner_of[:, None] == jnp.arange(owners, dtype=jnp.int32)[None, :]).astype(jnp.int32)
    slot_rank = jnp.sum((jnp.cumsum(one_hot, axis=0) - 1) * one_hot, axis=1)
    slot_of = owner_of * capacity + slot_rank
    asked_rows = (
        jnp.zeros((owners * capacity,), jnp.int32).at[slot_of].set(row_of).reshape(owners, capacity)
    )
    wanted = lax.all_to_all(asked_rows, "shard", split_axis=0, concat_axis=0, tiled=True)
    found = jnp.take(neg_pool, wanted, axis=0)
    sent_back = lax.all_to_all(found, "shard", split_axis=0, concat_axis=0, tiled=True)
    negatives = jnp.take(sent_back.reshape(owners * capacity, features), slot_of, axis=0).reshape(
        q_rows, neg_count, features
    )
    hard_scores = (
        jnp.einsum("qd,qkd->qk", queries, negatives, preferred_element_type=jnp.float32) * scaling
    )

    def score_rows(shard_rows):
        return (
            lax.dot_general(
                queries, shard_rows, (((1,), (1,)), ((), ())), preferred_element_type=jnp.float32
            )
            * scaling
        )

    hard_max = jnp.max(hard_scores, axis=1)
    hard_total = jnp.sum(jnp.exp(hard_scores - hard_max[:, None]), axis=1)
    start_state = (hard_max, hard_total)
    score_blk = score_rows(lax.all_gather(my_tile, "blk", axis=0, tiled=True))
    row_max = jnp.maximum(start_state[0], jnp.max(score_blk, axis=1))
    exp_total = start_state[1] * jnp.exp(start_state[0] - row_max) + jnp.sum(
        jnp.exp(score_blk - row_max[:, None]), axis=1
    )
    log_total = row_max + jnp.log(exp_total)
    shard_rows = lax.all_gather(my_tile, "blk", axis=0, tiled=True)
    count = shard_rows.shape[0]
    score_blk = score_rows(shard_rows)
    hit = (positives[:, None] == jnp.arange(count, dtype=jnp.int32)[None, :]).astype(jnp.float32)
    grad_w = (jnp.exp(score_blk - log_total[:, None]) - hit).astype(jnp.bfloat16)
    query_acc = jnp.dot(grad_w, shard_rows, preferred_element_type=jnp.float32)
    updated = lax.dot_general(
        grad_w, queries, (((0,), (0,)), ((), ())), preferred_element_type=jnp.float32
    )
    query_acc, passage_acc = (query_acc, updated)
    passage_grad = (
        lax.psum_scatter(passage_acc, ("blk", "shard"), scatter_dimension=0, tiled=True) * scaling
    )
    hard_weights = jnp.exp(hard_scores - log_total[:, None]).astype(jnp.bfloat16)
    hard_weights = lax.optimization_barrier(hard_weights)
    hard_part = jnp.einsum(
        "qk,qkd->qd", hard_weights, negatives, preferred_element_type=jnp.float32
    )
    query_grad = (query_acc + hard_part) * scaling
    slot_terms = (
        hard_weights.astype(jnp.float32)[:, :, None] * queries.astype(jnp.float32)[:, None, :]
    ).astype(jnp.bfloat16)
    grad_slots = (
        jnp.zeros((owners * capacity, features), jnp.bfloat16)
        .at[slot_of]
        .set(slot_terms.reshape(requests, features))
    )
    returned = lax.all_to_all(
        grad_slots.reshape(owners, capacity, features),
        "shard",
        split_axis=0,
        concat_axis=0,
        tiled=True,
    )
    pool_grad = (
        jnp.zeros((pool_rows, features), jnp.float32)
        .at[wanted.reshape(-1)]
        .add(returned.reshape(owners * capacity, features).astype(jnp.float32))
        * scaling
    )
    return (query_grad, passage_grad, pool_grad)


def solution(mesh):
    in_specs = (
        P(("blk", "shard"), None),
        P(("blk", "shard"), None),
        P(("blk", "shard"), None),
        P(("blk", "shard"), None),
        P(("blk", "shard")),
    )
    out_specs = (P(("blk", "shard"), None), P(("blk", "shard"), None), P(("blk", "shard"), None))
    return jax.shard_map(body, mesh=mesh, in_specs=in_specs, out_specs=out_specs, check_vma=False)
```

profile of v0, /device:TPU:0, one launch (start us, length us, event | category | flops | bytes accessed | tf_op | source)
XLA Modules:
  0.0 263.6 jit_solution(5534285759282947909)
XLA Ops:
  7.2 0.9 copy.23
  8.1 0.2 reshape.257
  8.8 0.6 reduce-window.6
  9.4 0.2 slice_reduce_fusion
  9.9 5.3 %scatter_custom_fusion = s32[1194]{0:T(1024)S(1)} fusion(s32[896]{0:T(1024)S(1)} %fusion.25, s32[896]{0:T(1024)S(1)} %get-tuple-element.3, s32[]{:T(128)} %constant.46.clone.1), kind=kCustom, calls=%fused_computation.67 | custom fusion | bytes 4780 | tf_op jit(solution)/shard_map/scatter | solution.py:23
  15.3 7.8 %all_to_all.25 = s32[2,1,597]{2,1,0:T(1,128)S(1)} all-to-all(s32[2,1,597]{2,1,0:T(1,128)S(1)} %all_to_all.16), channel_id=1, replica_groups=mesh['blk'=16,'shard'=2] {'shard'}, dimensions={0} | all-to-all | bytes 9552 | tf_op jit(solution)/shard_map/all_to_all | solution.py:25
  23.2 5.4 %gather_fusion = bf16[1194,1536]{1,0:T(8,128)(2,1)} fusion(bf16[1024,1536]{1,0:T(8,128)(2,1)S(1)} %copy-done, s32[2048]{0:T(1024)S(1)} %pad_clamp_fusion), kind=kCustom, calls=%fused_computation | custom fusion | bytes 7340712 | tf_op jit(solution)/shard_map/jit(_take)/gather | solution.py:26
  28.6 4.6 %reshape.264 = bf16[2,597,1536]{2,1,0:T(8,128)(2,1)} reshape(bf16[1194,1536]{1,0:T(8,128)(2,1)} %gather_fusion) | data formatting | bytes 7335936 | tf_op jit(solution)/shard_map/jit(_take)/gather | solution.py:26
  33.1 4.3 %broadcast_select_fusion = bf16[2,597,1536]{2,1,0:T(8,128)(2,1)} fusion(bf16[2,597,1536]{2,1,0:T(8,128)(2,1)} %reshape.264, pred[2,597]{1,0:T(4,128)(4,1)S(1)} %compare_and_fusion), kind=kLoop, calls=%fused_computation.6 | loop fusion | flops 1833984 | bytes 7337130 | tf_op jit(solution)/shard_map/jit(_take)/select_n | solution.py:26
  37.4 5.5 %all-to-all-start.1 = ((bf16[2,597,1536]{2,1,0:T(8,128)(2,1)}), bf16[2,597,1536]{2,1,0:T(8,128)(2,1)}, u32[]{:S(2)}, u32[]{:S(2)}) async-start(bf16[2,597,1536]{2,1,0:T(8,128)(2,1)} %broadcast_select_fusion), calls=%async_computation.1 | async-start | bytes 7372800 | tf_op jit(solution)/shard_map/all_to_all | solution.py:27
  43.4 3.5 %mul.94 = f32[128,7,1536]{2,1,0:T(8,128)} broadcast(bf16[128,1536]{1,0:T(8,128)(2,1)S(1)} %copy-done.4), dimensions={0,2} | broadcast | bytes 5898240 | tf_op jit(solution)/shard_map/mul | solution.py:72
  46.9 7.0 %mul.95 = f32[896,1536]{1,0:T(8,128)} reshape(f32[128,7,1536]{2,1,0:T(8,128)} %mul.94) | data formatting | bytes 11010048 | tf_op jit(solution)/shard_map/mul | solution.py:72
  53.9 30.2 %all_gather.7 = bf16[16,1536]{1,0:T(8,128)(2,1)S(1)} all-gather(bf16[8,1536]{1,0:T(8,128)(2,1)S(1)} %copy-done.5), channel_id=1, replica_groups=mesh['blk'=16,'shard'=2] {'shard'}, dimensions={0}, use_global_device_ids=true | all-gather | bytes 73728 | tf_op jit(solution)/shard_map/all_gather | solution.py:15
  84.1 24.1 %all_gather.8 = bf16[256,1536]{1,0:T(8,128)(2,1)S(1)} all-gather(bf16[16,1536]{1,0:T(8,128)(2,1)S(1)} %all_gather.7), channel_id=1, replica_groups=mesh['blk'=16,'shard'=2] {'blk'}, dimensions={0}, use_global_device_ids=true | all-gather | bytes 835584 | tf_op jit(solution)/shard_map/all_gather | solution.py:52
  108.2 0.5 fusion.30
  108.7 0.4 copy-done.2
  109.1 4.6 %reshape.258 = bf16[1194,1536]{1,0:T(8,128)(2,1)} reshape(bf16[2,597,1536]{2,1,0:T(8,128)(2,1)} %all-to-all-done.1) | data formatting | bytes 7335936 | tf_op jit(solution)/shard_map/reshape | solution.py:28
  113.7 9.4 %gather_fusion.1 = bf16[896,1536]{1,0:T(8,128)(2,1)S(1)} fusion(bf16[1194,1536]{1,0:T(8,128)(2,1)} %reshape.258, s32[1024]{0:T(1024)S(1)} %pad_clamp_fusion.1), kind=kCustom, calls=%fused_computation.1 | custom fusion | bytes 5508608 | tf_op jit(solution)/shard_map/jit(_take)/gather | solution.py:28
  123.1 2.6 gather.12
  125.7 4.3 %fusion.3 = f32[128,1,7]{2,1,0:T(1,128)S(1)} fusion(bf16[128,7,1536]{2,1,0:T(8,128)(2,1)} %gather.12, pred[128,7]{1,0:T(8,128)(4,1)S(1)} %copy.26, bf16[128,1536,1]{1,0,2:T(8,128)(2,1)S(1)} %bitcast.34), kind=kOutput, calls=%fused_computation.12 | convolution fusion | flops 4128768 | bytes 3150208 | tf_op jit(solution)/shard_map/qd,qkd->qk/dot_general | solution.py:32
  130.7 13.6 %scatter_custom_fusion.1 = bf16[1194,1536]{1,0:T(8,128)(2,1)} fusion(s32[896]{0:T(1024)S(1)} %fusion.25, f32[896,1536]{1,0:T(8,128)} %mul.95, f32[896]{0:T(1024)S(1)} %reshape.261, bf16[]{:T(256)} %constant.80.clone.1), kind=kCustom, calls=%fused_computation.13 | custom fusion | flops 2752512 | bytes 9177090 | tf_op jit(solution)/shard_map/scatter | solution.py:77
  144.3 4.6 %reshape.260 = bf16[2,597,1536]{2,1,0:T(8,128)(2,1)} reshape(bf16[1194,1536]{1,0:T(8,128)(2,1)} %scatter_custom_fusion.1) | data formatting | bytes 7335936 | tf_op jit(solution)/shard_map/reshape | solution.py:80
  148.9 5.5 %all-to-all-start.2 = ((bf16[2,597,1536]{2,1,0:T(8,128)(2,1)}), bf16[2,597,1536]{2,1,0:T(8,128)(2,1)}, u32[]{:S(2)}, u32[]{:S(2)}) async-start(bf16[2,597,1536]{2,1,0:T(8,128)(2,1)} %reshape.260), calls=%async_computation.3 | async-start | bytes 7372800 | tf_op jit(solution)/shard_map/all_to_all | solution.py:79
  154.4 1.6 fusion.29
  156.4 2.9 %fusion.2 = f32[128,1,1536]{2,1,0:T(1,128)S(1)} fusion(bf16[128,7,1]{1,2,0:T(2,128)(2,1)S(1)} %copy.31, bf16[128,7,1536]{2,1,0:T(8,128)(2,1)} %gather.12, pred[128,7]{1,0:T(8,128)(4,1)S(1)} %copy.26), kind=kOutput, calls=%fused_computation.11 | convolution fusion | flops 4128768 | bytes 3541632 | tf_op jit(solution)/shard_map/qk,qkd->qd/dot_general | solution.py:67
  159.3 1.2 fusion.6
  160.5 36.6 %all-to-all-done.2 = bf16[2,597,1536]{2,1,0:T(8,128)(2,1)} async-done(((bf16[2,597,1536]{2,1,0:T(8,128)(2,1)}), bf16[2,597,1536]{2,1,0:T(8,128)(2,1)}, u32[]{:S(2)}, u32[]{:S(2)}) %all-to-all-start.2) | async-done | bytes 3668000 | tf_op jit(solution)/shard_map/all_to_all | solution.py:79
  197.1 5.7 %reshape.299 = f32[1194,1536]{1,0:T(8,128)} reshape(bf16[2,597,1536]{2,1,0:T(8,128)(2,1)} %all-to-all-done.2) | data formatting | bytes 11003904 | tf_op jit(solution)/shard_map/convert_element_type | solution.py:89
  202.8 19.8 %scatter_custom_fusion.2 = f32[1024,1536]{1,0:T(8,128)} fusion(s32[1194]{0:T(1024)S(1)} %fusion.13, f32[1194,1536]{1,0:T(8,128)} %reshape.299, f32[]{:T(128)} %constant.79.clone.1), kind=kCustom, calls=%fused_computation.8 | custom fusion | flops 1833984 | bytes 6291968 | tf_op jit(solution)/shard_map/scatter-add | solution.py:89
  222.7 6.3 %broadcast_multiply_fusion = f32[1024,1536]{1,0:T(8,128)} fusion(f32[1024,1536]{1,0:T(8,128)} %scatter_custom_fusion.2), kind=kLoop, calls=%fused_computation.7 | loop fusion | flops 1572864 | bytes 12582912 | tf_op jit(solution)/shard_map/mul | solution.py:87
  229.0 26.3 %reduce-scatter.2.cloned.1.call-done = f32[8,1536]{1,0:T(8,128)} async-done(((f32[256,1536]{1,0:T(8,128)}), f32[8,1536]{1,0:T(8,128)}) %reduce-scatter.2.cloned.1.call-update) | async-done | bytes 49168 | tf_op jit(solution)/shard_map/reduce_scatter | solution.py:63
  255.3 1.4 broadcast_multiply_fusion.1
  (50 shorter events, 2.4 us)
Async XLA Ops:
  7.2 16.0 %copy-start = (bf16[1024,1536]{1,0:T(8,128)(2,1)S(1)}, bf16[1024,1536]{1,0:T(8,128)(2,1)}, u32[]{:S(2)}) copy-start(bf16[1024,1536]{1,0:T(8,128)(2,1)} %param.7) | copy-start | bytes 9437188
  37.4 5.8 %copy-start.6 = (s32[128,7]{0,1:T(8,128)S(1)}, s32[128,7]{0,1:T(8,128)}, u32[]{:S(2)}) copy-start(s32[128,7]{0,1:T(8,128)} %param.8) | copy-start | bytes 10756
  37.4 6.0 %copy-start.4 = (bf16[128,1536]{1,0:T(8,128)(2,1)S(1)}, bf16[128,1536]{1,0:T(8,128)(2,1)}, u32[]{:S(2)}) copy-start(bf16[128,1536]{1,0:T(8,128)(2,1)} %param.5) | copy-start | bytes 1179652
  37.4 71.3 %all-to-all-start.1 = ((bf16[2,597,1536]{2,1,0:T(8,128)(2,1)}), bf16[2,597,1536]{2,1,0:T(8,128)(2,1)}, u32[]{:S(2)}, u32[]{:S(2)}) async-start(bf16[2,597,1536]{2,1,0:T(8,128)(2,1)} %broadcast_select_fusion), calls=%async_computation.1 | async-start | bytes 7372800 | tf_op jit(solution)/shard_map/all_to_all | solution.py:27
  46.9 7.1 %copy-start.5 = (bf16[8,1536]{1,0:T(8,128)(2,1)S(1)}, bf16[8,1536]{1,0:T(8,128)(2,1)}, u32[]{:S(2)}) copy-start(bf16[8,1536]{1,0:T(8,128)(2,1)} %param.6) | copy-start | bytes 73732
  108.2 0.9 copy-start.2
  148.8 5.6 %copy-start.7 = (s32[128]{0:T(128)S(1)}, s32[128]{0:T(128)}, u32[]{:S(2)}) copy-start(s32[128]{0:T(128)} %param.9) | copy-start | bytes 1540
  148.9 48.3 %all-to-all-start.2 = ((bf16[2,597,1536]{2,1,0:T(8,128)(2,1)}), bf16[2,597,1536]{2,1,0:T(8,128)(2,1)}, u32[]{:S(2)}, u32[]{:S(2)}) async-start(bf16[2,597,1536]{2,1,0:T(8,128)(2,1)} %reshape.260), calls=%async_computation.3 | async-start | bytes 7372800 | tf_op jit(solution)/shard_map/all_to_all | solution.py:79
  154.4 100.9 %reduce-scatter.2.cloned.1.call-start = ((), (), s32[]{:S(2)}) async-start(), calls=%async_computation.4 | async-start | bytes 1622016 | tf_op jit(solution)/shard_map/reduce_scatter | solution.py:63
  156.1 3.3 %copy-start.3 = (bf16[256,1536]{1,0:T(8,128)(2,1)S(1)}, bf16[256,1536]{1,0:T(8,128)(2,1)}, u32[]{:S(2)}) copy-start(bf16[256,1536]{1,0:T(8,128)(2,1)} %copy-done.2) | copy-start | bytes 2359300
  202.8 53.9 %copy-start.1 = (bf16[1024,1536]{1,0:T(8,128)(2,1)S(1)}, bf16[1024,1536]{1,0:T(8,128)(2,1)}, u32[]{:S(2)}) copy-start(bf16[1024,1536]{1,0:T(8,128)(2,1)} %param.7) | copy-start | bytes 9437188
Sparse Core Ops, SparseCore 0:
  160.4 94.7 reduce-scatter.1
where the time goes:
time: 264 us
  waiting for transfers between devices  62.9 us (24%)
  blocking collectives  62.1 us (24%)
  local copies, waits for them, and re-layouts  56 us (21%)
  other arithmetic  46.7 us (18%)
  between operations  14.2 us (5%)
  starting transfers between devices  11.1 us (4%)
  matrix products  10.5 us (4%)
    all_to_all x1, waiting for transfers between devices, body(): lax.all_to_all(grad_slots.reshape(owners, capacity, features), 'shard', s...  36.6 us
    all_gather x1, blocking collectives, body(): my_tile = lax.all_gather(passages, 'shard', axis=0, tiled=True)  30.2 us
    reduce_scatter x1, waiting for transfers between devices, body(): lax.psum_scatter(passage_acc, ('blk', 'shard'), scatter_dimension=0, tile...  26.3 us
    all_gather x1, blocking collectives, body(): shard_rows = lax.all_gather(my_tile, 'blk', axis=0, tiled=True)  24.1 us
    scatter-add x1, other arithmetic, body(): pool_grad = jnp.zeros((pool_rows, features), jnp.float32).at[wanted.resha...  19.8 us
    scatter x1, other arithmetic, body(): grad_slots = jnp.zeros((owners * capacity, features), jnp.bfloat16).at[sl...  13.6 us
    gather x2, local copies, waits for them, and re-layouts, body(): jnp.take(sent_back.reshape(owners * capacity, features), slot_of, axis=0)  12 us
    mul x4, local copies, waits for them, and re-layouts, body(): hard_weights.astype(jnp.float32)[:, :, None]  10.9 us
  transfers between devices with their start and end apart: 3, of which 2 were waited for; matrix products, arithmetic and copies ran while one was open for 19% of the time, Pallas kernels for 0%

commit v1 on v0

v1 whole, which is shorter than its diff:
```python
import jax
import jax.numpy as jnp
from jax import lax
from jax.sharding import PartitionSpec as P


def bit_order(count):
    bits = [1 << t for t in range(count.bit_length() - 1)]
    return bits[2:] + bits[:2][::-1]


def across(x, axis, count, distance):
    return lax.ppermute(x, axis, [(i, i ^ distance) for i in range(count)])


def shifted(x, axis, count, distance):
    return lax.ppermute(x, axis, [((i + distance) % count, i) for i in range(count)])


def body(queries, passages, neg_pool, hard_ids, positives):
    rows, features = queries.shape
    neg_count = hard_ids.shape[1]
    tile = passages.shape[0]
    pool_rows = neg_pool.shape[0]
    scaling = features ** (-0.5)
    owners = lax.axis_size("shard")
    blocks = lax.axis_size("blk")
    my_shard = lax.axis_index("shard")
    my_blk = lax.axis_index("blk")

    marks = jnp.concatenate([hard_ids, positives[:, None]], axis=1)
    group_marks = jnp.concatenate(
        [marks] + [shifted(marks, "shard", owners, d) for d in range(1, owners)], axis=0
    )
    group_q = jnp.concatenate(
        [queries] + [shifted(queries, "shard", owners, d) for d in range(1, owners)], axis=0
    )

    order = bit_order(blocks)
    keys = passages
    key_blk = jnp.zeros((1,), jnp.int32)
    for bit in order:
        keys = jnp.concatenate([keys, across(keys, "blk", blocks, bit)], axis=0)
        key_blk = jnp.concatenate([key_blk, key_blk ^ bit], axis=0)
    key_ids = (
        ((key_blk ^ my_blk) * owners + my_shard)[:, None] * tile
        + jnp.arange(tile, dtype=jnp.int32)[None, :]
    ).reshape(-1)

    def dots(a, b):
        return lax.dot_general(a, b, (((1,), (1,)), ((), ())), preferred_element_type=jnp.float32)

    local_ids = group_marks[:, :neg_count] - my_shard * pool_rows
    slots = jnp.arange(pool_rows, dtype=jnp.int32)[None, :]
    times = sum((local_ids[:, k : k + 1] == slots).astype(jnp.float32) for k in range(neg_count))
    hard = jnp.where(times > 0, dots(group_q, neg_pool) * scaling, -jnp.inf)
    score = dots(group_q, keys) * scaling
    part_max = jnp.maximum(jnp.max(hard, axis=1), jnp.max(score, axis=1))
    part_sum = jnp.sum(times * jnp.exp(hard - part_max[:, None]), axis=1) + jnp.sum(
        jnp.exp(score - part_max[:, None]), axis=1
    )
    part = jnp.stack([part_max, part_sum])
    if owners == 2:
        other = shifted(part, "shard", owners, 1)
        parts = jnp.stack([part, jnp.roll(other, rows, axis=1)])
    else:
        whole = lax.all_gather(jnp.roll(part, my_shard * rows, axis=1), "shard", axis=0)
        parts = jnp.roll(whole, -my_shard * rows, axis=2)
    row_max = jnp.max(parts[:, 0], axis=0)
    log_total = row_max + jnp.log(
        jnp.sum(parts[:, 1] * jnp.exp(parts[:, 0] - row_max[None, :]), axis=0)
    )

    hit = (group_marks[:, neg_count:] == key_ids[None, :]).astype(jnp.float32)
    weights = (jnp.exp(score - log_total[:, None]) - hit).astype(jnp.bfloat16)
    hard_weights = jnp.exp(hard - log_total[:, None]).astype(jnp.bfloat16)
    hard_weights = (times * hard_weights.astype(jnp.float32)).astype(jnp.bfloat16)

    def spread(w, q):
        return lax.dot_general(w, q, (((0,), (0,)), ((), ())), preferred_element_type=jnp.float32)

    passage_acc = spread(weights, group_q) * scaling
    for bit in order[::-1]:
        half = passage_acc.shape[0] // 2
        sent = across(passage_acc[half:].astype(jnp.bfloat16), "blk", blocks, bit)
        passage_acc = passage_acc[:half] + sent.astype(jnp.float32)

    def query_part(d):
        piece = slice(d * rows, (d + 1) * rows)
        return (
            jnp.dot(weights[piece], keys, preferred_element_type=jnp.float32)
            + jnp.dot(hard_weights[piece], neg_pool, preferred_element_type=jnp.float32)
        ) * scaling

    back = [
        shifted(query_part(d).astype(jnp.bfloat16), "shard", owners, owners - d)
        for d in range(1, owners)
    ]
    query_grad = query_part(0) + sum(b.astype(jnp.float32) for b in back)
    pool_grad = spread(hard_weights, group_q) * scaling
    return query_grad, passage_acc, pool_grad


def solution(mesh):
    both = P(("blk", "shard"), None)
    in_specs = (both, both, both, both, P(("blk", "shard")))
    return jax.shard_map(
        body, mesh=mesh, in_specs=in_specs, out_specs=(both, both, both), check_vma=False
    )
```

time: 264 us -> 64.1 us (0.24)
  blocking collectives: 62.1 us -> 0 us
  local copies, waits for them, and re-layouts: 56 us -> 5.75 us
  waiting for transfers between devices: 62.9 us -> 19.9 us
  other arithmetic: 46.7 us -> 8.11 us
  between operations: 14.2 us -> 0.89 us
  starting transfers between devices: 11.1 us -> 17.8 us
    all_gather x2 -> x0, blocking collectives: 54.3 us -> none  [the longest x1 30.2 us: body(): my_tile = lax.all_gather(passages, 'shard', axis=0, tiled=True)]
    all_to_all x2 -> x0, waiting for transfers between devices: 36.6 us -> none  [the longest x1 36.6 us: body(): lax.all_to_all(grad_slots.reshape(owners, capacity, features), 'shard', s...]
    reduce_scatter x1 -> x0, waiting for transfers between devices: 26.3 us -> none  [body(): lax.psum_scatter(passage_acc, ('blk', 'shard'), scatter_dimension=0, tile...]
    gather x4 -> x0, local copies, waits for them, and re-layouts: 21.9 us -> none  [the longest x2 12 us: body(): jnp.take(sent_back.reshape(owners * capacity, features), slot_of, axis=0)]
    ppermute x0 -> x12, waiting for transfers between devices: none -> 19.9 us  [the longest x8 12.5 us: across(): return lax.ppermute(x, axis, [(i, i ^ distance) for i in range(count)])]
    scatter-add x1 -> x0, other arithmetic: 19.8 us -> none  [body(): pool_grad = jnp.zeros((pool_rows, features), jnp.float32).at[wanted.resha...]
    ppermute x0 -> x12, starting transfers between devices: none -> 17.8 us  [the longest x8 10.7 us: across(): return lax.ppermute(x, axis, [(i, i ^ distance) for i in range(count)])]
    scatter x1 -> x0, other arithmetic: 13.6 us -> none  [body(): grad_slots = jnp.zeros((owners * capacity, features), jnp.bfloat16).at[sl...]
  transfers between devices with their start and end apart: 3 -> 12, of which waited for: 2 -> 8; matrix products, arithmetic and copies ran while one was open for 19% -> 21% of each run, Pallas kernels for 0% -> 0%
where the time goes in v1:
time: 64.1 us; the launch traced here: 63.5 us
  waiting for transfers between devices  19.9 us (31%)
  starting transfers between devices  17.8 us (28%)
  matrix products  11 us (17%)
  other arithmetic  8.11 us (13%)
  local copies, waits for them, and re-layouts  5.75 us (9%)
  between operations  0.89 us (1%)
    ppermute x8, waiting for transfers between devices, across(): return lax.ppermute(x, axis, [(i, i ^ distance) for i in range(count)])  12.5 us
    ppermute x8, starting transfers between devices, across(): return lax.ppermute(x, axis, [(i, i ^ distance) for i in range(count)])  10.7 us
    ppermute x4, waiting for transfers between devices, shifted(): lax.ppermute(x, axis, [((i + distance) % count, i) for i in range(count)])  7.37 us
    ppermute x4, starting transfers between devices, shifted(): lax.ppermute(x, axis, [((i + distance) % count, i) for i in range(count)])  7.14 us
    dot_general x2, matrix products, dots(): lax.dot_general(a, b, (((1,), (1,)), ((), ())), preferred_element_type=jn...  4.38 us
    dot_general x2, matrix products, spread(): lax.dot_general(w, q, (((0,), (0,)), ((), ())), preferred_element_type=jn...  3.99 us
    unnamed x15, local copies, waits for them, and re-layouts  3.29 us
    concatenate x3, other arithmetic, body(): keys = jnp.concatenate([keys, across(keys, 'blk', blocks, bit)], axis=0)  2.29 us
  transfers between devices with their start and end apart: 12, of which 8 were waited for; matrix products, arithmetic and copies ran while one was open for 21% of the time, Pallas kernels for 0%

profile of v1, /device:TPU:0, one launch (start us, length us, event | category | flops | bytes accessed | tf_op | source)
XLA Modules:
  0.0 63.5 jit_solution(5662161950759620822)
XLA Ops:
  0.6 0.9 %pad_add_fusion.1 = s32[128,8]{0,1:T(8,128)S(1)} fusion(s32[128,1]{0,1:T(1,128)} %bitcast.59, s32[128,7]{0,1:T(8,128)} %param.8), kind=kLoop, calls=%fused_computation.51 | loop fusion | flops 1024 | bytes 8192 | tf_op jit(solution)/shard_map/concatenate | solution.py:31
  1.5 2.9 %collective-permute-start.5 = (s32[128,8]{0,1:T(8,128)S(1)}, s32[128,8]{0,1:T(8,128)S(1)}, u32[]{:S(2)}, u32[]{:S(2)}) collective-permute-start(s32[128,8]{0,1:T(8,128)S(1)} %pad_add_fusion.1), channel_id=1, source_target_pairs={{1,0},{0,1},{3,2},{2,3},{5,4},{4,5},{7,6},{6,7},{9,8},{8,9},{11,10... | collective-permute-start | bytes 12296 | tf_op jit(solution)/shard_map/ppermute | solution.py:17
  4.4 1.6 %collective-permute-start.1 = (bf16[8,1536]{1,0:T(8,128)(2,1)}, bf16[8,1536]{1,0:T(8,128)(2,1)}, u32[]{:S(2)}, u32[]{:S(2)}) collective-permute-start(bf16[8,1536]{1,0:T(8,128)(2,1)} %param.6), channel_id=1, source_target_pairs={{0,8},{2,10},{4,12},{6,14},{8,0},{10,2},{12,4},{14,6},{16,24},{18,... | collective-permute-start | bytes 73736 | tf_op jit(solution)/shard_map/ppermute | solution.py:13
  6.6 0.7 %constant_dynamic-update-slice_fusion.6 = bf16[128,1536]{1,0:T(8,128)(2,1)S(1)} fusion(bf16[8,1536]{1,0:T(8,128)(2,1)} %param.6), kind=kLoop, calls=%fused_computation.47 | loop fusion | bytes 49152
  7.3 1.8 %constant_dynamic-update-slice_fusion.1 = bf16[256,1536]{1,0:T(8,128)(2,1)} fusion(bf16[128,1536]{1,0:T(8,128)(2,1)} %param.5), kind=kLoop, calls=%fused_computation.42 | loop fusion | bytes 786432
  9.1 0.7 %add_multiply_fusion = s32[16]{0:T(128)S(1)} fusion(s32[16]{0:T(128)} %constant.8.clone.1, s32[]{:T(128)S(6)} %axis_index.22, s32[]{:T(128)S(6)} %axis_index.25), kind=kLoop, calls=%fused_computation.65 | loop fusion | flops 64 | bytes 136 | tf_op jit(solution)/shard_map/mul | solution.py:46
  10.4 0.7 %pad_add_fusion = s32[256,8]{0,1:T(8,128)S(1)} fusion(s32[128,8]{0,1:T(8,128)S(1)} %collective-permute-done.5, s32[128,1]{0,1:T(1,128)} %bitcast.60, s32[128,7]{0,1:T(8,128)} %param.8), kind=kLoop, calls=%fused_computation.49 | loop fusion | flops 4096 | bytes 16384 | tf_op jit(solution)/shard_map/concatenate | solution.py:32
  11.1 0.8 %pad_maximum_fusion.2 = bf16[16,1536]{1,0:T(8,128)(2,1)S(1)} fusion(bf16[8,1536]{1,0:T(8,128)(2,1)} %collective-permute-done.1, bf16[8,1536]{1,0:T(8,128)(2,1)} %param.6), kind=kLoop, calls=%fused_computation.38 | loop fusion | flops 98304 | bytes 98304 | tf_op jit(solution)/shard_map/concatenate | solution.py:43
  11.9 2.6 %collective-permute-start.2 = (bf16[16,1536]{1,0:T(8,128)(2,1)S(1)}, bf16[16,1536]{1,0:T(8,128)(2,1)S(1)}, u32[]{:S(2)}, u32[]{:S(2)}) collective-permute-start(bf16[16,1536]{1,0:T(8,128)(2,1)S(1)} %pad_maximum_fusion.2), channel_id=1, source_target_pairs={{0,16},{2,18},{4,20},{6,22},{8,24},{10,26},{12,28},{14,30},{16,0},... | collective-permute-start | bytes 147464 | tf_op jit(solution)/shard_map/ppermute | solution.py:13
  14.5 0.7 %constant_dynamic-update-slice_fusion.5 = bf16[128,1536]{1,0:T(8,128)(2,1)S(1)} fusion(bf16[128,1536]{1,0:T(8,128)(2,1)S(1)} %constant_dynamic-update-slice_fusion.6, bf16[8,1536]{1,0:T(8,128)(2,1)} %collective-permute-done.1), kind=kLoop, calls=%fused_computation.46 | loop fusion | bytes 49152
  15.2 1.7 %collective-permute-done.2 = bf16[16,1536]{1,0:T(8,128)(2,1)S(1)} collective-permute-done((bf16[16,1536]{1,0:T(8,128)(2,1)S(1)}, bf16[16,1536]{1,0:T(8,128)(2,1)S(1)}, u32[]{:S(2)}, u32[]{:S(2)}) %collective-permute-start.2) | collective-permute-done | bytes 49184 | tf_op jit(solution)/shard_map/ppermute | solution.py:13
  17.0 0.8 %pad_maximum_fusion.1 = bf16[32,1536]{1,0:T(8,128)(2,1)S(1)} fusion(bf16[16,1536]{1,0:T(8,128)(2,1)S(1)} %collective-permute-done.2, bf16[8,1536]{1,0:T(8,128)(2,1)} %collective-permute-done.1, bf16[8,1536]{1,0:T(8,128)(2,1)} %param.6), kind=kLoop, calls=%fused_computation.35 | loop fusion | flops 294912 | bytes 196608 | tf_op jit(solution)/shard_map/concatenate | solution.py:43
  17.7 1.9 %collective-permute-start.3 = (bf16[32,1536]{1,0:T(8,128)(2,1)S(1)}, bf16[32,1536]{1,0:T(8,128)(2,1)S(1)}, u32[]{:S(2)}, u32[]{:S(2)}) collective-permute-start(bf16[32,1536]{1,0:T(8,128)(2,1)S(1)} %pad_maximum_fusion.1), channel_id=1, source_target_pairs={{0,4},{2,6},{4,0},{6,2},{8,12},{10,14},{12,8},{14,10},{16,20},{18,... | collective-permute-start | bytes 294920 | tf_op jit(solution)/shard_map/ppermute | solution.py:13
  19.6 2.8 %collective-permute-done.3 = bf16[32,1536]{1,0:T(8,128)(2,1)S(1)} collective-permute-done((bf16[32,1536]{1,0:T(8,128)(2,1)S(1)}, bf16[32,1536]{1,0:T(8,128)(2,1)S(1)}, u32[]{:S(2)}, u32[]{:S(2)}) %collective-permute-start.3) | collective-permute-done | bytes 98336 | tf_op jit(solution)/shard_map/ppermute | solution.py:13
  22.4 0.8 %pad_maximum_fusion = bf16[64,1536]{1,0:T(8,128)(2,1)S(1)} fusion(bf16[32,1536]{1,0:T(8,128)(2,1)S(1)} %collective-permute-done.3, bf16[16,1536]{1,0:T(8,128)(2,1)S(1)} %collective-permute-done.2, bf16[8,1536]{1,0:T(8,128)(2,1)} %collective-permute-done.1, bf16[8,1536]{1,0:T(8,128)(2,1)} %param.6), kind=kLoop, calls=%fused_computation.30 | loop fusion | flops 786432 | bytes 393216 | tf_op jit(solution)/shard_map/concatenate | solution.py:43
  23.3 1.4 %collective-permute-done.4 = bf16[64,1536]{1,0:T(8,128)(2,1)S(1)} collective-permute-done((bf16[64,1536]{1,0:T(8,128)(2,1)S(1)}, bf16[64,1536]{1,0:T(8,128)(2,1)S(1)}, u32[]{:S(2)}, u32[]{:S(2)}) %collective-permute-start.4) | collective-permute-done | bytes 196640 | tf_op jit(solution)/shard_map/ppermute | solution.py:13
  24.7 1.8 %constant_dynamic-update-slice_fusion = bf16[256,1536]{1,0:T(8,128)(2,1)} fusion(bf16[256,1536]{1,0:T(8,128)(2,1)} %constant_dynamic-update-slice_fusion.1, bf16[128,1536]{1,0:T(8,128)(2,1)} %collective-permute-done), kind=kLoop, calls=%fused_computation.41 | loop fusion | bytes 786432 | tf_op jit(solution)/shard_map/concatenate | solution.py:35
  26.5 1.5 %fusion.22 = (f32[256]{0:T(256)S(1)}, f32[256,128]{0,1:T(8,128)S(1)}) fusion(bf16[256,1536]{1,0:T(8,128)(2,1)} %constant_dynamic-update-slice_fusion, bf16[128,1536]{1,0:T(8,128)(2,1)S(1)} %constant_dynamic-update-slice_fusion.2), kind=kOutput, calls=%fused_computation.71 | convolution fusion | flops 100728576 | bytes 1311744 | tf_op jit(solution)/shard_map/dot_general | solution.py:51
  28.1 2.9 %fusion.21 = (f32[256]{0:T(256)S(1)}, f32[256,1024]{1,0:T(8,128)S(1)}) fusion(bf16[256,1536]{1,0:T(8,128)(2,1)} %constant_dynamic-update-slice_fusion, bf16[1024,1536]{1,0:T(8,128)(2,1)S(1)} %copy-done, s32[256]{0:T(256)S(1)} %bitcast.41, s32[256]{0:T(256)S(1)} %bitcast.44, s32[256]{0:T(256)S(1)} %bitcast.47, s32[256]{0:T(256)S(1)} %bitcast.50, ...), kind=kOutput, calls=%fused_computation.70 | convolution fusion | flops 811597568 | bytes 4988928 | tf_op jit(solution)/shard_map/dot_general | solution.py:51
  31.0 1.5 %multiply_reduce_fusion = f32[256]{0:T(256)S(1)} fusion(f32[256,1024]{1,0:T(8,128)S(1)} %get-tuple-element.17, f32[256]{0:T(256)S(1)} %max.17, s32[256]{0:T(256)S(1)} %bitcast.42, s32[256]{0:T(256)S(1)} %bitcast.45, s32[256]{0:T(256)S(1)} %bitcast.48, s32[256]{0:T(256)S(1)} %bitcast.51, s32[256]{0:T(256)S(1)} %bitcast.54, s32[256]{0:T(256)S(1)} %bitcast.57, ...), kind=kLoop, calls=%fused_computation.13 | loop fusion | flops 6029056 | bytes 1057792 | tf_op jit(solution)/shard_map/reduce_sum | solution.py:59
  32.5 1.9 %collective-permute-start.6 = (f32[2,256]{1,0:T(2,128)S(1)}, f32[2,256]{1,0:T(2,128)S(1)}, u32[]{:S(2)}, u32[]{:S(2)}) collective-permute-start(f32[2,256]{1,0:T(2,128)S(1)} %get-tuple-element.13), channel_id=1, source_target_pairs={{1,0},{0,1},{3,2},{2,3},{5,4},{4,5},{7,6},{6,7},{9,8},{8,9},{11,10... | collective-permute-start | bytes 6152 | tf_op jit(solution)/shard_map/ppermute | solution.py:17
  34.4 1.7 %collective-permute-done.6 = f32[2,256]{1,0:T(2,128)S(1)} collective-permute-done((f32[2,256]{1,0:T(2,128)S(1)}, f32[2,256]{1,0:T(2,128)S(1)}, u32[]{:S(2)}, u32[]{:S(2)}) %collective-permute-start.6) | collective-permute-done | bytes 2080 | tf_op jit(solution)/shard_map/ppermute | solution.py:17
  36.2 1.1 %multiply_convert_fusion = bf16[256,1024]{1,0:T(8,128)(2,1)S(1)} fusion(f32[256,1024]{1,0:T(8,128)S(1)} %get-tuple-element.17, f32[256]{0:T(256)S(1)} %log_add_fusion, s32[256]{0:T(256)S(1)} %bitcast.43, s32[256]{0:T(256)S(1)} %bitcast.46, s32[256]{0:T(256)S(1)} %bitcast.49, s32[256]{0:T(256)S(1)} %bitcast.52, s32[256]{0:T(256)S(1)} %bitcast.55, ...), kind=kLoop, calls=%fused_computation.11 | loop fusion | flops 6553600 | bytes 1581056 | tf_op jit(solution)/shard_map/convert_element_type | solution.py:77
  37.8 3.7 %convolution_multiply_fusion = f32[1024,1536]{1,0:T(8,128)} fusion(bf16[256,1024]{1,0:T(8,128)(2,1)S(1)} %multiply_convert_fusion, bf16[256,1536]{1,0:T(8,128)(2,1)S(1)} %copy-done.1), kind=kOutput, calls=%fused_computation | convolution fusion | flops 806879232 | bytes 7602176 | tf_op jit(solution)/shard_map/dot_general | solution.py:80
  41.6 1.9 %collective-permute-start.9 = (bf16[32,1536]{1,0:T(8,128)(2,1)S(1)}, bf16[32,1536]{1,0:T(8,128)(2,1)S(1)}, u32[]{:S(2)}, u32[]{:S(2)}) collective-permute-start(bf16[32,1536]{1,0:T(8,128)(2,1)S(1)} %slice.155), channel_id=1, source_target_pairs={{0,4},{2,6},{4,0},{6,2},{8,12},{10,14},{12,8},{14,10},{16,20},{18,... | collective-permute-start | bytes 294920 | tf_op jit(solution)/shard_map/ppermute | solution.py:13
  44.1 2.9 %collective-permute-done.9 = bf16[32,1536]{1,0:T(8,128)(2,1)S(1)} collective-permute-done((bf16[32,1536]{1,0:T(8,128)(2,1)S(1)}, bf16[32,1536]{1,0:T(8,128)(2,1)S(1)}, u32[]{:S(2)}, u32[]{:S(2)}) %collective-permute-start.9) | collective-permute-done | bytes 98336 | tf_op jit(solution)/shard_map/ppermute | solution.py:13
  47.0 2.5 %collective-permute-start.10 = (bf16[16,1536]{1,0:T(8,128)(2,1)S(1)}, bf16[16,1536]{1,0:T(8,128)(2,1)S(1)}, u32[]{:S(2)}, u32[]{:S(2)}) collective-permute-start(bf16[16,1536]{1,0:T(8,128)(2,1)S(1)} %slice.156), channel_id=1, source_target_pairs={{0,16},{2,18},{4,20},{6,22},{8,24},{10,26},{12,28},{14,30},{16,0},... | collective-permute-start | bytes 147464 | tf_op jit(solution)/shard_map/ppermute | solution.py:13
  50.1 2.0 %collective-permute-done.10 = bf16[16,1536]{1,0:T(8,128)(2,1)S(1)} collective-permute-done((bf16[16,1536]{1,0:T(8,128)(2,1)S(1)}, bf16[16,1536]{1,0:T(8,128)(2,1)S(1)}, u32[]{:S(2)}, u32[]{:S(2)}) %collective-permute-start.10) | collective-permute-done | bytes 49184 | tf_op jit(solution)/shard_map/ppermute | solution.py:13
  52.6 1.8 %collective-permute-start.7 = (bf16[128,1536]{1,0:T(8,128)(2,1)S(1)}, bf16[128,1536]{1,0:T(8,128)(2,1)S(1)}, u32[]{:S(2)}, u32[]{:S(2)}) collective-permute-start(bf16[128,1536]{1,0:T(8,128)(2,1)S(1)} %fusion.3), channel_id=1, source_target_pairs={{1,0},{0,1},{3,2},{2,3},{5,4},{4,5},{7,6},{6,7},{9,8},{8,9},{11,10... | collective-permute-start | bytes 1179656 | tf_op jit(solution)/shard_map/ppermute | solution.py:17
  54.3 1.7 %collective-permute-done.11 = bf16[8,1536]{1,0:T(8,128)(2,1)S(1)} collective-permute-done((bf16[8,1536]{1,0:T(8,128)(2,1)S(1)}, bf16[8,1536]{1,0:T(8,128)(2,1)S(1)}, u32[]{:S(2)}, u32[]{:S(2)}) %collective-permute-start.11) | collective-permute-done | bytes 24608 | tf_op jit(solution)/shard_map/ppermute | solution.py:13
  56.7 5.6 %collective-permute-done.7 = bf16[128,1536]{1,0:T(8,128)(2,1)S(1)} collective-permute-done((bf16[128,1536]{1,0:T(8,128)(2,1)S(1)}, bf16[128,1536]{1,0:T(8,128)(2,1)S(1)}, u32[]{:S(2)}, u32[]{:S(2)}) %collective-permute-start.7) | collective-permute-done | bytes 393248 | tf_op jit(solution)/shard_map/ppermute | solution.py:17
  62.3 1.2 %fusion.2 = f32[128,1536]{1,0:T(8,128)} fusion(f32[128,1536]{1,0:T(8,128)S(1)} %fusion.7, bf16[128,1536]{1,0:T(8,128)(2,1)S(1)} %constant_dynamic-update-slice_fusion.2, bf16[128,1536]{1,0:T(8,128)(2,1)S(1)} %collective-permute-done.7, bf16[256,128]{0,1:T(8,128)(2,1)S(1)} %subtract_convert_fusion), kind=kOutput, calls=%fused_computation.6 | convolution fusion | flops 51118080 | bytes 2392064 | tf_op jit(solution)/shard_map/dot_general | solution.py:91
  (50 shorter events, 4.2 us)
Async XLA Ops:
  0.6 27.4 %copy-start = (bf16[1024,1536]{1,0:T(8,128)(2,1)S(1)}, bf16[1024,1536]{1,0:T(8,128)(2,1)}, u32[]{:S(2)}) copy-start(bf16[1024,1536]{1,0:T(8,128)(2,1)} %param.7) | copy-start | bytes 9437188
  1.5 8.9 %collective-permute-start.5 = (s32[128,8]{0,1:T(8,128)S(1)}, s32[128,8]{0,1:T(8,128)S(1)}, u32[]{:S(2)}, u32[]{:S(2)}) collective-permute-start(s32[128,8]{0,1:T(8,128)S(1)} %pad_add_fusion.1), channel_id=1, source_target_pairs={{1,0},{0,1},{3,2},{2,3},{5,4},{4,5},{7,6},{6,7},{9,8},{8,9},{11,10... | collective-permute-start | bytes 12296 | tf_op jit(solution)/shard_map/ppermute | solution.py:17
  4.4 6.7 %collective-permute-start.1 = (bf16[8,1536]{1,0:T(8,128)(2,1)}, bf16[8,1536]{1,0:T(8,128)(2,1)}, u32[]{:S(2)}, u32[]{:S(2)}) collective-permute-start(bf16[8,1536]{1,0:T(8,128)(2,1)} %param.6), channel_id=1, source_target_pairs={{0,8},{2,10},{4,12},{6,14},{8,0},{10,2},{12,4},{14,6},{16,24},{18,... | collective-permute-start | bytes 73736 | tf_op jit(solution)/shard_map/ppermute | solution.py:13
  6.0 18.7 %collective-permute-start = (bf16[128,1536]{1,0:T(8,128)(2,1)}, bf16[128,1536]{1,0:T(8,128)(2,1)}, u32[]{:S(2)}, u32[]{:S(2)}) collective-permute-start(bf16[128,1536]{1,0:T(8,128)(2,1)} %param.5), channel_id=1, source_target_pairs={{1,0},{0,1},{3,2},{2,3},{5,4},{4,5},{7,6},{6,7},{9,8},{8,9},{11,10... | collective-permute-start | bytes 1179656 | tf_op jit(solution)/shard_map/ppermute | solution.py:17
  11.9 5.1 %collective-permute-start.2 = (bf16[16,1536]{1,0:T(8,128)(2,1)S(1)}, bf16[16,1536]{1,0:T(8,128)(2,1)S(1)}, u32[]{:S(2)}, u32[]{:S(2)}) collective-permute-start(bf16[16,1536]{1,0:T(8,128)(2,1)S(1)} %pad_maximum_fusion.2), channel_id=1, source_target_pairs={{0,16},{2,18},{4,20},{6,22},{8,24},{10,26},{12,28},{14,30},{16,0},... | collective-permute-start | bytes 147464 | tf_op jit(solution)/shard_map/ppermute | solution.py:13
  17.7 4.7 %collective-permute-start.3 = (bf16[32,1536]{1,0:T(8,128)(2,1)S(1)}, bf16[32,1536]{1,0:T(8,128)(2,1)S(1)}, u32[]{:S(2)}, u32[]{:S(2)}) collective-permute-start(bf16[32,1536]{1,0:T(8,128)(2,1)S(1)} %pad_maximum_fusion.1), channel_id=1, source_target_pairs={{0,4},{2,6},{4,0},{6,2},{8,12},{10,14},{12,8},{14,10},{16,20},{18,... | collective-permute-start | bytes 294920 | tf_op jit(solution)/shard_map/ppermute | solution.py:13
  23.2 1.5 %collective-permute-start.4 = (bf16[64,1536]{1,0:T(8,128)(2,1)S(1)}, bf16[64,1536]{1,0:T(8,128)(2,1)S(1)}, u32[]{:S(2)}, u32[]{:S(2)}) collective-permute-start(bf16[64,1536]{1,0:T(8,128)(2,1)S(1)} %pad_maximum_fusion), channel_id=1, source_target_pairs={{0,2},{2,0},{4,6},{6,4},{8,10},{10,8},{12,14},{14,12},{16,18},{18,... | collective-permute-start | bytes 589832 | tf_op jit(solution)/shard_map/ppermute | solution.py:13
  28.0 6.4 %copy-start.2 = (s32[128,7]{0,1:T(8,128)S(1)}, s32[128,7]{0,1:T(8,128)}, u32[]{:S(2)}) copy-start(s32[128,7]{0,1:T(8,128)} %param.8) | copy-start | bytes 10756
  28.0 6.3 %copy-start.3 = (s32[128]{0:T(128)S(1)}, s32[128]{0:T(128)}, u32[]{:S(2)}) copy-start(s32[128]{0:T(128)} %param.9) | copy-start | bytes 1540
  28.1 9.3 %copy-start.4 = (s32[128]{0:T(128)S(1)}, s32[128]{0:T(128)}, u32[]{:S(2)}) copy-start(s32[128]{0:T(128)} %add.103) | copy-start | bytes 1540
  30.9 6.5 %copy-start.1 = (bf16[256,1536]{1,0:T(8,128)(2,1)S(1)}, bf16[256,1536]{1,0:T(8,128)(2,1)}, u32[]{:S(2)}) copy-start(bf16[256,1536]{1,0:T(8,128)(2,1)} %constant_dynamic-update-slice_fusion) | copy-start | bytes 2359300
  32.5 3.7 %collective-permute-start.6 = (f32[2,256]{1,0:T(2,128)S(1)}, f32[2,256]{1,0:T(2,128)S(1)}, u32[]{:S(2)}, u32[]{:S(2)}) collective-permute-start(f32[2,256]{1,0:T(2,128)S(1)} %get-tuple-element.13), channel_id=1, source_target_pairs={{1,0},{0,1},{3,2},{2,3},{5,4},{4,5},{7,6},{6,7},{9,8},{8,9},{11,10... | collective-permute-start | bytes 6152 | tf_op jit(solution)/shard_map/ppermute | solution.py:17
  37.8 3.8 %collective-permute-start.8 = (bf16[64,1536]{1,0:T(8,128)(2,1)S(1)}, bf16[64,1536]{1,0:T(8,128)(2,1)S(1)}, u32[]{:S(2)}, u32[]{:S(2)}) collective-permute-start(bf16[64,1536]{1,0:T(8,128)(2,1)S(1)} %slice.154), channel_id=1, source_target_pairs={{0,2},{2,0},{4,6},{6,4},{8,10},{10,8},{12,14},{14,12},{16,18},{18,... | collective-permute-start | bytes 589832 | tf_op jit(solution)/shard_map/ppermute | solution.py:13
  41.6 5.4 %collective-permute-start.9 = (bf16[32,1536]{1,0:T(8,128)(2,1)S(1)}, bf16[32,1536]{1,0:T(8,128)(2,1)S(1)}, u32[]{:S(2)}, u32[]{:S(2)}) collective-permute-start(bf16[32,1536]{1,0:T(8,128)(2,1)S(1)} %slice.155), channel_id=1, source_target_pairs={{0,4},{2,6},{4,0},{6,2},{8,12},{10,14},{12,8},{14,10},{16,20},{18,... | collective-permute-start | bytes 294920 | tf_op jit(solution)/shard_map/ppermute | solution.py:13
  47.0 5.1 %collective-permute-start.10 = (bf16[16,1536]{1,0:T(8,128)(2,1)S(1)}, bf16[16,1536]{1,0:T(8,128)(2,1)S(1)}, u32[]{:S(2)}, u32[]{:S(2)}) collective-permute-start(bf16[16,1536]{1,0:T(8,128)(2,1)S(1)} %slice.156), channel_id=1, source_target_pairs={{0,16},{2,18},{4,20},{6,22},{8,24},{10,26},{12,28},{14,30},{16,0},... | collective-permute-start | bytes 147464 | tf_op jit(solution)/shard_map/ppermute | solution.py:13
  52.2 3.9 %collective-permute-start.11 = (bf16[8,1536]{1,0:T(8,128)(2,1)S(1)}, bf16[8,1536]{1,0:T(8,128)(2,1)S(1)}, u32[]{:S(2)}, u32[]{:S(2)}) collective-permute-start(bf16[8,1536]{1,0:T(8,128)(2,1)S(1)} %slice.157), channel_id=1, source_target_pairs={{0,8},{2,10},{4,12},{6,14},{8,0},{10,2},{12,4},{14,6},{16,24},{18,... | collective-permute-start | bytes 73736 | tf_op jit(solution)/shard_map/ppermute | solution.py:13
  52.6 9.8 %collective-permute-start.7 = (bf16[128,1536]{1,0:T(8,128)(2,1)S(1)}, bf16[128,1536]{1,0:T(8,128)(2,1)S(1)}, u32[]{:S(2)}, u32[]{:S(2)}) collective-permute-start(bf16[128,1536]{1,0:T(8,128)(2,1)S(1)} %fusion.3), channel_id=1, source_target_pairs={{1,0},{0,1},{3,2},{2,3},{5,4},{4,5},{7,6},{6,7},{9,8},{8,9},{11,10... | collective-permute-start | bytes 1179656 | tf_op jit(solution)/shard_map/ppermute | solution.py:17

commit v2 on v1

v2 whole, which is shorter than its diff:
```python
import functools

import jax
import jax.numpy as jnp
from jax import lax
from jax.experimental import pallas as pl
from jax.experimental.pallas import tpu as pltpu
from jax.sharding import PartitionSpec as P

VMEM = pl.BlockSpec(memory_space=pltpu.VMEM)
ANY = pl.BlockSpec(memory_space=pl.ANY)
HBM = pl.BlockSpec(memory_space=pltpu.HBM)
PARAMS = pltpu.CompilerParams(vmem_limit_bytes=40 * 2**20)
F32, BF16 = jnp.float32, jnp.bfloat16


def cost(micros):
    return pl.CostEstimate(flops=0, bytes_accessed=int(micros * 3.69e6), transcendentals=0)


NONE = -1e30


def across(x, axis, count, distance):
    return lax.ppermute(x, axis, [(i, i ^ distance) for i in range(count)])


def shifted(x, axis, count, distance):
    return lax.ppermute(x, axis, [((i + distance) % count, i) for i in range(count)])


def after(x, *others):
    return lax.optimization_barrier((x, *others))


def dot(a, b, over):
    return lax.dot_general(a, b, (over, ((), ())), preferred_element_type=F32)


ROWS_ROWS = ((1,), (1,))
ROWS_COLS = ((1,), (0,))
COLS_COLS = ((0,), (0,))


def count_ids(chunk, ids, times_ref):
    pool_rows, rows = times_ref.shape
    ids = ids - lax.axis_index("shard") * pool_rows
    for c in range(0, pool_rows, chunk):
        slot = lax.broadcasted_iota(jnp.int32, (chunk, rows), 0) + c
        times = jnp.zeros((chunk, rows), F32)
        for k in range(ids.shape[0]):
            times = times + jnp.where(slot == ids[k : k + 1, :], 1.0, 0.0)
        times_ref[c : c + chunk, :] = times


def scores_of(chunk, scaling, q_ref, pool_ref, hard_ref, times_ref, stat_ref, ready):
    pool_rows, rows = hard_ref.shape
    top = jnp.full((1, rows), NONE, F32)
    for c in range(0, pool_rows, chunk):
        ready(c)
        score = dot(pool_ref[c : c + chunk, :], q_ref[...], ROWS_ROWS) * scaling
        score = jnp.where(times_ref[c : c + chunk, :] > 0, score, NONE)
        hard_ref[c : c + chunk, :] = score
        top = jnp.maximum(top, jnp.max(score, axis=0, keepdims=True))
    total = jnp.zeros((1, rows), F32)
    for c in range(0, pool_rows, chunk):
        part = times_ref[c : c + chunk, :] * jnp.exp(hard_ref[c : c + chunk, :] - top)
        total = total + jnp.sum(part, axis=0, keepdims=True)
    stat_ref[0:1, :] = top
    stat_ref[1:2, :] = total


def own_kernel(
    chunk, scaling, ids_ref, pos_ref, tile_ref, q_ref, pool_ref,
    tile_here, all_q_ref, pool_here, marks_ref, hard_ref, times_ref, stat_ref, sems,
):
    rows = q_ref.shape[0]
    neg_count = ids_ref.shape[0]
    half = pool_ref.shape[0] // 2
    marks = [
        pltpu.make_async_copy(ids_ref, marks_ref.at[0:neg_count, :], sems.at[0]),
        pltpu.make_async_copy(pos_ref, marks_ref.at[neg_count : neg_count + 1, :], sems.at[1]),
    ]
    others = [
        pltpu.make_async_copy(q_ref, all_q_ref.at[0:rows, :], sems.at[2]),
        pltpu.make_async_copy(tile_ref, tile_here, sems.at[3]),
    ]
    halves = [
        pltpu.make_async_copy(
            pool_ref.at[c : c + half, :], pool_here.at[c : c + half, :], sems.at[4 + c // half]
        )
        for c in (0, half)
    ]
    for copy in marks + others + halves:
        copy.start()
    for copy in marks:
        copy.wait()
    count_ids(chunk, marks_ref[0:neg_count, :], times_ref)
    for copy in others:
        copy.wait()

    def ready(c):
        if c % half == 0:
            halves[c // half].wait()

    scores_of(
        chunk, scaling, all_q_ref.at[0:rows, :], pool_here, hard_ref, times_ref, stat_ref, ready
    )


def hard_shapes(pool_rows, rows):
    return [
        pltpu.VMEM((pool_rows, rows), F32),
        pltpu.VMEM((pool_rows, rows), F32),
        pltpu.VMEM((2, rows), F32),
    ]


def own_scores(pieces, ids, pos, tile, q, pool):
    rows, features = q.shape
    pool_rows = pool.shape[0]
    chunk = min(pool_rows, 128)
    return pl.pallas_call(
        functools.partial(own_kernel, chunk, features ** (-0.5)),
        in_specs=[HBM] * 5,
        out_specs=[VMEM] * 7,
        out_shape=[
            pltpu.VMEM(tile.shape, BF16),
            pltpu.VMEM((pieces * rows, features), BF16),
            pltpu.VMEM((pool_rows, features), BF16),
            pltpu.VMEM((ids.shape[0] + 1, rows), jnp.int32),
        ]
        + hard_shapes(pool_rows, rows),
        scratch_shapes=[pltpu.SemaphoreType.DMA((6,))],
        compiler_params=PARAMS,
        cost_estimate=cost(20),
        name="own_scores",
    )(*(pltpu.with_memory_space_constraint(x, pltpu.HBM) for x in (ids, pos, tile, q, pool)))


def group_kernel(piece, chunk, scaling, marks_ref, q_ref, pool_ref, _, all_q_ref, hard_ref, times_ref, stat_ref):
    rows = q_ref.shape[0]
    all_q_ref[piece * rows : (piece + 1) * rows, :] = q_ref[...]
    count_ids(chunk, marks_ref[0 : marks_ref.shape[0] - 1, :], times_ref)
    scores_of(
        chunk, scaling, q_ref, pool_ref, hard_ref, times_ref, stat_ref, lambda c: None
    )


def group_scores(piece, marks, q, pool, all_q):
    rows, features = q.shape
    pool_rows = pool.shape[0]
    return pl.pallas_call(
        functools.partial(group_kernel, piece, min(pool_rows, 128), features ** (-0.5)),
        in_specs=[VMEM] * 3 + [ANY],
        out_specs=[VMEM] * 4,
        out_shape=[jax.ShapeDtypeStruct(all_q.shape, BF16)] + hard_shapes(pool_rows, rows),
        input_output_aliases={3: 0},
        compiler_params=PARAMS,
        cost_estimate=cost(20),
        name="group_scores",
    )(marks, q, pool, all_q)


def score_kernel(scaling, keys_ref, q_ref, *refs):
    score_ref, part_ref = refs[-2:]
    stats = [r[...] for r in refs[:-2]]
    score = dot(keys_ref[...], q_ref[...], ROWS_ROWS) * scaling
    score_ref[...] = score
    stat = jnp.concatenate(stats, axis=1)
    hard_top, hard_sum = stat[0:1, :], stat[1:2, :]
    top = jnp.maximum(hard_top, jnp.max(score, axis=0, keepdims=True))
    part_ref[0:1, :] = top
    part_ref[1:2, :] = hard_sum * jnp.exp(hard_top - top) + jnp.sum(
        jnp.exp(score - top), axis=0, keepdims=True
    )


def passage_scores(keys, all_q, stats):
    held, group = keys.shape[0], all_q.shape[0]
    return pl.pallas_call(
        functools.partial(score_kernel, keys.shape[1] ** (-0.5)),
        in_specs=[VMEM] * (2 + len(stats)),
        out_specs=[VMEM] * 2,
        out_shape=[
            jax.ShapeDtypeStruct((held, group), F32),
            jax.ShapeDtypeStruct((2, group), F32),
        ],
        compiler_params=PARAMS,
        name="passage_scores",
    )(keys, all_q, *stats)


def weight_kernel(far, tile, owners, scaling, score_ref, q_ref, part_ref, other_ref, *refs):
    w_ref, log_ref, keep_ref, send_ref = refs[-4:]
    pos = jnp.concatenate([r[r.shape[0] - 1 :, :] for r in refs[:-4]], axis=1)
    held, group = score_ref.shape
    rows = group // owners
    if owners == 2:
        other = other_ref[...]
        parts = [
            part_ref[...],
            jnp.concatenate([other[:, rows:], other[:, :rows]], axis=1),
        ]
    else:
        parts = [other_ref[d] for d in range(owners)]
    top = functools.reduce(jnp.maximum, [p[0:1, :] for p in parts])
    total = sum(p[1:2, :] * jnp.exp(p[0:1, :] - top) for p in parts)
    log_total = top + jnp.log(total)
    log_ref[...] = log_total
    line = lax.broadcasted_iota(jnp.int32, (held, 1), 0)
    place = line // tile
    key_blk = (place % far) * 4 + ((place // far) % 2) * 2 + place // (2 * far)
    key_blk = key_blk ^ lax.axis_index("blk")
    key_id = (key_blk * owners + lax.axis_index("shard")) * tile + line % tile
    hit = jnp.where(key_id == pos, 1.0, 0.0)
    w = (jnp.exp(score_ref[...] - log_total) - hit).astype(BF16)
    w_ref[...] = w
    half = held // 2
    keep_ref[...] = dot(w[:half], q_ref[...], ROWS_COLS) * scaling
    send_ref[...] = (dot(w[half:], q_ref[...], ROWS_COLS) * scaling).astype(BF16)


def passage_weights(far, tile, owners, score, all_q, part, other, pos):
    held, group = score.shape
    features = all_q.shape[1]
    return pl.pallas_call(
        functools.partial(weight_kernel, far, tile, owners, features ** (-0.5)),
        in_specs=[VMEM] * (4 + len(pos)),
        out_specs=[VMEM] * 4,
        out_shape=[
            jax.ShapeDtypeStruct((held, group), BF16),
            jax.ShapeDtypeStruct((1, group), F32),
            jax.ShapeDtypeStruct((held // 2, features), F32),
            jax.ShapeDtypeStruct((held // 2, features), BF16),
        ],
        compiler_params=PARAMS,
        name="passage_weights",
    )(score, all_q, part, other, *pos)


def query_kernel(piece, scaling, hard_ref, times_ref, log_ref, w_ref, keys_ref, pool_ref, grad_ref, hw_ref):
    rows = hard_ref.shape[1]
    here = slice(piece * rows, (piece + 1) * rows)
    w = jnp.exp(hard_ref[...] - log_ref[:, here]).astype(BF16).astype(F32)
    hw = (times_ref[...] * w).astype(BF16)
    hw_ref[...] = hw
    grad = dot(hw, pool_ref[...], COLS_COLS) + dot(w_ref[:, here], keys_ref[...], COLS_COLS)
    grad_ref[...] = (grad * scaling).astype(grad_ref.dtype)


def query_part(piece, hard, times, log_total, w, keys, pool, dtype, micros=10):
    pool_rows, rows = hard.shape
    features = pool.shape[1]
    return pl.pallas_call(
        functools.partial(query_kernel, piece, features ** (-0.5)),
        in_specs=[VMEM] * 6,
        out_specs=[VMEM] * 2,
        out_shape=[
            jax.ShapeDtypeStruct((rows, features), dtype),
            jax.ShapeDtypeStruct((pool_rows, rows), BF16),
        ],
        compiler_params=PARAMS,
        cost_estimate=cost(micros),
        name="query_part",
    )(hard, times, log_total, w, keys, pool)


def pool_kernel(first, chunk, scaling, owners, q_ref, *refs):
    weights, (out_ref, buffer, sems) = refs[:owners], refs[-3:]
    copies = []
    for c in range(0, buffer.shape[0], chunk):
        w = jnp.concatenate([r[first + c : first + c + chunk, :] for r in weights], axis=1)
        buffer[c : c + chunk, :] = dot(w, q_ref[...], ROWS_COLS) * scaling
        copy = pltpu.make_async_copy(
            buffer.at[c : c + chunk, :],
            out_ref.at[first + c : first + c + chunk, :],
            sems.at[c // chunk],
        )
        copy.start()
        copies.append(copy)
    for copy in copies:
        copy.wait()


def pool_rows_grad(first, count, all_q, weights, so_far, micros):
    pool_rows = weights[0].shape[0]
    features = all_q.shape[1]
    chunk = min(count, 128)
    earlier = [] if so_far is None else [so_far]
    return pl.pallas_call(
        functools.partial(pool_kernel, first, chunk, features ** (-0.5), len(weights)),
        in_specs=[VMEM] * (1 + len(weights)) + [ANY] * len(earlier),
        out_specs=ANY,
        out_shape=jax.ShapeDtypeStruct((pool_rows, features), F32),
        scratch_shapes=[
            pltpu.VMEM((count, features), F32),
            pltpu.SemaphoreType.DMA((count // chunk,)),
        ],
        input_output_aliases={1 + len(weights): 0} if earlier else {},
        compiler_params=PARAMS,
        cost_estimate=cost(micros),
        name="pool_grad",
    )(all_q, *weights, *earlier)


def sum_kernel(chunk, *refs):
    terms, (out_ref, buffer, sems) = refs[:-3], refs[-3:]
    copies = []
    for c in range(0, buffer.shape[0], chunk):
        here = slice(c, c + chunk)
        buffer[here, :] = functools.reduce(jnp.add, [t[here, :].astype(F32) for t in terms])
        copy = pltpu.make_async_copy(
            buffer.at[here, :], out_ref.at[here, :], sems.at[c // chunk]
        )
        copy.start()
        copies.append(copy)
    for copy in copies:
        copy.wait()


def sum_terms(terms):
    rows = terms[0].shape[0]
    chunk = min(rows, 32)
    return pl.pallas_call(
        functools.partial(sum_kernel, chunk),
        in_specs=[VMEM] * len(terms),
        out_specs=ANY,
        out_shape=jax.ShapeDtypeStruct(terms[0].shape, F32),
        scratch_shapes=[
            pltpu.VMEM(terms[0].shape, F32),
            pltpu.SemaphoreType.DMA((rows // chunk,)),
        ],
        compiler_params=PARAMS,
        cost_estimate=cost(20),
        name="query_grad",
    )(*terms)


def body(queries, passages, neg_pool, hard_ids, positives):
    rows = queries.shape[0]
    tile = passages.shape[0]
    owners = lax.axis_size("shard")
    blocks = lax.axis_size("blk")
    my_shard = lax.axis_index("shard")

    group_q = [shifted(queries, "shard", owners, d) for d in range(1, owners)]
    my_tile, all_q, pool, marks, *found = own_scores(
        owners, hard_ids.T, positives.reshape(1, rows), passages, queries, neg_pool
    )
    group_marks = [marks] + [shifted(marks, "shard", owners, d) for d in range(1, owners)]
    hard = [found]
    for d in range(1, owners):
        all_q, *found = group_scores(d, group_marks[d], group_q[d - 1], pool, all_q)
        hard.append(found)

    far = blocks // 4
    keys = jnp.concatenate([my_tile] + [across(passages, "blk", blocks, 4 * z) for z in range(1, far)], axis=0)
    keys = lax.optimization_barrier(keys)
    for bit in (2, 1):
        if bit == 1:
            keys, hard, all_q = after(keys, hard, all_q)
        keys = lax.optimization_barrier(
            jnp.concatenate([keys, across(keys, "blk", blocks, bit)], axis=0)
        )

    score, part = passage_scores(keys, all_q, [h[2] for h in hard])
    if owners == 2:
        other = shifted(part, "shard", owners, 1)
    else:
        other = lax.all_gather(jnp.roll(part, my_shard * rows, axis=1), "shard", axis=0)
        other = jnp.roll(other, -my_shard * rows, axis=2)
    w, log_total, keep, send = passage_weights(
        far, tile, owners, score, all_q, part, other, group_marks
    )

    for step, bit in enumerate((1, 2)):
        got = across(send, "blk", blocks, bit).astype(F32)
        passage_grad = keep + got
        half = passage_grad.shape[0] // 2
        keep, send = passage_grad[:half], passage_grad[half:].astype(BF16)
        if step == 0:
            made = [
                query_part(d, hard[d][0], hard[d][1], log_total, w, keys, pool, BF16)
                for d in range(1, owners)
            ]
            own, own_w = query_part(0, hard[0][0], hard[0][1], log_total, w, keys, pool, F32)
            keep, send, made, own = after(keep, send, made, own)
            back = [
                shifted(grad, "shard", owners, owners - d) for d, (grad, _) in enumerate(made, 1)
            ]
            hard_w = [own_w] + [hw for _, hw in made]
    sent = passage_grad[tile:].astype(BF16)
    far_terms = [
        across(sent[(z - 1) * tile : z * tile], "blk", blocks, 4 * z) for z in range(1, far)
    ]
    pool_grad = pool_rows_grad(0, neg_pool.shape[0], all_q, hard_w, None, 20)
    query_grad = sum_terms([own] + back)
    passage_grad, pool_grad, query_grad = after(passage_grad, pool_grad, query_grad)
    passage_grad = passage_grad[:tile] + sum(t.astype(F32) for t in far_terms)

    return query_grad, passage_grad, pool_grad


def solution(mesh):
    both = P(("blk", "shard"), None)
    in_specs = (both, both, both, both, P(("blk", "shard")))
    return jax.shard_map(
        body, mesh=mesh, in_specs=in_specs, out_specs=(both, both, both), check_vma=False
    )
```

time: 64.1 us -> 40.6 us (0.63)
  matrix products: 11 us -> 0 us
  waiting for transfers between devices: 19.9 us -> 9.53 us
  Pallas kernels: 0 us -> 10.2 us
  other arithmetic: 8.11 us -> 0.74 us
  local copies, waits for them, and re-layouts: 5.75 us -> 0.04 us
  starting transfers between devices: 17.8 us -> 19.1 us
    dot_general x8 -> x0, matrix products: 11 us -> none  [the longest x2 4.38 us: dots(): lax.dot_general(a, b, (((1,), (1,)), ((), ())), preferred_element_type=jn...]
    pallas_call x0 -> x8, Pallas kernels: none -> 10.2 us  [the longest x1 3.01 us: pool_rows_grad(): pl.pallas_call(functools.partial(pool_kernel, first, chunk, features ** (...]
    ppermute x8 -> x10, waiting for transfers between devices: 12.5 us -> 6.21 us  [across(): return lax.ppermute(x, axis, [(i, i ^ distance) for i in range(count)])]
    ppermute x4, waiting for transfers between devices: 7.37 us -> 3.32 us  [shifted(): lax.ppermute(x, axis, [((i + distance) % count, i) for i in range(count)])]
    concatenate x6 -> x3, other arithmetic: 3.88 us -> 0.05 us  [the longest x2 0.04 us: body(): jnp.concatenate([keys, across(keys, 'blk', blocks, bit)], axis=0)]
    unnamed x15 -> x0, local copies, waits for them, and re-layouts: 3.29 us -> none
    ppermute x8 -> x10, starting transfers between devices: 10.7 us -> 13.1 us  [across(): return lax.ppermute(x, axis, [(i, i ^ distance) for i in range(count)])]
    concatenate x2 -> x0, local copies, waits for them, and re-layouts: 1.78 us -> none  [the longest x1 1.77 us: body(): jnp.concatenate([queries] + [shifted(queries, 'shard', owners, d) for d i...]
  transfers between devices with their start and end apart: 12 -> 14, of which waited for: 8 -> 8; matrix products, arithmetic and copies ran while one was open for 21% -> 0% of each run, Pallas kernels for 0% -> 20%
where the time goes in v2:
time: 40.6 us; the launch traced here: 40.4 us
  starting transfers between devices  19.1 us (47%)
  Pallas kernels  10.2 us (25%)
  waiting for transfers between devices  9.53 us (23%)
  between operations  0.79 us (2%)
  other arithmetic  0.74 us (2%)
    ppermute x10, starting transfers between devices, across(): return lax.ppermute(x, axis, [(i, i ^ distance) for i in range(count)])  13.1 us
    ppermute x10, waiting for transfers between devices, across(): return lax.ppermute(x, axis, [(i, i ^ distance) for i in range(count)])  6.21 us
    ppermute x4, starting transfers between devices, shifted(): lax.ppermute(x, axis, [((i + distance) % count, i) for i in range(count)])  6.04 us
    ppermute x4, waiting for transfers between devices, shifted(): lax.ppermute(x, axis, [((i + distance) % count, i) for i in range(count)])  3.32 us
    pallas_call x1, Pallas kernels, pool_rows_grad(): pl.pallas_call(functools.partial(pool_kernel, first, chunk, features ** (...  3.01 us
    pallas_call x1, Pallas kernels, own_scores(): pl.pallas_call(functools.partial(own_kernel, chunk, features ** (-0.5)),...  2.9 us
    pallas_call x2, Pallas kernels, query_part(): pl.pallas_call(functools.partial(query_kernel, piece, features ** (-0.5))...  1.44 us
    pallas_call x1, Pallas kernels, group_scores(): pl.pallas_call(functools.partial(group_kernel, piece, min(pool_rows, 128)...  1.11 us
  transfers between devices with their start and end apart: 14, of which 8 were waited for; matrix products, arithmetic and copies ran while one was open for 0% of the time, Pallas kernels for 20%

profile of v2, /device:TPU:0, one launch (start us, length us, event | category | flops | bytes accessed | tf_op | source)
XLA Modules:
  0.0 40.4 jit_solution(14865047672710746445)
XLA Ops:
  0.6 3.1 %collective-permute-start = (bf16[8,1536]{1,0:T(8,128)(2,1)}, bf16[8,1536]{1,0:T(8,128)(2,1)S(1)}, u32[]{:S(2)}, u32[]{:S(2)}) collective-permute-start(bf16[8,1536]{1,0:T(8,128)(2,1)} %tile_ref.1), channel_id=1, source_target_pairs={{0,8},{2,10},{4,12},{6,14},{8,0},{10,2},{12,4},{14,6},{16,24},{18,... | collective-permute-start | bytes 73736 | tf_op jit(solution)/shard_map/ppermute | solution.py:25
  3.7 2.5 %collective-permute-start.2 = (bf16[8,1536]{1,0:T(8,128)(2,1)}, bf16[8,1536]{1,0:T(8,128)(2,1)S(1)}, u32[]{:S(2)}, u32[]{:S(2)}) collective-permute-start(bf16[8,1536]{1,0:T(8,128)(2,1)} %tile_ref.1), channel_id=1, source_target_pairs={{0,24},{2,26},{4,28},{6,30},{8,16},{10,18},{12,20},{14,22},{16,8},... | collective-permute-start | bytes 73736 | tf_op jit(solution)/shard_map/ppermute | solution.py:25
  6.2 0.1 collective-permute-start.1
  6.3 1.5 %collective-permute-start.5 = (bf16[128,1536]{1,0:T(8,128)(2,1)}, bf16[128,1536]{1,0:T(8,128)(2,1)S(1)}, u32[]{:S(2)}, u32[]{:S(2)}) collective-permute-start(bf16[128,1536]{1,0:T(8,128)(2,1)} %q_ref.1), channel_id=1, source_target_pairs={{1,0},{0,1},{3,2},{2,3},{5,4},{4,5},{7,6},{6,7},{9,8},{8,9},{11,10... | collective-permute-start | bytes 1179656 | tf_op jit(solution)/shard_map/ppermute | solution.py:29
  7.8 2.9 %own_scores.1 = (bf16[8,1536]{1,0:T(8,128)(2,1)S(1)}, bf16[256,1536]{1,0:T(8,128)(2,1)S(1)}, bf16[1024,1536]{1,0:T(8,128)(2,1)S(1)}, s32[8,128]{1,0:T(8,128)S(1)...) custom-call(s32[7,128]{1,0:T(8,128)} %bitcast.2, s32[1,128]{1,0:T(1,128)} %bitcast.3, ...), custom_call_target="tpu_custom_call" | custom-call | bytes 73800000 | tf_op jit(solution)/shard_map/own_scores/pallas_call | solution.py:123
  10.7 0.0 collective-permute-done
  10.7 0.0 collective-permute-done.2
  10.7 0.7 %collective-permute-done.1 = bf16[8,1536]{1,0:T(8,128)(2,1)S(1)} collective-permute-done((bf16[8,1536]{1,0:T(8,128)(2,1)}, bf16[8,1536]{1,0:T(8,128)(2,1)S(1)}, u32[]{:S(2)}, u32[]{:S(2)}) %collective-permute-start.1) | collective-permute-done | bytes 24608 | tf_op jit(solution)/shard_map/ppermute | solution.py:25
  11.4 1.6 %collective-permute-start.3 = (bf16[32,1536]{1,0:T(8,128)(2,1)S(1)}, bf16[32,1536]{1,0:T(8,128)(2,1)S(1)}, u32[]{:S(2)}, u32[]{:S(2)}) collective-permute-start(bf16[32,1536]{1,0:T(8,128)(2,1)S(1)} %pad_maximum_fusion.2), channel_id=1, source_target_pairs={{0,4},{2,6},{4,0},{6,2},{8,12},{10,14},{12,8},{14,10},{16,20},{18,... | collective-permute-start | bytes 294920 | tf_op jit(solution)/shard_map/ppermute | solution.py:25
  13.0 1.5 %collective-permute-start.4 = (s32[8,128]{1,0:T(8,128)S(1)}, s32[8,128]{1,0:T(8,128)S(1)}, u32[]{:S(2)}, u32[]{:S(2)}) collective-permute-start(s32[8,128]{1,0:T(8,128)S(1)} %get-tuple-element.44.refs_0_), channel_id=1, source_target_pairs={{1,0},{0,1},{3,2},{2,3},{5,4},{4,5},{7,6},{6,7},{9,8},{8,9},{11,10... | collective-permute-start | bytes 12296 | tf_op jit(solution)/shard_map/ppermute | solution.py:29
  14.5 1.6 %collective-permute-done.3 = bf16[32,1536]{1,0:T(8,128)(2,1)S(1)} collective-permute-done((bf16[32,1536]{1,0:T(8,128)(2,1)S(1)}, bf16[32,1536]{1,0:T(8,128)(2,1)S(1)}, u32[]{:S(2)}, u32[]{:S(2)}) %collective-permute-start.3) | collective-permute-done | bytes 98336 | tf_op jit(solution)/shard_map/ppermute | solution.py:25
  16.1 0.8 %collective-permute-done.4.marks_ref.refs_1_ = s32[8,128]{1,0:T(8,128)S(1)} collective-permute-done((s32[8,128]{1,0:T(8,128)S(1)}, s32[8,128]{1,0:T(8,128)S(1)}, u32[]{:S(2)}, u32[]{:S(2)}) %collective-permute-start.4) | collective-permute-done | bytes 4128 | tf_op jit(solution)/shard_map/ppermute | solution.py:29
  16.9 1.1 %group_scores.1 = (bf16[256,1536]{1,0:T(8,128)(2,1)S(1)}, f32[1024,128]{1,0:T(8,128)S(1)}, f32[1024,128]{1,0:T(8,128)S(1)}, f32[2,128]{1,0:T(2,128)S(1)}) custom-call(s32[8,128]{1,0:T(8,128)S(1)} %collective-permute-done.4.marks_ref.refs_1_, bf16[128,1536]{1,0:T(8,128)(2,1)S(1)} %collective-permute-done.5.q_ref, ...), custom_call_target="tpu_custom_call", output_to_operand_aliasing={{0}: (3, {})} | custom-call | bytes 73800000 | tf_op jit(solution)/shard_map/group_scores/pallas_call | solution.py:153
  18.0 0.1 collective-permute-start.6
  18.1 1.4 %collective-permute-done.6 = bf16[64,1536]{1,0:T(8,128)(2,1)S(1)} collective-permute-done((bf16[64,1536]{1,0:T(8,128)(2,1)S(1)}, bf16[64,1536]{1,0:T(8,128)(2,1)S(1)}, u32[]{:S(2)}, u32[]{:S(2)}) %collective-permute-start.6) | collective-permute-done | bytes 196640 | tf_op jit(solution)/shard_map/ppermute | solution.py:25
  19.6 0.4 %passage_scores.1 = (f32[128,256]{1,0:T(8,128)S(1)}, f32[2,256]{1,0:T(2,128)S(1)}) custom-call(bf16[128,1536]{1,0:T(8,128)(2,1)S(1)} %pad_maximum_fusion.keys_ref, bf16[256,1536]{1,0:T(8,128)(2,1)S(1)} %get-tuple-element.52.q_ref, f32[2,128]{1,0:T(2,128)S(1)} %get-tuple-element.53.refs_0_, f32[2,128]{1,0:T(2,128)S(1)} %get-tuple-element.54.refs_1_), custom_call_target="tpu_custom_call" | custom-call | tf_op jit(solution)/shard_map/passage_scores/pallas_call | solution.py:181
  20.0 1.6 %collective-permute-start.7 = (f32[2,256]{1,0:T(2,128)S(1)}, f32[2,256]{1,0:T(2,128)S(1)}, u32[]{:S(2)}, u32[]{:S(2)}) collective-permute-start(f32[2,256]{1,0:T(2,128)S(1)} %get-tuple-element.56.part_ref), channel_id=1, source_target_pairs={{1,0},{0,1},{3,2},{2,3},{5,4},{4,5},{7,6},{6,7},{9,8},{8,9},{11,10... | collective-permute-start | bytes 6152 | tf_op jit(solution)/shard_map/ppermute | solution.py:29
  21.6 2.1 %collective-permute-done.7.other_ref = f32[2,256]{1,0:T(2,128)S(1)} collective-permute-done((f32[2,256]{1,0:T(2,128)S(1)}, f32[2,256]{1,0:T(2,128)S(1)}, u32[]{:S(2)}, u32[]{:S(2)}) %collective-permute-start.7) | collective-permute-done | bytes 2080 | tf_op jit(solution)/shard_map/ppermute | solution.py:29
  23.6 0.4 %passage_weights.1 = (bf16[128,256]{1,0:T(8,128)(2,1)S(1)}, f32[1,256]{1,0:T(1,128)S(1)}, f32[64,1536]{1,0:T(8,128)S(1)}, bf16[64,1536]{1,0:T(8,128)(2,1)S(1)}) custom-call(f32[128,256]{1,0:T(8,128)S(1)} %get-tuple-element.55.score_ref, bf16[256,1536]{1,0:T(8,128)(2,1)S(1)} %get-tuple-element.52.q_ref, f32[2,256]{1,0:T(2,128)S(1)} %get-tuple-element.56.part_ref, ...), custom_call_target="tpu_custom_call" | custom-call | tf_op jit(solution)/shard_map/passage_weights/pallas_call | solution.py:227
  24.1 0.1 collective-permute-start.8
  24.1 0.7 %query_part.2 = (bf16[128,1536]{1,0:T(8,128)(2,1)S(1)}, bf16[1024,128]{1,0:T(8,128)(2,1)S(1)}) custom-call(f32[1024,128]{1,0:T(8,128)S(1)} %get-tuple-element.59.hard_ref, f32[1024,128]{1,0:T(8,128)S(1)} %get-tuple-element.60.times_ref, f32[1,256]{1,0:T(1,128)S(1)} %get-tuple-element.61.log_ref, bf16[128,256]{1,0:T(8,128)(2,1)S(1)} %get-tuple-element.62.w_ref, ...), custom_call_target="tpu_custom_call" | custom-call | bytes 36900000 | tf_op jit(solution)/shard_map/query_part/pallas_call | solution.py:255
  24.9 0.7 %query_part.3 = (f32[128,1536]{1,0:T(8,128)S(1)}, bf16[1024,128]{1,0:T(8,128)(2,1)S(1)}) custom-call(f32[1024,128]{1,0:T(8,128)S(1)} %get-tuple-element.65.hard_ref, f32[1024,128]{1,0:T(8,128)S(1)} %get-tuple-element.66.times_ref, f32[1,256]{1,0:T(1,128)S(1)} %get-tuple-element.61.log_ref, bf16[128,256]{1,0:T(8,128)(2,1)S(1)} %get-tuple-element.62.w_ref, ...), custom_call_target="tpu_custom_call" | custom-call | bytes 36900000 | tf_op jit(solution)/shard_map/query_part/pallas_call | solution.py:255
  25.7 1.6 %collective-permute-start.9 = (bf16[32,1536]{1,0:T(8,128)(2,1)S(1)}, bf16[32,1536]{1,0:T(8,128)(2,1)S(1)}, u32[]{:S(2)}, u32[]{:S(2)}) collective-permute-start(bf16[32,1536]{1,0:T(8,128)(2,1)S(1)} %slice.37), channel_id=1, source_target_pairs={{0,4},{2,6},{4,0},{6,2},{8,12},{10,14},{12,8},{14,10},{16,20},{18,... | collective-permute-start | bytes 294920 | tf_op jit(solution)/shard_map/ppermute | solution.py:25
  27.3 1.5 %collective-permute-start.10 = (bf16[128,1536]{1,0:T(8,128)(2,1)S(1)}, bf16[128,1536]{1,0:T(8,128)(2,1)S(1)}, u32[]{:S(2)}, u32[]{:S(2)}) collective-permute-start(bf16[128,1536]{1,0:T(8,128)(2,1)S(1)} %get-tuple-element.73), channel_id=1, source_target_pairs={{1,0},{0,1},{3,2},{2,3},{5,4},{4,5},{7,6},{6,7},{9,8},{8,9},{11,10... | collective-permute-start | bytes 1179656 | tf_op jit(solution)/shard_map/ppermute | solution.py:29
  28.8 2.2 %collective-permute-done.9 = bf16[32,1536]{1,0:T(8,128)(2,1)S(1)} collective-permute-done((bf16[32,1536]{1,0:T(8,128)(2,1)S(1)}, bf16[32,1536]{1,0:T(8,128)(2,1)S(1)}, u32[]{:S(2)}, u32[]{:S(2)}) %collective-permute-start.9) | collective-permute-done | bytes 98336 | tf_op jit(solution)/shard_map/ppermute | solution.py:25
  31.0 1.6 %collective-permute-start.11 = (bf16[8,1536]{1,0:T(8,128)(2,1)S(1)}, bf16[8,1536]{1,0:T(8,128)(2,1)S(1)}, u32[]{:S(2)}, u32[]{:S(2)}) collective-permute-start(bf16[8,1536]{1,0:T(8,128)(2,1)S(1)} %get-tuple-element.79), channel_id=1, source_target_pairs={{0,8},{2,10},{4,12},{6,14},{8,0},{10,2},{12,4},{14,6},{16,24},{18,... | collective-permute-start | bytes 73736 | tf_op jit(solution)/shard_map/ppermute | solution.py:25
  32.6 2.5 %collective-permute-start.13 = (bf16[8,1536]{1,0:T(8,128)(2,1)S(1)}, bf16[8,1536]{1,0:T(8,128)(2,1)S(1)}, u32[]{:S(2)}, u32[]{:S(2)}) collective-permute-start(bf16[8,1536]{1,0:T(8,128)(2,1)S(1)} %get-tuple-element.80), channel_id=1, source_target_pairs={{0,24},{2,26},{4,28},{6,30},{8,16},{10,18},{12,20},{14,22},{16,8},... | collective-permute-start | bytes 73736 | tf_op jit(solution)/shard_map/ppermute | solution.py:25
  35.1 3.0 %pool_grad.1 = f32[1024,1536]{1,0:T(8,128)} custom-call(bf16[256,1536]{1,0:T(8,128)(2,1)S(1)} %get-tuple-element.52.q_ref, bf16[1024,128]{1,0:T(8,128)(2,1)S(1)} %get-tuple-element.70.refs_0_, bf16[1024,128]{1,0:T(8,128)(2,1)S(1)} %get-tuple-element.71.refs_1_), custom_call_target="tpu_custom_call" | custom-call | bytes 73800000 | tf_op jit(solution)/shard_map/pool_grad/pallas_call | solution.py:291
  38.1 0.4 %collective-permute-done.10.refs_1_ = bf16[128,1536]{1,0:T(8,128)(2,1)S(1)} collective-permute-done((bf16[128,1536]{1,0:T(8,128)(2,1)S(1)}, bf16[128,1536]{1,0:T(8,128)(2,1)S(1)}, u32[]{:S(2)}, u32[]{:S(2)}) %collective-permute-start.10) | collective-permute-done | bytes 393248 | tf_op jit(solution)/shard_map/ppermute | solution.py:29
  38.5 0.9 %query_grad.1 = f32[128,1536]{1,0:T(8,128)} custom-call(f32[128,1536]{1,0:T(8,128)S(1)} %get-tuple-element.72.refs_0_, bf16[128,1536]{1,0:T(8,128)(2,1)S(1)} %collective-permute-done.10.refs_1_), custom_call_target="tpu_custom_call" | custom-call | bytes 73800000 | tf_op jit(solution)/shard_map/query_grad/pallas_call | solution.py:325
  39.5 0.3 collective-permute-done.12
  39.8 0.6 %add_add_fusion = f32[8,1536]{1,0:T(8,128)} fusion(bf16[8,1536]{1,0:T(8,128)(2,1)S(1)} %collective-permute-done.13, bf16[8,1536]{1,0:T(8,128)(2,1)S(1)} %collective-permute-done.12, bf16[8,1536]{1,0:T(8,128)(2,1)S(1)} %collective-permute-done.11, f32[32,1536]{1,0:T(8,128)S(1)} %get-tuple-element.75), kind=kLoop, calls=%fused_computation.6 | loop fusion | flops 73728 | bytes 172032 | tf_op jit(solution)/shard_map/add | solution.py:400
  (13 shorter events, 0.2 us)
Async XLA Ops:
  0.6 10.1 %collective-permute-start = (bf16[8,1536]{1,0:T(8,128)(2,1)}, bf16[8,1536]{1,0:T(8,128)(2,1)S(1)}, u32[]{:S(2)}, u32[]{:S(2)}) collective-permute-start(bf16[8,1536]{1,0:T(8,128)(2,1)} %tile_ref.1), channel_id=1, source_target_pairs={{0,8},{2,10},{4,12},{6,14},{8,0},{10,2},{12,4},{14,6},{16,24},{18,... | collective-permute-start | bytes 73736 | tf_op jit(solution)/shard_map/ppermute | solution.py:25
  3.7 7.0 %collective-permute-start.2 = (bf16[8,1536]{1,0:T(8,128)(2,1)}, bf16[8,1536]{1,0:T(8,128)(2,1)S(1)}, u32[]{:S(2)}, u32[]{:S(2)}) collective-permute-start(bf16[8,1536]{1,0:T(8,128)(2,1)} %tile_ref.1), channel_id=1, source_target_pairs={{0,24},{2,26},{4,28},{6,30},{8,16},{10,18},{12,20},{14,22},{16,8},... | collective-permute-start | bytes 73736 | tf_op jit(solution)/shard_map/ppermute | solution.py:25
  6.2 5.2 %collective-permute-start.1 = (bf16[8,1536]{1,0:T(8,128)(2,1)}, bf16[8,1536]{1,0:T(8,128)(2,1)S(1)}, u32[]{:S(2)}, u32[]{:S(2)}) collective-permute-start(bf16[8,1536]{1,0:T(8,128)(2,1)} %tile_ref.1), channel_id=1, source_target_pairs={{0,16},{2,18},{4,20},{6,22},{8,24},{10,26},{12,28},{14,30},{16,0},... | collective-permute-start | bytes 73736 | tf_op jit(solution)/shard_map/ppermute | solution.py:25
  6.3 10.6 %collective-permute-start.5 = (bf16[128,1536]{1,0:T(8,128)(2,1)}, bf16[128,1536]{1,0:T(8,128)(2,1)S(1)}, u32[]{:S(2)}, u32[]{:S(2)}) collective-permute-start(bf16[128,1536]{1,0:T(8,128)(2,1)} %q_ref.1), channel_id=1, source_target_pairs={{1,0},{0,1},{3,2},{2,3},{5,4},{4,5},{7,6},{6,7},{9,8},{8,9},{11,10... | collective-permute-start | bytes 1179656 | tf_op jit(solution)/shard_map/ppermute | solution.py:29
  11.4 4.7 %collective-permute-start.3 = (bf16[32,1536]{1,0:T(8,128)(2,1)S(1)}, bf16[32,1536]{1,0:T(8,128)(2,1)S(1)}, u32[]{:S(2)}, u32[]{:S(2)}) collective-permute-start(bf16[32,1536]{1,0:T(8,128)(2,1)S(1)} %pad_maximum_fusion.2), channel_id=1, source_target_pairs={{0,4},{2,6},{4,0},{6,2},{8,12},{10,14},{12,8},{14,10},{16,20},{18,... | collective-permute-start | bytes 294920 | tf_op jit(solution)/shard_map/ppermute | solution.py:25
  13.0 3.9 %collective-permute-start.4 = (s32[8,128]{1,0:T(8,128)S(1)}, s32[8,128]{1,0:T(8,128)S(1)}, u32[]{:S(2)}, u32[]{:S(2)}) collective-permute-start(s32[8,128]{1,0:T(8,128)S(1)} %get-tuple-element.44.refs_0_), channel_id=1, source_target_pairs={{1,0},{0,1},{3,2},{2,3},{5,4},{4,5},{7,6},{6,7},{9,8},{8,9},{11,10... | collective-permute-start | bytes 12296 | tf_op jit(solution)/shard_map/ppermute | solution.py:29
  18.0 1.5 %collective-permute-start.6 = (bf16[64,1536]{1,0:T(8,128)(2,1)S(1)}, bf16[64,1536]{1,0:T(8,128)(2,1)S(1)}, u32[]{:S(2)}, u32[]{:S(2)}) collective-permute-start(bf16[64,1536]{1,0:T(8,128)(2,1)S(1)} %pad_maximum_fusion.1), channel_id=1, source_target_pairs={{0,2},{2,0},{4,6},{6,4},{8,10},{10,8},{12,14},{14,12},{16,18},{18,... | collective-permute-start | bytes 589832 | tf_op jit(solution)/shard_map/ppermute | solution.py:25
  20.0 3.6 %collective-permute-start.7 = (f32[2,256]{1,0:T(2,128)S(1)}, f32[2,256]{1,0:T(2,128)S(1)}, u32[]{:S(2)}, u32[]{:S(2)}) collective-permute-start(f32[2,256]{1,0:T(2,128)S(1)} %get-tuple-element.56.part_ref), channel_id=1, source_target_pairs={{1,0},{0,1},{3,2},{2,3},{5,4},{4,5},{7,6},{6,7},{9,8},{8,9},{11,10... | collective-permute-start | bytes 6152 | tf_op jit(solution)/shard_map/ppermute | solution.py:29
  24.1 1.5 %collective-permute-start.8 = (bf16[64,1536]{1,0:T(8,128)(2,1)S(1)}, bf16[64,1536]{1,0:T(8,128)(2,1)S(1)}, u32[]{:S(2)}, u32[]{:S(2)}) collective-permute-start(bf16[64,1536]{1,0:T(8,128)(2,1)S(1)} %get-tuple-element.58), channel_id=1, source_target_pairs={{0,2},{2,0},{4,6},{6,4},{8,10},{10,8},{12,14},{14,12},{16,18},{18,... | collective-permute-start | bytes 589832 | tf_op jit(solution)/shard_map/ppermute | solution.py:25
  25.7 5.3 %collective-permute-start.9 = (bf16[32,1536]{1,0:T(8,128)(2,1)S(1)}, bf16[32,1536]{1,0:T(8,128)(2,1)S(1)}, u32[]{:S(2)}, u32[]{:S(2)}) collective-permute-start(bf16[32,1536]{1,0:T(8,128)(2,1)S(1)} %slice.37), channel_id=1, source_target_pairs={{0,4},{2,6},{4,0},{6,2},{8,12},{10,14},{12,8},{14,10},{16,20},{18,... | collective-permute-start | bytes 294920 | tf_op jit(solution)/shard_map/ppermute | solution.py:25
  27.3 11.2 %collective-permute-start.10 = (bf16[128,1536]{1,0:T(8,128)(2,1)S(1)}, bf16[128,1536]{1,0:T(8,128)(2,1)S(1)}, u32[]{:S(2)}, u32[]{:S(2)}) collective-permute-start(bf16[128,1536]{1,0:T(8,128)(2,1)S(1)} %get-tuple-element.73), channel_id=1, source_target_pairs={{1,0},{0,1},{3,2},{2,3},{5,4},{4,5},{7,6},{6,7},{9,8},{8,9},{11,10... | collective-permute-start | bytes 1179656 | tf_op jit(solution)/shard_map/ppermute | solution.py:29
  31.0 8.5 %collective-permute-start.11 = (bf16[8,1536]{1,0:T(8,128)(2,1)S(1)}, bf16[8,1536]{1,0:T(8,128)(2,1)S(1)}, u32[]{:S(2)}, u32[]{:S(2)}) collective-permute-start(bf16[8,1536]{1,0:T(8,128)(2,1)S(1)} %get-tuple-element.79), channel_id=1, source_target_pairs={{0,8},{2,10},{4,12},{6,14},{8,0},{10,2},{12,4},{14,6},{16,24},{18,... | collective-permute-start | bytes 73736 | tf_op jit(solution)/shard_map/ppermute | solution.py:25
  32.6 6.9 %collective-permute-start.13 = (bf16[8,1536]{1,0:T(8,128)(2,1)S(1)}, bf16[8,1536]{1,0:T(8,128)(2,1)S(1)}, u32[]{:S(2)}, u32[]{:S(2)}) collective-permute-start(bf16[8,1536]{1,0:T(8,128)(2,1)S(1)} %get-tuple-element.80), channel_id=1, source_target_pairs={{0,24},{2,26},{4,28},{6,30},{8,16},{10,18},{12,20},{14,22},{16,8},... | collective-permute-start | bytes 73736 | tf_op jit(solution)/shard_map/ppermute | solution.py:25
  35.1 4.7 %collective-permute-start.12 = (bf16[8,1536]{1,0:T(8,128)(2,1)S(1)}, bf16[8,1536]{1,0:T(8,128)(2,1)S(1)}, u32[]{:S(2)}, u32[]{:S(2)}) collective-permute-start(bf16[8,1536]{1,0:T(8,128)(2,1)S(1)} %get-tuple-element.81), channel_id=1, source_target_pairs={{0,16},{2,18},{4,20},{6,22},{8,24},{10,26},{12,28},{14,30},{16,0},... | collective-permute-start | bytes 73736 | tf_op jit(solution)/shard_map/ppermute | solution.py:25

commit v3 on v2

--- a/solution.py
+++ b/solution.py
@@ -138,28 +138,44 @@
     )(*(pltpu.with_memory_space_constraint(x, pltpu.HBM) for x in (ids, pos, tile, q, pool)))
 
 
-def group_kernel(piece, chunk, scaling, marks_ref, q_ref, pool_ref, _, all_q_ref, hard_ref, times_ref, stat_ref):
+def join_kernel(piece, q_ref, _, all_q_ref):
     rows = q_ref.shape[0]
     all_q_ref[piece * rows : (piece + 1) * rows, :] = q_ref[...]
+
+
+def join_queries(piece, q, all_q):
+    return pl.pallas_call(
+        functools.partial(join_kernel, piece),
+        in_specs=[VMEM, ANY],
+        out_specs=VMEM,
+        out_shape=pltpu.VMEM(all_q.shape, BF16),
+        input_output_aliases={1: 0},
+        compiler_params=PARAMS,
+        cost_estimate=cost(20),
+        name="join_queries",
+    )(q, all_q)
+
+
+def group_kernel(piece, chunk, scaling, marks_ref, all_q_ref, pool_ref, hard_ref, times_ref, stat_ref):
+    rows = hard_ref.shape[1]
     count_ids(chunk, marks_ref[0 : marks_ref.shape[0] - 1, :], times_ref)
     scores_of(
-        chunk, scaling, q_ref, pool_ref, hard_ref, times_ref, stat_ref, lambda c: None
-    )
-
-
-def group_scores(piece, marks, q, pool, all_q):
-    rows, features = q.shape
-    pool_rows = pool.shape[0]
-    return pl.pallas_call(
-        functools.partial(group_kernel, piece, min(pool_rows, 128), features ** (-0.5)),
-        in_specs=[VMEM] * 3 + [ANY],
-        out_specs=[VMEM] * 4,
-        out_shape=[jax.ShapeDtypeStruct(all_q.shape, BF16)] + hard_shapes(pool_rows, rows),
-        input_output_aliases={3: 0},
+        chunk, scaling, all_q_ref.at[piece * rows : (piece + 1) * rows, :], pool_ref,
+        hard_ref, times_ref, stat_ref, lambda c: None,
+    )
+
+
+def group_scores(piece, marks, all_q, pool):
+    pool_rows, rows = pool.shape[0], marks.shape[1]
+    return pl.pallas_call(
+        functools.partial(group_kernel, piece, min(pool_rows, 128), pool.shape[1] ** (-0.5)),
+        in_specs=[VMEM] * 3,
+        out_specs=[VMEM] * 3,
+        out_shape=hard_shapes(pool_rows, rows),
         compiler_params=PARAMS,
         cost_estimate=cost(20),
         name="group_scores",
-    )(marks, q, pool, all_q)
+    )(marks, all_q, pool)
 
 
 def score_kernel(scaling, keys_ref, q_ref, *refs):
@@ -344,6 +360,9 @@
     blocks = lax.axis_size("blk")
     my_shard = lax.axis_index("shard")
 
+    far = blocks // 4
+    far_tiles = [across(passages, "blk", blocks, 4 * z) for z in range(far - 1, 0, -1)][::-1]
+
     group_q = [shifted(queries, "shard", owners, d) for d in range(1, owners)]
     my_tile, all_q, pool, marks, *found = own_scores(
         owners, hard_ids.T, positives.reshape(1, rows), passages, queries, neg_pool
@@ -351,18 +370,18 @@
     group_marks = [marks] + [shifted(marks, "shard", owners, d) for d in range(1, owners)]
     hard = [found]
     for d in range(1, owners):
-        all_q, *found = group_scores(d, group_marks[d], group_q[d - 1], pool, all_q)
-        hard.append(found)
-
-    far = blocks // 4
-    keys = jnp.concatenate([my_tile] + [across(passages, "blk", blocks, 4 * z) for z in range(1, far)], axis=0)
+        all_q = join_queries(d, group_q[d - 1], all_q)
+
+    keys = jnp.concatenate([my_tile] + far_tiles, axis=0)
     keys = lax.optimization_barrier(keys)
     for bit in (2, 1):
         if bit == 1:
-            keys, hard, all_q = after(keys, hard, all_q)
+            keys, all_q, group_marks = after(keys, all_q, group_marks)
         keys = lax.optimization_barrier(
             jnp.concatenate([keys, across(keys, "blk", blocks, bit)], axis=0)
         )
+    for d in range(1, owners):
+        hard.append(group_scores(d, group_marks[d], all_q, pool))
 
     score, part = passage_scores(keys, all_q, [h[2] for h in hard])
     if owners == 2:
@@ -390,11 +409,15 @@
                 shifted(grad, "shard", owners, owners - d) for d, (grad, _) in enumerate(made, 1)
             ]
             hard_w = [own_w] + [hw for _, hw in made]
+    part = neg_pool.shape[0] // 2
+    pool_grad = pool_rows_grad(0, part, all_q, hard_w, None, 0.5)
+    passage_grad, pool_grad = after(passage_grad, pool_grad)
     sent = passage_grad[tile:].astype(BF16)
     far_terms = [
-        across(sent[(z - 1) * tile : z * tile], "blk", blocks, 4 * z) for z in range(1, far)
+        across(sent[(z - 1) * tile : z * tile], "blk", blocks, 4 * z)
+        for z in range(far - 1, 0, -1)
     ]
-    pool_grad = pool_rows_grad(0, neg_pool.shape[0], all_q, hard_w, None, 20)
+    pool_grad = pool_rows_grad(part, neg_pool.shape[0] - part, all_q, hard_w, pool_grad, 20)
     query_grad = sum_terms([own] + back)
     passage_grad, pool_grad, query_grad = after(passage_grad, pool_grad, query_grad)
     passage_grad = passage_grad[:tile] + sum(t.astype(F32) for t in far_terms)

time: 40.6 us -> 39.2 us (0.966)
  waiting for transfers between devices: 9.53 us -> 6.74 us
  Pallas kernels: 10.2 us -> 11.2 us
    ppermute x10, waiting for transfers between devices: 6.21 us -> 2.82 us  [across(): return lax.ppermute(x, axis, [(i, i ^ distance) for i in range(count)])]
    pallas_call x1 -> x2, Pallas kernels: 3.01 us -> 3.97 us  [pool_rows_grad(): pl.pallas_call(functools.partial(pool_kernel, first, chunk, features ** (...]
    ppermute x4, waiting for transfers between devices: 3.32 us -> 3.92 us  [shifted(): lax.ppermute(x, axis, [((i + distance) % count, i) for i in range(count)])]
  transfers between devices with their start and end apart: 14 -> 14, of which waited for: 8 -> 7; matrix products, arithmetic and copies ran while one was open for 0% -> 0% of each run, Pallas kernels for 20% -> 27%
where the time goes in v3:
time: 39.2 us; the launch traced here: 39 us
  starting transfers between devices  19.5 us (50%)
  Pallas kernels  11.2 us (29%)
  waiting for transfers between devices  6.74 us (17%)
  between operations  0.82 us (2%)
  other arithmetic  0.76 us (2%)
    ppermute x10, starting transfers between devices, across(): return lax.ppermute(x, axis, [(i, i ^ distance) for i in range(count)])  13.4 us
    ppermute x4, starting transfers between devices, shifted(): lax.ppermute(x, axis, [((i + distance) % count, i) for i in range(count)])  6.01 us
    pallas_call x2, Pallas kernels, pool_rows_grad(): pl.pallas_call(functools.partial(pool_kernel, first, chunk, features ** (...  3.97 us
    ppermute x4, waiting for transfers between devices, shifted(): lax.ppermute(x, axis, [((i + distance) % count, i) for i in range(count)])  3.92 us
    pallas_call x1, Pallas kernels, own_scores(): pl.pallas_call(functools.partial(own_kernel, chunk, features ** (-0.5)),...  2.9 us
    ppermute x10, waiting for transfers between devices, across(): return lax.ppermute(x, axis, [(i, i ^ distance) for i in range(count)])  2.82 us
    pallas_call x2, Pallas kernels, query_part(): pl.pallas_call(functools.partial(query_kernel, piece, features ** (-0.5))...  1.45 us
    pallas_call x1, Pallas kernels, group_scores(): pl.pallas_call(functools.partial(group_kernel, piece, min(pool_rows, 128)...  1.1 us
  transfers between devices with their start and end apart: 14, of which 7 were waited for; matrix products, arithmetic and copies ran while one was open for 0% of the time, Pallas kernels for 27%

profile of v3, /device:TPU:0, one launch (start us, length us, event | category | flops | bytes accessed | tf_op | source)
XLA Modules:
  0.0 39.0 jit_solution(9980263707885526626)
XLA Ops:
  0.6 3.1 %collective-permute-start = (bf16[8,1536]{1,0:T(8,128)(2,1)}, bf16[8,1536]{1,0:T(8,128)(2,1)S(1)}, u32[]{:S(2)}, u32[]{:S(2)}) collective-permute-start(bf16[8,1536]{1,0:T(8,128)(2,1)} %tile_ref.1), channel_id=1, source_target_pairs={{0,8},{2,10},{4,12},{6,14},{8,0},{10,2},{12,4},{14,6},{16,24},{18,... | collective-permute-start | bytes 73736 | tf_op jit(solution)/shard_map/ppermute | solution.py:25
  3.7 2.5 %collective-permute-start.2 = (bf16[8,1536]{1,0:T(8,128)(2,1)}, bf16[8,1536]{1,0:T(8,128)(2,1)S(1)}, u32[]{:S(2)}, u32[]{:S(2)}) collective-permute-start(bf16[8,1536]{1,0:T(8,128)(2,1)} %tile_ref.1), channel_id=1, source_target_pairs={{0,24},{2,26},{4,28},{6,30},{8,16},{10,18},{12,20},{14,22},{16,8},... | collective-permute-start | bytes 73736 | tf_op jit(solution)/shard_map/ppermute | solution.py:25
  6.2 0.1 collective-permute-start.1
  6.3 1.5 %collective-permute-start.4 = (bf16[128,1536]{1,0:T(8,128)(2,1)}, bf16[128,1536]{1,0:T(8,128)(2,1)S(1)}, u32[]{:S(2)}, u32[]{:S(2)}) collective-permute-start(bf16[128,1536]{1,0:T(8,128)(2,1)} %q_ref.1), channel_id=1, source_target_pairs={{1,0},{0,1},{3,2},{2,3},{5,4},{4,5},{7,6},{6,7},{9,8},{8,9},{11,10... | collective-permute-start | bytes 1179656 | tf_op jit(solution)/shard_map/ppermute | solution.py:29
  7.8 2.9 %own_scores.1 = (bf16[8,1536]{1,0:T(8,128)(2,1)S(1)}, bf16[256,1536]{1,0:T(8,128)(2,1)S(1)}, bf16[1024,1536]{1,0:T(8,128)(2,1)S(1)}, s32[8,128]{1,0:T(8,128)S(1)...) custom-call(s32[7,128]{1,0:T(8,128)} %bitcast.2, s32[1,128]{1,0:T(1,128)} %bitcast.3, ...), custom_call_target="tpu_custom_call" | custom-call | bytes 73800000 | tf_op jit(solution)/shard_map/own_scores/pallas_call | solution.py:123
  10.7 0.7 %collective-permute-done.1 = bf16[8,1536]{1,0:T(8,128)(2,1)S(1)} collective-permute-done((bf16[8,1536]{1,0:T(8,128)(2,1)}, bf16[8,1536]{1,0:T(8,128)(2,1)S(1)}, u32[]{:S(2)}, u32[]{:S(2)}) %collective-permute-start.1) | collective-permute-done | bytes 24608 | tf_op jit(solution)/shard_map/ppermute | solution.py:25
  11.4 1.6 %collective-permute-start.3 = (bf16[32,1536]{1,0:T(8,128)(2,1)S(1)}, bf16[32,1536]{1,0:T(8,128)(2,1)S(1)}, u32[]{:S(2)}, u32[]{:S(2)}) collective-permute-start(bf16[32,1536]{1,0:T(8,128)(2,1)S(1)} %pad_maximum_fusion.2), channel_id=1, source_target_pairs={{0,4},{2,6},{4,0},{6,2},{8,12},{10,14},{12,8},{14,10},{16,20},{18,... | collective-permute-start | bytes 294920 | tf_op jit(solution)/shard_map/ppermute | solution.py:25
  13.0 1.5 %collective-permute-start.5 = (s32[8,128]{1,0:T(8,128)S(1)}, s32[8,128]{1,0:T(8,128)S(1)}, u32[]{:S(2)}, u32[]{:S(2)}) collective-permute-start(s32[8,128]{1,0:T(8,128)S(1)} %get-tuple-element.48.refs_0_), channel_id=1, source_target_pairs={{1,0},{0,1},{3,2},{2,3},{5,4},{4,5},{7,6},{6,7},{9,8},{8,9},{11,10... | collective-permute-start | bytes 12296 | tf_op jit(solution)/shard_map/ppermute | solution.py:29
  14.5 1.6 %collective-permute-done.3 = bf16[32,1536]{1,0:T(8,128)(2,1)S(1)} collective-permute-done((bf16[32,1536]{1,0:T(8,128)(2,1)S(1)}, bf16[32,1536]{1,0:T(8,128)(2,1)S(1)}, u32[]{:S(2)}, u32[]{:S(2)}) %collective-permute-start.3) | collective-permute-done | bytes 98336 | tf_op jit(solution)/shard_map/ppermute | solution.py:25
  16.1 0.8 %collective-permute-done.4.q_ref = bf16[128,1536]{1,0:T(8,128)(2,1)S(1)} collective-permute-done((bf16[128,1536]{1,0:T(8,128)(2,1)}, bf16[128,1536]{1,0:T(8,128)(2,1)S(1)}, u32[]{:S(2)}, u32[]{:S(2)}) %collective-permute-start.4) | collective-permute-done | bytes 393248 | tf_op jit(solution)/shard_map/ppermute | solution.py:29
  16.9 0.0 collective-permute-done.5.marks_ref.refs_1_
  16.9 0.1 collective-permute-start.6
  17.0 1.1 %group_scores.1 = (f32[1024,128]{1,0:T(8,128)S(1)}, f32[1024,128]{1,0:T(8,128)S(1)}, f32[2,128]{1,0:T(2,128)S(1)}) custom-call(s32[8,128]{1,0:T(8,128)S(1)} %collective-permute-done.5.marks_ref.refs_1_, bf16[256,1536]{1,0:T(8,128)(2,1)S(1)} %join_queries.1.all_q_ref.q_ref, bf16[1024,1536]{1,0:T(8,128)(2,1)S(1)} %get-tuple-element.44.pool_ref), custom_call_target="tpu_custom_call" | custom-call | bytes 73800000 | tf_op jit(solution)/shard_map/group_scores/pallas_call | solution.py:170
  18.1 0.3 collective-permute-done.6
  18.4 0.4 %passage_scores.1 = (f32[128,256]{1,0:T(8,128)S(1)}, f32[2,256]{1,0:T(2,128)S(1)}) custom-call(bf16[128,1536]{1,0:T(8,128)(2,1)S(1)} %pad_maximum_fusion.keys_ref, bf16[256,1536]{1,0:T(8,128)(2,1)S(1)} %join_queries.1.all_q_ref.q_ref, f32[2,128]{1,0:T(2,128)S(1)} %get-tuple-element.42.refs_0_, f32[2,128]{1,0:T(2,128)S(1)} %get-tuple-element.45.refs_1_), custom_call_target="tpu_custom_call" | custom-call | tf_op jit(solution)/shard_map/passage_scores/pallas_call | solution.py:197
  18.9 1.6 %collective-permute-start.7 = (f32[2,256]{1,0:T(2,128)S(1)}, f32[2,256]{1,0:T(2,128)S(1)}, u32[]{:S(2)}, u32[]{:S(2)}) collective-permute-start(f32[2,256]{1,0:T(2,128)S(1)} %get-tuple-element.47.part_ref), channel_id=1, source_target_pairs={{1,0},{0,1},{3,2},{2,3},{5,4},{4,5},{7,6},{6,7},{9,8},{8,9},{11,10... | collective-permute-start | bytes 6152 | tf_op jit(solution)/shard_map/ppermute | solution.py:29
  20.4 2.1 %collective-permute-done.7.other_ref = f32[2,256]{1,0:T(2,128)S(1)} collective-permute-done((f32[2,256]{1,0:T(2,128)S(1)}, f32[2,256]{1,0:T(2,128)S(1)}, u32[]{:S(2)}, u32[]{:S(2)}) %collective-permute-start.7) | collective-permute-done | bytes 2080 | tf_op jit(solution)/shard_map/ppermute | solution.py:29
  22.5 0.4 %passage_weights.1 = (bf16[128,256]{1,0:T(8,128)(2,1)S(1)}, f32[1,256]{1,0:T(1,128)S(1)}, f32[64,1536]{1,0:T(8,128)S(1)}, bf16[64,1536]{1,0:T(8,128)(2,1)S(1)}) custom-call(f32[128,256]{1,0:T(8,128)S(1)} %get-tuple-element.46.score_ref, bf16[256,1536]{1,0:T(8,128)(2,1)S(1)} %join_queries.1.all_q_ref.q_ref, f32[2,256]{1,0:T(2,128)S(1)} %get-tuple-element.47.part_ref, ...), custom_call_target="tpu_custom_call" | custom-call | tf_op jit(solution)/shard_map/passage_weights/pallas_call | solution.py:243
  23.0 0.1 collective-permute-start.8
  23.0 0.7 %query_part.2 = (bf16[128,1536]{1,0:T(8,128)(2,1)S(1)}, bf16[1024,128]{1,0:T(8,128)(2,1)S(1)}) custom-call(f32[1024,128]{1,0:T(8,128)S(1)} %get-tuple-element.51.hard_ref, f32[1024,128]{1,0:T(8,128)S(1)} %get-tuple-element.52.times_ref, f32[1,256]{1,0:T(1,128)S(1)} %get-tuple-element.53.log_ref, bf16[128,256]{1,0:T(8,128)(2,1)S(1)} %get-tuple-element.54.w_ref, ...), custom_call_target="tpu_custom_call" | custom-call | bytes 36900000 | tf_op jit(solution)/shard_map/query_part/pallas_call | solution.py:271
  23.8 0.7 %query_part.3 = (f32[128,1536]{1,0:T(8,128)S(1)}, bf16[1024,128]{1,0:T(8,128)(2,1)S(1)}) custom-call(f32[1024,128]{1,0:T(8,128)S(1)} %get-tuple-element.57.hard_ref, f32[1024,128]{1,0:T(8,128)S(1)} %get-tuple-element.58.times_ref, f32[1,256]{1,0:T(1,128)S(1)} %get-tuple-element.53.log_ref, bf16[128,256]{1,0:T(8,128)(2,1)S(1)} %get-tuple-element.54.w_ref, ...), custom_call_target="tpu_custom_call" | custom-call | bytes 36900000 | tf_op jit(solution)/shard_map/query_part/pallas_call | solution.py:271
  24.6 1.6 %collective-permute-start.9 = (bf16[32,1536]{1,0:T(8,128)(2,1)S(1)}, bf16[32,1536]{1,0:T(8,128)(2,1)S(1)}, u32[]{:S(2)}, u32[]{:S(2)}) collective-permute-start(bf16[32,1536]{1,0:T(8,128)(2,1)S(1)} %slice.37), channel_id=1, source_target_pairs={{0,4},{2,6},{4,0},{6,2},{8,12},{10,14},{12,8},{14,10},{16,20},{18,... | collective-permute-start | bytes 294920 | tf_op jit(solution)/shard_map/ppermute | solution.py:25
  26.2 1.5 %collective-permute-start.10 = (bf16[128,1536]{1,0:T(8,128)(2,1)S(1)}, bf16[128,1536]{1,0:T(8,128)(2,1)S(1)}, u32[]{:S(2)}, u32[]{:S(2)}) collective-permute-start(bf16[128,1536]{1,0:T(8,128)(2,1)S(1)} %get-tuple-element.67), channel_id=1, source_target_pairs={{1,0},{0,1},{3,2},{2,3},{5,4},{4,5},{7,6},{6,7},{9,8},{8,9},{11,10... | collective-permute-start | bytes 1179656 | tf_op jit(solution)/shard_map/ppermute | solution.py:29
  27.7 2.0 %pool_grad.2.refs_2_ = f32[1024,1536]{1,0:T(8,128)} custom-call(bf16[256,1536]{1,0:T(8,128)(2,1)S(1)} %join_queries.1.all_q_ref.q_ref, bf16[1024,128]{1,0:T(8,128)(2,1)S(1)} %get-tuple-element.62.refs_0_, bf16[1024,128]{1,0:T(8,128)(2,1)S(1)} %get-tuple-element.63.refs_1_), custom_call_target="tpu_custom_call" | custom-call | bytes 1845000 | tf_op jit(solution)/shard_map/pool_grad/pallas_call | solution.py:307
  29.7 0.2 collective-permute-done.9
  29.9 2.7 %collective-permute-start.11 = (bf16[8,1536]{1,0:T(8,128)(2,1)S(1)}, bf16[8,1536]{1,0:T(8,128)(2,1)S(1)}, u32[]{:S(2)}, u32[]{:S(2)}) collective-permute-start(bf16[8,1536]{1,0:T(8,128)(2,1)S(1)} %get-tuple-element.71), channel_id=1, source_target_pairs={{0,24},{2,26},{4,28},{6,30},{8,16},{10,18},{12,20},{14,22},{16,8},... | collective-permute-start | bytes 73736 | tf_op jit(solution)/shard_map/ppermute | solution.py:25
  32.6 0.5 %collective-permute-start.13 = (bf16[8,1536]{1,0:T(8,128)(2,1)S(1)}, bf16[8,1536]{1,0:T(8,128)(2,1)S(1)}, u32[]{:S(2)}, u32[]{:S(2)}) collective-permute-start(bf16[8,1536]{1,0:T(8,128)(2,1)S(1)} %get-tuple-element.72), channel_id=1, source_target_pairs={{0,8},{2,10},{4,12},{6,14},{8,0},{10,2},{12,4},{14,6},{16,24},{18,... | collective-permute-start | bytes 73736 | tf_op jit(solution)/shard_map/ppermute | solution.py:25
  33.1 1.3 %collective-permute-start.12 = (bf16[8,1536]{1,0:T(8,128)(2,1)S(1)}, bf16[8,1536]{1,0:T(8,128)(2,1)S(1)}, u32[]{:S(2)}, u32[]{:S(2)}) collective-permute-start(bf16[8,1536]{1,0:T(8,128)(2,1)S(1)} %get-tuple-element.73), channel_id=1, source_target_pairs={{0,16},{2,18},{4,20},{6,22},{8,24},{10,26},{12,28},{14,30},{16,0},... | collective-permute-start | bytes 73736 | tf_op jit(solution)/shard_map/ppermute | solution.py:25
  34.4 2.0 %pool_grad.3 = f32[1024,1536]{1,0:T(8,128)} custom-call(bf16[256,1536]{1,0:T(8,128)(2,1)S(1)} %join_queries.1.all_q_ref.q_ref, bf16[1024,128]{1,0:T(8,128)(2,1)S(1)} %get-tuple-element.62.refs_0_, bf16[1024,128]{1,0:T(8,128)(2,1)S(1)} %get-tuple-element.63.refs_1_, f32[1024,1536]{1,0:T(8,128)} %pool_grad.2.refs_2_), custom_call_target="tpu_custom_call", output_to_operand_aliasing={{}: (3, {})} | custom-call | bytes 73800000 | tf_op jit(solution)/shard_map/pool_grad/pallas_call | solution.py:307
  36.4 1.1 %collective-permute-done.10.refs_1_ = bf16[128,1536]{1,0:T(8,128)(2,1)S(1)} collective-permute-done((bf16[128,1536]{1,0:T(8,128)(2,1)S(1)}, bf16[128,1536]{1,0:T(8,128)(2,1)S(1)}, u32[]{:S(2)}, u32[]{:S(2)}) %collective-permute-start.10) | collective-permute-done | bytes 393248 | tf_op jit(solution)/shard_map/ppermute | solution.py:29
  37.4 0.9 %query_grad.1 = f32[128,1536]{1,0:T(8,128)} custom-call(f32[128,1536]{1,0:T(8,128)S(1)} %get-tuple-element.66.refs_0_, bf16[128,1536]{1,0:T(8,128)(2,1)S(1)} %collective-permute-done.10.refs_1_), custom_call_target="tpu_custom_call" | custom-call | bytes 73800000 | tf_op jit(solution)/shard_map/query_grad/pallas_call | solution.py:341
  38.4 0.6 %add_add_fusion = f32[8,1536]{1,0:T(8,128)} fusion(bf16[8,1536]{1,0:T(8,128)(2,1)S(1)} %collective-permute-done.13, bf16[8,1536]{1,0:T(8,128)(2,1)S(1)} %collective-permute-done.12, bf16[8,1536]{1,0:T(8,128)(2,1)S(1)} %collective-permute-done.11, f32[32,1536]{1,0:T(8,128)S(1)} %convert_add_fusion.1), kind=kLoop, calls=%fused_computation.6 | loop fusion | flops 73728 | bytes 172032 | tf_op jit(solution)/shard_map/add | solution.py:423
  (16 shorter events, 0.2 us)
Async XLA Ops:
  0.6 10.1 %collective-permute-start = (bf16[8,1536]{1,0:T(8,128)(2,1)}, bf16[8,1536]{1,0:T(8,128)(2,1)S(1)}, u32[]{:S(2)}, u32[]{:S(2)}) collective-permute-start(bf16[8,1536]{1,0:T(8,128)(2,1)} %tile_ref.1), channel_id=1, source_target_pairs={{0,8},{2,10},{4,12},{6,14},{8,0},{10,2},{12,4},{14,6},{16,24},{18,... | collective-permute-start | bytes 73736 | tf_op jit(solution)/shard_map/ppermute | solution.py:25
  3.7 7.0 %collective-permute-start.2 = (bf16[8,1536]{1,0:T(8,128)(2,1)}, bf16[8,1536]{1,0:T(8,128)(2,1)S(1)}, u32[]{:S(2)}, u32[]{:S(2)}) collective-permute-start(bf16[8,1536]{1,0:T(8,128)(2,1)} %tile_ref.1), channel_id=1, source_target_pairs={{0,24},{2,26},{4,28},{6,30},{8,16},{10,18},{12,20},{14,22},{16,8},... | collective-permute-start | bytes 73736 | tf_op jit(solution)/shard_map/ppermute | solution.py:25
  6.2 5.2 %collective-permute-start.1 = (bf16[8,1536]{1,0:T(8,128)(2,1)}, bf16[8,1536]{1,0:T(8,128)(2,1)S(1)}, u32[]{:S(2)}, u32[]{:S(2)}) collective-permute-start(bf16[8,1536]{1,0:T(8,128)(2,1)} %tile_ref.1), channel_id=1, source_target_pairs={{0,16},{2,18},{4,20},{6,22},{8,24},{10,26},{12,28},{14,30},{16,0},... | collective-permute-start | bytes 73736 | tf_op jit(solution)/shard_map/ppermute | solution.py:25
  6.3 10.5 %collective-permute-start.4 = (bf16[128,1536]{1,0:T(8,128)(2,1)}, bf16[128,1536]{1,0:T(8,128)(2,1)S(1)}, u32[]{:S(2)}, u32[]{:S(2)}) collective-permute-start(bf16[128,1536]{1,0:T(8,128)(2,1)} %q_ref.1), channel_id=1, source_target_pairs={{1,0},{0,1},{3,2},{2,3},{5,4},{4,5},{7,6},{6,7},{9,8},{8,9},{11,10... | collective-permute-start | bytes 1179656 | tf_op jit(solution)/shard_map/ppermute | solution.py:29
  11.4 4.7 %collective-permute-start.3 = (bf16[32,1536]{1,0:T(8,128)(2,1)S(1)}, bf16[32,1536]{1,0:T(8,128)(2,1)S(1)}, u32[]{:S(2)}, u32[]{:S(2)}) collective-permute-start(bf16[32,1536]{1,0:T(8,128)(2,1)S(1)} %pad_maximum_fusion.2), channel_id=1, source_target_pairs={{0,4},{2,6},{4,0},{6,2},{8,12},{10,14},{12,8},{14,10},{16,20},{18,... | collective-permute-start | bytes 294920 | tf_op jit(solution)/shard_map/ppermute | solution.py:25
  13.0 3.9 %collective-permute-start.5 = (s32[8,128]{1,0:T(8,128)S(1)}, s32[8,128]{1,0:T(8,128)S(1)}, u32[]{:S(2)}, u32[]{:S(2)}) collective-permute-start(s32[8,128]{1,0:T(8,128)S(1)} %get-tuple-element.48.refs_0_), channel_id=1, source_target_pairs={{1,0},{0,1},{3,2},{2,3},{5,4},{4,5},{7,6},{6,7},{9,8},{8,9},{11,10... | collective-permute-start | bytes 12296 | tf_op jit(solution)/shard_map/ppermute | solution.py:29
  16.9 1.5 %collective-permute-start.6 = (bf16[64,1536]{1,0:T(8,128)(2,1)S(1)}, bf16[64,1536]{1,0:T(8,128)(2,1)S(1)}, u32[]{:S(2)}, u32[]{:S(2)}) collective-permute-start(bf16[64,1536]{1,0:T(8,128)(2,1)S(1)} %pad_maximum_fusion.1), channel_id=1, source_target_pairs={{0,2},{2,0},{4,6},{6,4},{8,10},{10,8},{12,14},{14,12},{16,18},{18,... | collective-permute-start | bytes 589832 | tf_op jit(solution)/shard_map/ppermute | solution.py:25
  18.9 3.6 %collective-permute-start.7 = (f32[2,256]{1,0:T(2,128)S(1)}, f32[2,256]{1,0:T(2,128)S(1)}, u32[]{:S(2)}, u32[]{:S(2)}) collective-permute-start(f32[2,256]{1,0:T(2,128)S(1)} %get-tuple-element.47.part_ref), channel_id=1, source_target_pairs={{1,0},{0,1},{3,2},{2,3},{5,4},{4,5},{7,6},{6,7},{9,8},{8,9},{11,10... | collective-permute-start | bytes 6152 | tf_op jit(solution)/shard_map/ppermute | solution.py:29
  23.0 1.5 %collective-permute-start.8 = (bf16[64,1536]{1,0:T(8,128)(2,1)S(1)}, bf16[64,1536]{1,0:T(8,128)(2,1)S(1)}, u32[]{:S(2)}, u32[]{:S(2)}) collective-permute-start(bf16[64,1536]{1,0:T(8,128)(2,1)S(1)} %get-tuple-element.50), channel_id=1, source_target_pairs={{0,2},{2,0},{4,6},{6,4},{8,10},{10,8},{12,14},{14,12},{16,18},{18,... | collective-permute-start | bytes 589832 | tf_op jit(solution)/shard_map/ppermute | solution.py:25
  24.6 5.3 %collective-permute-start.9 = (bf16[32,1536]{1,0:T(8,128)(2,1)S(1)}, bf16[32,1536]{1,0:T(8,128)(2,1)S(1)}, u32[]{:S(2)}, u32[]{:S(2)}) collective-permute-start(bf16[32,1536]{1,0:T(8,128)(2,1)S(1)} %slice.37), channel_id=1, source_target_pairs={{0,4},{2,6},{4,0},{6,2},{8,12},{10,14},{12,8},{14,10},{16,20},{18,... | collective-permute-start | bytes 294920 | tf_op jit(solution)/shard_map/ppermute | solution.py:25
  26.2 11.2 %collective-permute-start.10 = (bf16[128,1536]{1,0:T(8,128)(2,1)S(1)}, bf16[128,1536]{1,0:T(8,128)(2,1)S(1)}, u32[]{:S(2)}, u32[]{:S(2)}) collective-permute-start(bf16[128,1536]{1,0:T(8,128)(2,1)S(1)} %get-tuple-element.67), channel_id=1, source_target_pairs={{1,0},{0,1},{3,2},{2,3},{5,4},{4,5},{7,6},{6,7},{9,8},{8,9},{11,10... | collective-permute-start | bytes 1179656 | tf_op jit(solution)/shard_map/ppermute | solution.py:29
  29.9 8.4 %collective-permute-start.11 = (bf16[8,1536]{1,0:T(8,128)(2,1)S(1)}, bf16[8,1536]{1,0:T(8,128)(2,1)S(1)}, u32[]{:S(2)}, u32[]{:S(2)}) collective-permute-start(bf16[8,1536]{1,0:T(8,128)(2,1)S(1)} %get-tuple-element.71), channel_id=1, source_target_pairs={{0,24},{2,26},{4,28},{6,30},{8,16},{10,18},{12,20},{14,22},{16,8},... | collective-permute-start | bytes 73736 | tf_op jit(solution)/shard_map/ppermute | solution.py:25
  32.6 5.7 %collective-permute-start.13 = (bf16[8,1536]{1,0:T(8,128)(2,1)S(1)}, bf16[8,1536]{1,0:T(8,128)(2,1)S(1)}, u32[]{:S(2)}, u32[]{:S(2)}) collective-permute-start(bf16[8,1536]{1,0:T(8,128)(2,1)S(1)} %get-tuple-element.72), channel_id=1, source_target_pairs={{0,8},{2,10},{4,12},{6,14},{8,0},{10,2},{12,4},{14,6},{16,24},{18,... | collective-permute-start | bytes 73736 | tf_op jit(solution)/shard_map/ppermute | solution.py:25
  33.1 5.3 %collective-permute-start.12 = (bf16[8,1536]{1,0:T(8,128)(2,1)S(1)}, bf16[8,1536]{1,0:T(8,128)(2,1)S(1)}, u32[]{:S(2)}, u32[]{:S(2)}) collective-permute-start(bf16[8,1536]{1,0:T(8,128)(2,1)S(1)} %get-tuple-element.73), channel_id=1, source_target_pairs={{0,16},{2,18},{4,20},{6,22},{8,24},{10,26},{12,28},{14,30},{16,0},... | collective-permute-start | bytes 73736 | tf_op jit(solution)/shard_map/ppermute | solution.py:25

commit v4 on v3

--- a/solution.py
+++ b/solution.py
@@ -72,9 +72,8 @@
 
 def own_kernel(
     chunk, scaling, ids_ref, pos_ref, tile_ref, q_ref, pool_ref,
-    tile_here, all_q_ref, pool_here, marks_ref, hard_ref, times_ref, stat_ref, sems,
+    tile_here, own_q_ref, pool_here, marks_ref, hard_ref, times_ref, stat_ref, sems,
 ):
-    rows = q_ref.shape[0]
     neg_count = ids_ref.shape[0]
     half = pool_ref.shape[0] // 2
     marks = [
@@ -82,7 +81,7 @@
         pltpu.make_async_copy(pos_ref, marks_ref.at[neg_count : neg_count + 1, :], sems.at[1]),
     ]
     others = [
-        pltpu.make_async_copy(q_ref, all_q_ref.at[0:rows, :], sems.at[2]),
+        pltpu.make_async_copy(q_ref, own_q_ref, sems.at[2]),
         pltpu.make_async_copy(tile_ref, tile_here, sems.at[3]),
     ]
     halves = [
@@ -104,7 +103,7 @@
             halves[c // half].wait()
 
     scores_of(
-        chunk, scaling, all_q_ref.at[0:rows, :], pool_here, hard_ref, times_ref, stat_ref, ready
+        chunk, scaling, own_q_ref, pool_here, hard_ref, times_ref, stat_ref, ready
     )
 
 
@@ -116,17 +115,17 @@
     ]
 
 
-def own_scores(pieces, ids, pos, tile, q, pool):
+def own_scores(ids, pos, tile, q, pool):
     rows, features = q.shape
     pool_rows = pool.shape[0]
-    chunk = min(pool_rows, 128)
+    chunk = min(pool_rows // 2, 128)
     return pl.pallas_call(
         functools.partial(own_kernel, chunk, features ** (-0.5)),
         in_specs=[HBM] * 5,
         out_specs=[VMEM] * 7,
         out_shape=[
             pltpu.VMEM(tile.shape, BF16),
-            pltpu.VMEM((pieces * rows, features), BF16),
+            pltpu.VMEM((rows, features), BF16),
             pltpu.VMEM((pool_rows, features), BF16),
             pltpu.VMEM((ids.shape[0] + 1, rows), jnp.int32),
         ]
@@ -138,22 +137,23 @@
     )(*(pltpu.with_memory_space_constraint(x, pltpu.HBM) for x in (ids, pos, tile, q, pool)))
 
 
-def join_kernel(piece, q_ref, _, all_q_ref):
-    rows = q_ref.shape[0]
-    all_q_ref[piece * rows : (piece + 1) * rows, :] = q_ref[...]
-
-
-def join_queries(piece, q, all_q):
-    return pl.pallas_call(
-        functools.partial(join_kernel, piece),
-        in_specs=[VMEM, ANY],
+def join_kernel(*refs):
+    rows = refs[0].shape[0]
+    for d, ref in enumerate(refs[:-1]):
+        refs[-1][d * rows : (d + 1) * rows, :] = ref[...]
+
+
+def join_queries(pieces):
+    rows, features = pieces[0].shape
+    return pl.pallas_call(
+        join_kernel,
+        in_specs=[VMEM] * len(pieces),
         out_specs=VMEM,
-        out_shape=pltpu.VMEM(all_q.shape, BF16),
-        input_output_aliases={1: 0},
+        out_shape=pltpu.VMEM((len(pieces) * rows, features), BF16),
         compiler_params=PARAMS,
         cost_estimate=cost(20),
         name="join_queries",
-    )(q, all_q)
+    )(*pieces)
 
 
 def group_kernel(piece, chunk, scaling, marks_ref, all_q_ref, pool_ref, hard_ref, times_ref, stat_ref):
@@ -233,8 +233,9 @@
     w = (jnp.exp(score_ref[...] - log_total) - hit).astype(BF16)
     w_ref[...] = w
     half = held // 2
-    keep_ref[...] = dot(w[:half], q_ref[...], ROWS_COLS) * scaling
-    send_ref[...] = (dot(w[half:], q_ref[...], ROWS_COLS) * scaling).astype(BF16)
+    terms = dot(w, q_ref[...], ROWS_COLS) * scaling
+    keep_ref[...] = terms[:half]
+    send_ref[...] = terms[half:].astype(BF16)
 
 
 def passage_weights(far, tile, owners, score, all_q, part, other, pos):
@@ -364,13 +365,12 @@
     far_tiles = [across(passages, "blk", blocks, 4 * z) for z in range(far - 1, 0, -1)][::-1]
 
     group_q = [shifted(queries, "shard", owners, d) for d in range(1, owners)]
-    my_tile, all_q, pool, marks, *found = own_scores(
-        owners, hard_ids.T, positives.reshape(1, rows), passages, queries, neg_pool
+    my_tile, own_q, pool, marks, *found = own_scores(
+        hard_ids.T, positives.reshape(1, rows), passages, queries, neg_pool
     )
     group_marks = [marks] + [shifted(marks, "shard", owners, d) for d in range(1, owners)]
     hard = [found]
-    for d in range(1, owners):
-        all_q = join_queries(d, group_q[d - 1], all_q)
+    all_q = join_queries([own_q] + group_q)
 
     keys = jnp.concatenate([my_tile] + far_tiles, axis=0)
     keys = lax.optimization_barrier(keys)
@@ -410,7 +410,7 @@
             ]
             hard_w = [own_w] + [hw for _, hw in made]
     part = neg_pool.shape[0] // 2
-    pool_grad = pool_rows_grad(0, part, all_q, hard_w, None, 0.5)
+    pool_grad = pool_rows_grad(0, part, all_q, hard_w, None, 20)
     passage_grad, pool_grad = after(passage_grad, pool_grad)
     sent = passage_grad[tile:].astype(BF16)
     far_terms = [

time: 39.2 us -> 39.1 us (level)
  no operation moved by 1% of the time
where the time goes in v4:
time: 39.1 us; the launch traced here: 38.9 us
  starting transfers between devices  19.5 us (50%)
  Pallas kernels  11.1 us (28%)
  waiting for transfers between devices  6.74 us (17%)
  between operations  0.82 us (2%)
  other arithmetic  0.75 us (2%)
    ppermute x10, starting transfers between devices, across(): return lax.ppermute(x, axis, [(i, i ^ distance) for i in range(count)])  13.4 us
    ppermute x4, starting transfers between devices, shifted(): lax.ppermute(x, axis, [((i + distance) % count, i) for i in range(count)])  6.02 us
    pallas_call x2, Pallas kernels, pool_rows_grad(): pl.pallas_call(functools.partial(pool_kernel, first, chunk, features ** (...  3.96 us
    ppermute x4, waiting for transfers between devices, shifted(): lax.ppermute(x, axis, [((i + distance) % count, i) for i in range(count)])  3.92 us
    pallas_call x1, Pallas kernels, own_scores(): pl.pallas_call(functools.partial(own_kernel, chunk, features ** (-0.5)),...  2.9 us
    ppermute x10, waiting for transfers between devices, across(): return lax.ppermute(x, axis, [(i, i ^ distance) for i in range(count)])  2.82 us
    pallas_call x2, Pallas kernels, query_part(): pl.pallas_call(functools.partial(query_kernel, piece, features ** (-0.5))...  1.42 us
    pallas_call x1, Pallas kernels, group_scores(): pl.pallas_call(functools.partial(group_kernel, piece, min(pool_rows, 128)...  1.09 us
  transfers between devices with their start and end apart: 14, of which 7 were waited for; matrix products, arithmetic and copies ran while one was open for 0% of the time, Pallas kernels for 27%

profile of v4, /device:TPU:0, one launch (start us, length us, event | category | flops | bytes accessed | tf_op | source)
XLA Modules:
  0.0 38.9 jit_solution(951745322591493199)
XLA Ops:
  0.6 3.1 %collective-permute-start = (bf16[8,1536]{1,0:T(8,128)(2,1)}, bf16[8,1536]{1,0:T(8,128)(2,1)S(1)}, u32[]{:S(2)}, u32[]{:S(2)}) collective-permute-start(bf16[8,1536]{1,0:T(8,128)(2,1)} %tile_ref.1), channel_id=1, source_target_pairs={{0,8},{2,10},{4,12},{6,14},{8,0},{10,2},{12,4},{14,6},{16,24},{18,... | collective-permute-start | bytes 73736 | tf_op jit(solution)/shard_map/ppermute | solution.py:25
  3.7 2.5 %collective-permute-start.2 = (bf16[8,1536]{1,0:T(8,128)(2,1)}, bf16[8,1536]{1,0:T(8,128)(2,1)S(1)}, u32[]{:S(2)}, u32[]{:S(2)}) collective-permute-start(bf16[8,1536]{1,0:T(8,128)(2,1)} %tile_ref.1), channel_id=1, source_target_pairs={{0,24},{2,26},{4,28},{6,30},{8,16},{10,18},{12,20},{14,22},{16,8},... | collective-permute-start | bytes 73736 | tf_op jit(solution)/shard_map/ppermute | solution.py:25
  6.2 0.1 collective-permute-start.1
  6.3 1.5 %collective-permute-start.4 = (bf16[128,1536]{1,0:T(8,128)(2,1)}, bf16[128,1536]{1,0:T(8,128)(2,1)S(1)}, u32[]{:S(2)}, u32[]{:S(2)}) collective-permute-start(bf16[128,1536]{1,0:T(8,128)(2,1)} %q_ref.1), channel_id=1, source_target_pairs={{1,0},{0,1},{3,2},{2,3},{5,4},{4,5},{7,6},{6,7},{9,8},{8,9},{11,10... | collective-permute-start | bytes 1179656 | tf_op jit(solution)/shard_map/ppermute | solution.py:29
  7.8 2.9 %own_scores.1 = (bf16[8,1536]{1,0:T(8,128)(2,1)S(1)}, bf16[128,1536]{1,0:T(8,128)(2,1)S(1)}, bf16[1024,1536]{1,0:T(8,128)(2,1)S(1)}, s32[8,128]{1,0:T(8,128)S(1)...) custom-call(s32[7,128]{1,0:T(8,128)} %bitcast.2, s32[1,128]{1,0:T(1,128)} %bitcast.3, ...), custom_call_target="tpu_custom_call" | custom-call | bytes 73800000 | tf_op jit(solution)/shard_map/own_scores/pallas_call | solution.py:122
  10.7 0.7 %collective-permute-done.1 = bf16[8,1536]{1,0:T(8,128)(2,1)S(1)} collective-permute-done((bf16[8,1536]{1,0:T(8,128)(2,1)}, bf16[8,1536]{1,0:T(8,128)(2,1)S(1)}, u32[]{:S(2)}, u32[]{:S(2)}) %collective-permute-start.1) | collective-permute-done | bytes 24608 | tf_op jit(solution)/shard_map/ppermute | solution.py:25
  11.4 1.6 %collective-permute-start.3 = (bf16[32,1536]{1,0:T(8,128)(2,1)S(1)}, bf16[32,1536]{1,0:T(8,128)(2,1)S(1)}, u32[]{:S(2)}, u32[]{:S(2)}) collective-permute-start(bf16[32,1536]{1,0:T(8,128)(2,1)S(1)} %pad_maximum_fusion.2), channel_id=1, source_target_pairs={{0,4},{2,6},{4,0},{6,2},{8,12},{10,14},{12,8},{14,10},{16,20},{18,... | collective-permute-start | bytes 294920 | tf_op jit(solution)/shard_map/ppermute | solution.py:25
  13.0 1.5 %collective-permute-start.5 = (s32[8,128]{1,0:T(8,128)S(1)}, s32[8,128]{1,0:T(8,128)S(1)}, u32[]{:S(2)}, u32[]{:S(2)}) collective-permute-start(s32[8,128]{1,0:T(8,128)S(1)} %get-tuple-element.48.refs_0_), channel_id=1, source_target_pairs={{1,0},{0,1},{3,2},{2,3},{5,4},{4,5},{7,6},{6,7},{9,8},{8,9},{11,10... | collective-permute-start | bytes 12296 | tf_op jit(solution)/shard_map/ppermute | solution.py:29
  14.5 1.6 %collective-permute-done.3 = bf16[32,1536]{1,0:T(8,128)(2,1)S(1)} collective-permute-done((bf16[32,1536]{1,0:T(8,128)(2,1)S(1)}, bf16[32,1536]{1,0:T(8,128)(2,1)S(1)}, u32[]{:S(2)}, u32[]{:S(2)}) %collective-permute-start.3) | collective-permute-done | bytes 98336 | tf_op jit(solution)/shard_map/ppermute | solution.py:25
  16.1 0.8 %collective-permute-done.4.refs_1_ = bf16[128,1536]{1,0:T(8,128)(2,1)S(1)} collective-permute-done((bf16[128,1536]{1,0:T(8,128)(2,1)}, bf16[128,1536]{1,0:T(8,128)(2,1)S(1)}, u32[]{:S(2)}, u32[]{:S(2)}) %collective-permute-start.4) | collective-permute-done | bytes 393248 | tf_op jit(solution)/shard_map/ppermute | solution.py:29
  16.9 0.1 join_queries.1.all_q_ref.q_ref
  16.9 0.1 collective-permute-start.6
  17.0 1.1 %group_scores.1 = (f32[1024,128]{1,0:T(8,128)S(1)}, f32[1024,128]{1,0:T(8,128)S(1)}, f32[2,128]{1,0:T(2,128)S(1)}) custom-call(s32[8,128]{1,0:T(8,128)S(1)} %collective-permute-done.5.marks_ref.refs_1_, bf16[256,1536]{1,0:T(8,128)(2,1)S(1)} %join_queries.1.all_q_ref.q_ref, bf16[1024,1536]{1,0:T(8,128)(2,1)S(1)} %get-tuple-element.44.pool_ref), custom_call_target="tpu_custom_call" | custom-call | bytes 73800000 | tf_op jit(solution)/shard_map/group_scores/pallas_call | solution.py:170
  18.1 0.3 collective-permute-done.6
  18.5 0.4 %passage_scores.1 = (f32[128,256]{1,0:T(8,128)S(1)}, f32[2,256]{1,0:T(2,128)S(1)}) custom-call(bf16[128,1536]{1,0:T(8,128)(2,1)S(1)} %pad_maximum_fusion.keys_ref, bf16[256,1536]{1,0:T(8,128)(2,1)S(1)} %join_queries.1.all_q_ref.q_ref, f32[2,128]{1,0:T(2,128)S(1)} %get-tuple-element.42.refs_0_, f32[2,128]{1,0:T(2,128)S(1)} %get-tuple-element.45.refs_1_), custom_call_target="tpu_custom_call" | custom-call | tf_op jit(solution)/shard_map/passage_scores/pallas_call | solution.py:197
  18.9 1.6 %collective-permute-start.7 = (f32[2,256]{1,0:T(2,128)S(1)}, f32[2,256]{1,0:T(2,128)S(1)}, u32[]{:S(2)}, u32[]{:S(2)}) collective-permute-start(f32[2,256]{1,0:T(2,128)S(1)} %get-tuple-element.47.part_ref), channel_id=1, source_target_pairs={{1,0},{0,1},{3,2},{2,3},{5,4},{4,5},{7,6},{6,7},{9,8},{8,9},{11,10... | collective-permute-start | bytes 6152 | tf_op jit(solution)/shard_map/ppermute | solution.py:29
  20.5 2.1 %collective-permute-done.7.other_ref = f32[2,256]{1,0:T(2,128)S(1)} collective-permute-done((f32[2,256]{1,0:T(2,128)S(1)}, f32[2,256]{1,0:T(2,128)S(1)}, u32[]{:S(2)}, u32[]{:S(2)}) %collective-permute-start.7) | collective-permute-done | bytes 2080 | tf_op jit(solution)/shard_map/ppermute | solution.py:29
  22.6 0.3 passage_weights.1
  22.9 0.1 collective-permute-start.8
  23.0 0.7 %query_part.2 = (bf16[128,1536]{1,0:T(8,128)(2,1)S(1)}, bf16[1024,128]{1,0:T(8,128)(2,1)S(1)}) custom-call(f32[1024,128]{1,0:T(8,128)S(1)} %get-tuple-element.51.hard_ref, f32[1024,128]{1,0:T(8,128)S(1)} %get-tuple-element.52.times_ref, f32[1,256]{1,0:T(1,128)S(1)} %get-tuple-element.53.log_ref, bf16[128,256]{1,0:T(8,128)(2,1)S(1)} %get-tuple-element.54.w_ref, ...), custom_call_target="tpu_custom_call" | custom-call | bytes 36900000 | tf_op jit(solution)/shard_map/query_part/pallas_call | solution.py:272
  23.7 0.7 %query_part.3 = (f32[128,1536]{1,0:T(8,128)S(1)}, bf16[1024,128]{1,0:T(8,128)(2,1)S(1)}) custom-call(f32[1024,128]{1,0:T(8,128)S(1)} %get-tuple-element.57.hard_ref, f32[1024,128]{1,0:T(8,128)S(1)} %get-tuple-element.58.times_ref, f32[1,256]{1,0:T(1,128)S(1)} %get-tuple-element.53.log_ref, bf16[128,256]{1,0:T(8,128)(2,1)S(1)} %get-tuple-element.54.w_ref, ...), custom_call_target="tpu_custom_call" | custom-call | bytes 36900000 | tf_op jit(solution)/shard_map/query_part/pallas_call | solution.py:272
  24.5 1.6 %collective-permute-start.9 = (bf16[32,1536]{1,0:T(8,128)(2,1)S(1)}, bf16[32,1536]{1,0:T(8,128)(2,1)S(1)}, u32[]{:S(2)}, u32[]{:S(2)}) collective-permute-start(bf16[32,1536]{1,0:T(8,128)(2,1)S(1)} %slice.37), channel_id=1, source_target_pairs={{0,4},{2,6},{4,0},{6,2},{8,12},{10,14},{12,8},{14,10},{16,20},{18,... | collective-permute-start | bytes 294920 | tf_op jit(solution)/shard_map/ppermute | solution.py:25
  26.1 1.5 %collective-permute-start.10 = (bf16[128,1536]{1,0:T(8,128)(2,1)S(1)}, bf16[128,1536]{1,0:T(8,128)(2,1)S(1)}, u32[]{:S(2)}, u32[]{:S(2)}) collective-permute-start(bf16[128,1536]{1,0:T(8,128)(2,1)S(1)} %get-tuple-element.67), channel_id=1, source_target_pairs={{1,0},{0,1},{3,2},{2,3},{5,4},{4,5},{7,6},{6,7},{9,8},{8,9},{11,10... | collective-permute-start | bytes 1179656 | tf_op jit(solution)/shard_map/ppermute | solution.py:29
  27.6 2.0 %pool_grad.2.refs_2_ = f32[1024,1536]{1,0:T(8,128)} custom-call(bf16[256,1536]{1,0:T(8,128)(2,1)S(1)} %join_queries.1.all_q_ref.q_ref, bf16[1024,128]{1,0:T(8,128)(2,1)S(1)} %get-tuple-element.62.refs_0_, bf16[1024,128]{1,0:T(8,128)(2,1)S(1)} %get-tuple-element.63.refs_1_), custom_call_target="tpu_custom_call" | custom-call | bytes 73800000 | tf_op jit(solution)/shard_map/pool_grad/pallas_call | solution.py:308
  29.6 0.2 collective-permute-done.9
  29.8 2.7 %collective-permute-start.11 = (bf16[8,1536]{1,0:T(8,128)(2,1)S(1)}, bf16[8,1536]{1,0:T(8,128)(2,1)S(1)}, u32[]{:S(2)}, u32[]{:S(2)}) collective-permute-start(bf16[8,1536]{1,0:T(8,128)(2,1)S(1)} %get-tuple-element.71), channel_id=1, source_target_pairs={{0,24},{2,26},{4,28},{6,30},{8,16},{10,18},{12,20},{14,22},{16,8},... | collective-permute-start | bytes 73736 | tf_op jit(solution)/shard_map/ppermute | solution.py:25
  32.5 0.4 %collective-permute-start.13 = (bf16[8,1536]{1,0:T(8,128)(2,1)S(1)}, bf16[8,1536]{1,0:T(8,128)(2,1)S(1)}, u32[]{:S(2)}, u32[]{:S(2)}) collective-permute-start(bf16[8,1536]{1,0:T(8,128)(2,1)S(1)} %get-tuple-element.72), channel_id=1, source_target_pairs={{0,8},{2,10},{4,12},{6,14},{8,0},{10,2},{12,4},{14,6},{16,24},{18,... | collective-permute-start | bytes 73736 | tf_op jit(solution)/shard_map/ppermute | solution.py:25
  33.0 1.3 %collective-permute-start.12 = (bf16[8,1536]{1,0:T(8,128)(2,1)S(1)}, bf16[8,1536]{1,0:T(8,128)(2,1)S(1)}, u32[]{:S(2)}, u32[]{:S(2)}) collective-permute-start(bf16[8,1536]{1,0:T(8,128)(2,1)S(1)} %get-tuple-element.73), channel_id=1, source_target_pairs={{0,16},{2,18},{4,20},{6,22},{8,24},{10,26},{12,28},{14,30},{16,0},... | collective-permute-start | bytes 73736 | tf_op jit(solution)/shard_map/ppermute | solution.py:25
  34.3 2.0 %pool_grad.3 = f32[1024,1536]{1,0:T(8,128)} custom-call(bf16[256,1536]{1,0:T(8,128)(2,1)S(1)} %join_queries.1.all_q_ref.q_ref, bf16[1024,128]{1,0:T(8,128)(2,1)S(1)} %get-tuple-element.62.refs_0_, bf16[1024,128]{1,0:T(8,128)(2,1)S(1)} %get-tuple-element.63.refs_1_, f32[1024,1536]{1,0:T(8,128)} %pool_grad.2.refs_2_), custom_call_target="tpu_custom_call", output_to_operand_aliasing={{}: (3, {})} | custom-call | bytes 73800000 | tf_op jit(solution)/shard_map/pool_grad/pallas_call | solution.py:308
  36.3 1.1 %collective-permute-done.10.refs_1_ = bf16[128,1536]{1,0:T(8,128)(2,1)S(1)} collective-permute-done((bf16[128,1536]{1,0:T(8,128)(2,1)S(1)}, bf16[128,1536]{1,0:T(8,128)(2,1)S(1)}, u32[]{:S(2)}, u32[]{:S(2)}) %collective-permute-start.10) | collective-permute-done | bytes 393248 | tf_op jit(solution)/shard_map/ppermute | solution.py:29
  37.3 0.9 %query_grad.1 = f32[128,1536]{1,0:T(8,128)} custom-call(f32[128,1536]{1,0:T(8,128)S(1)} %get-tuple-element.66.refs_0_, bf16[128,1536]{1,0:T(8,128)(2,1)S(1)} %collective-permute-done.10.refs_1_), custom_call_target="tpu_custom_call" | custom-call | bytes 73800000 | tf_op jit(solution)/shard_map/query_grad/pallas_call | solution.py:342
  38.3 0.6 %add_add_fusion = f32[8,1536]{1,0:T(8,128)} fusion(bf16[8,1536]{1,0:T(8,128)(2,1)S(1)} %collective-permute-done.13, bf16[8,1536]{1,0:T(8,128)(2,1)S(1)} %collective-permute-done.12, bf16[8,1536]{1,0:T(8,128)(2,1)S(1)} %collective-permute-done.11, f32[32,1536]{1,0:T(8,128)S(1)} %convert_add_fusion.1), kind=kLoop, calls=%fused_computation.6 | loop fusion | flops 73728 | bytes 172032 | tf_op jit(solution)/shard_map/add | solution.py:423
  (16 shorter events, 0.2 us)
Async XLA Ops:
  0.6 10.1 %collective-permute-start = (bf16[8,1536]{1,0:T(8,128)(2,1)}, bf16[8,1536]{1,0:T(8,128)(2,1)S(1)}, u32[]{:S(2)}, u32[]{:S(2)}) collective-permute-start(bf16[8,1536]{1,0:T(8,128)(2,1)} %tile_ref.1), channel_id=1, source_target_pairs={{0,8},{2,10},{4,12},{6,14},{8,0},{10,2},{12,4},{14,6},{16,24},{18,... | collective-permute-start | bytes 73736 | tf_op jit(solution)/shard_map/ppermute | solution.py:25
  3.7 7.0 %collective-permute-start.2 = (bf16[8,1536]{1,0:T(8,128)(2,1)}, bf16[8,1536]{1,0:T(8,128)(2,1)S(1)}, u32[]{:S(2)}, u32[]{:S(2)}) collective-permute-start(bf16[8,1536]{1,0:T(8,128)(2,1)} %tile_ref.1), channel_id=1, source_target_pairs={{0,24},{2,26},{4,28},{6,30},{8,16},{10,18},{12,20},{14,22},{16,8},... | collective-permute-start | bytes 73736 | tf_op jit(solution)/shard_map/ppermute | solution.py:25
  6.2 5.2 %collective-permute-start.1 = (bf16[8,1536]{1,0:T(8,128)(2,1)}, bf16[8,1536]{1,0:T(8,128)(2,1)S(1)}, u32[]{:S(2)}, u32[]{:S(2)}) collective-permute-start(bf16[8,1536]{1,0:T(8,128)(2,1)} %tile_ref.1), channel_id=1, source_target_pairs={{0,16},{2,18},{4,20},{6,22},{8,24},{10,26},{12,28},{14,30},{16,0},... | collective-permute-start | bytes 73736 | tf_op jit(solution)/shard_map/ppermute | solution.py:25
  6.3 10.5 %collective-permute-start.4 = (bf16[128,1536]{1,0:T(8,128)(2,1)}, bf16[128,1536]{1,0:T(8,128)(2,1)S(1)}, u32[]{:S(2)}, u32[]{:S(2)}) collective-permute-start(bf16[128,1536]{1,0:T(8,128)(2,1)} %q_ref.1), channel_id=1, source_target_pairs={{1,0},{0,1},{3,2},{2,3},{5,4},{4,5},{7,6},{6,7},{9,8},{8,9},{11,10... | collective-permute-start | bytes 1179656 | tf_op jit(solution)/shard_map/ppermute | solution.py:29
  11.4 4.7 %collective-permute-start.3 = (bf16[32,1536]{1,0:T(8,128)(2,1)S(1)}, bf16[32,1536]{1,0:T(8,128)(2,1)S(1)}, u32[]{:S(2)}, u32[]{:S(2)}) collective-permute-start(bf16[32,1536]{1,0:T(8,128)(2,1)S(1)} %pad_maximum_fusion.2), channel_id=1, source_target_pairs={{0,4},{2,6},{4,0},{6,2},{8,12},{10,14},{12,8},{14,10},{16,20},{18,... | collective-permute-start | bytes 294920 | tf_op jit(solution)/shard_map/ppermute | solution.py:25
  13.0 3.9 %collective-permute-start.5 = (s32[8,128]{1,0:T(8,128)S(1)}, s32[8,128]{1,0:T(8,128)S(1)}, u32[]{:S(2)}, u32[]{:S(2)}) collective-permute-start(s32[8,128]{1,0:T(8,128)S(1)} %get-tuple-element.48.refs_0_), channel_id=1, source_target_pairs={{1,0},{0,1},{3,2},{2,3},{5,4},{4,5},{7,6},{6,7},{9,8},{8,9},{11,10... | collective-permute-start | bytes 12296 | tf_op jit(solution)/shard_map/ppermute | solution.py:29
  16.9 1.5 %collective-permute-start.6 = (bf16[64,1536]{1,0:T(8,128)(2,1)S(1)}, bf16[64,1536]{1,0:T(8,128)(2,1)S(1)}, u32[]{:S(2)}, u32[]{:S(2)}) collective-permute-start(bf16[64,1536]{1,0:T(8,128)(2,1)S(1)} %pad_maximum_fusion.1), channel_id=1, source_target_pairs={{0,2},{2,0},{4,6},{6,4},{8,10},{10,8},{12,14},{14,12},{16,18},{18,... | collective-permute-start | bytes 589832 | tf_op jit(solution)/shard_map/ppermute | solution.py:25
  18.9 3.6 %collective-permute-start.7 = (f32[2,256]{1,0:T(2,128)S(1)}, f32[2,256]{1,0:T(2,128)S(1)}, u32[]{:S(2)}, u32[]{:S(2)}) collective-permute-start(f32[2,256]{1,0:T(2,128)S(1)} %get-tuple-element.47.part_ref), channel_id=1, source_target_pairs={{1,0},{0,1},{3,2},{2,3},{5,4},{4,5},{7,6},{6,7},{9,8},{8,9},{11,10... | collective-permute-start | bytes 6152 | tf_op jit(solution)/shard_map/ppermute | solution.py:29
  22.9 1.5 %collective-permute-start.8 = (bf16[64,1536]{1,0:T(8,128)(2,1)S(1)}, bf16[64,1536]{1,0:T(8,128)(2,1)S(1)}, u32[]{:S(2)}, u32[]{:S(2)}) collective-permute-start(bf16[64,1536]{1,0:T(8,128)(2,1)S(1)} %get-tuple-element.50), channel_id=1, source_target_pairs={{0,2},{2,0},{4,6},{6,4},{8,10},{10,8},{12,14},{14,12},{16,18},{18,... | collective-permute-start | bytes 589832 | tf_op jit(solution)/shard_map/ppermute | solution.py:25
  24.5 5.3 %collective-permute-start.9 = (bf16[32,1536]{1,0:T(8,128)(2,1)S(1)}, bf16[32,1536]{1,0:T(8,128)(2,1)S(1)}, u32[]{:S(2)}, u32[]{:S(2)}) collective-permute-start(bf16[32,1536]{1,0:T(8,128)(2,1)S(1)} %slice.37), channel_id=1, source_target_pairs={{0,4},{2,6},{4,0},{6,2},{8,12},{10,14},{12,8},{14,10},{16,20},{18,... | collective-permute-start | bytes 294920 | tf_op jit(solution)/shard_map/ppermute | solution.py:25
  26.1 11.2 %collective-permute-start.10 = (bf16[128,1536]{1,0:T(8,128)(2,1)S(1)}, bf16[128,1536]{1,0:T(8,128)(2,1)S(1)}, u32[]{:S(2)}, u32[]{:S(2)}) collective-permute-start(bf16[128,1536]{1,0:T(8,128)(2,1)S(1)} %get-tuple-element.67), channel_id=1, source_target_pairs={{1,0},{0,1},{3,2},{2,3},{5,4},{4,5},{7,6},{6,7},{9,8},{8,9},{11,10... | collective-permute-start | bytes 1179656 | tf_op jit(solution)/shard_map/ppermute | solution.py:29
  29.8 8.4 %collective-permute-start.11 = (bf16[8,1536]{1,0:T(8,128)(2,1)S(1)}, bf16[8,1536]{1,0:T(8,128)(2,1)S(1)}, u32[]{:S(2)}, u32[]{:S(2)}) collective-permute-start(bf16[8,1536]{1,0:T(8,128)(2,1)S(1)} %get-tuple-element.71), channel_id=1, source_target_pairs={{0,24},{2,26},{4,28},{6,30},{8,16},{10,18},{12,20},{14,22},{16,8},... | collective-permute-start | bytes 73736 | tf_op jit(solution)/shard_map/ppermute | solution.py:25
  32.5 5.7 %collective-permute-start.13 = (bf16[8,1536]{1,0:T(8,128)(2,1)S(1)}, bf16[8,1536]{1,0:T(8,128)(2,1)S(1)}, u32[]{:S(2)}, u32[]{:S(2)}) collective-permute-start(bf16[8,1536]{1,0:T(8,128)(2,1)S(1)} %get-tuple-element.72), channel_id=1, source_target_pairs={{0,8},{2,10},{4,12},{6,14},{8,0},{10,2},{12,4},{14,6},{16,24},{18,... | collective-permute-start | bytes 73736 | tf_op jit(solution)/shard_map/ppermute | solution.py:25
  33.0 5.3 %collective-permute-start.12 = (bf16[8,1536]{1,0:T(8,128)(2,1)S(1)}, bf16[8,1536]{1,0:T(8,128)(2,1)S(1)}, u32[]{:S(2)}, u32[]{:S(2)}) collective-permute-start(bf16[8,1536]{1,0:T(8,128)(2,1)S(1)} %get-tuple-element.73), channel_id=1, source_target_pairs={{0,16},{2,18},{4,20},{6,22},{8,24},{10,26},{12,28},{14,30},{16,0},... | collective-permute-start | bytes 73736 | tf_op jit(solution)/shard_map/ppermute | solution.py:25

commit v5 on v4

--- a/solution.py
+++ b/solution.py
@@ -72,7 +72,7 @@
 
 def own_kernel(
     chunk, scaling, ids_ref, pos_ref, tile_ref, q_ref, pool_ref,
-    tile_here, own_q_ref, pool_here, marks_ref, hard_ref, times_ref, stat_ref, sems,
+    tile_here, own_q_ref, pool_here, marks_ref, turned_ref, hard_ref, times_ref, stat_ref, sems,
 ):
     neg_count = ids_ref.shape[0]
     half = pool_ref.shape[0] // 2
@@ -97,6 +97,7 @@
     count_ids(chunk, marks_ref[0:neg_count, :], times_ref)
     for copy in others:
         copy.wait()
+    turned_ref[...] = own_q_ref[...].T
 
     def ready(c):
         if c % half == 0:
@@ -122,12 +123,13 @@
     return pl.pallas_call(
         functools.partial(own_kernel, chunk, features ** (-0.5)),
         in_specs=[HBM] * 5,
-        out_specs=[VMEM] * 7,
+        out_specs=[VMEM] * 8,
         out_shape=[
             pltpu.VMEM(tile.shape, BF16),
             pltpu.VMEM((rows, features), BF16),
             pltpu.VMEM((pool_rows, features), BF16),
             pltpu.VMEM((ids.shape[0] + 1, rows), jnp.int32),
+            pltpu.VMEM((features, rows), BF16),
         ]
         + hard_shapes(pool_rows, rows),
         scratch_shapes=[pltpu.SemaphoreType.DMA((6,))],
@@ -156,8 +158,11 @@
     )(*pieces)
 
 
-def group_kernel(piece, chunk, scaling, marks_ref, all_q_ref, pool_ref, hard_ref, times_ref, stat_ref):
+def group_kernel(
+    piece, chunk, scaling, marks_ref, all_q_ref, pool_ref, turned_ref, hard_ref, times_ref, stat_ref
+):
     rows = hard_ref.shape[1]
+    turned_ref[...] = all_q_ref[piece * rows : (piece + 1) * rows, :].T
     count_ids(chunk, marks_ref[0 : marks_ref.shape[0] - 1, :], times_ref)
     scores_of(
         chunk, scaling, all_q_ref.at[piece * rows : (piece + 1) * rows, :], pool_ref,
@@ -170,18 +175,19 @@
     return pl.pallas_call(
         functools.partial(group_kernel, piece, min(pool_rows, 128), pool.shape[1] ** (-0.5)),
         in_specs=[VMEM] * 3,
-        out_specs=[VMEM] * 3,
-        out_shape=hard_shapes(pool_rows, rows),
+        out_specs=[VMEM] * 4,
+        out_shape=[pltpu.VMEM((pool.shape[1], rows), BF16)] + hard_shapes(pool_rows, rows),
         compiler_params=PARAMS,
         cost_estimate=cost(20),
         name="group_scores",
     )(marks, all_q, pool)
 
 
-def score_kernel(scaling, keys_ref, q_ref, *refs):
+def score_kernel(owners, scaling, keys_ref, *refs):
     score_ref, part_ref = refs[-2:]
-    stats = [r[...] for r in refs[:-2]]
-    score = dot(keys_ref[...], q_ref[...], ROWS_ROWS) * scaling
+    turned = jnp.concatenate([r[...] for r in refs[:owners]], axis=1)
+    stats = [r[...] for r in refs[owners:-2]]
+    score = dot(keys_ref[...], turned, ROWS_COLS) * scaling
     score_ref[...] = score
     stat = jnp.concatenate(stats, axis=1)
     hard_top, hard_sum = stat[0:1, :], stat[1:2, :]
@@ -192,11 +198,11 @@
     )
 
 
-def passage_scores(keys, all_q, stats):
-    held, group = keys.shape[0], all_q.shape[0]
-    return pl.pallas_call(
-        functools.partial(score_kernel, keys.shape[1] ** (-0.5)),
-        in_specs=[VMEM] * (2 + len(stats)),
+def passage_scores(keys, turned, stats):
+    held, group = keys.shape[0], len(turned) * turned[0].shape[1]
+    return pl.pallas_call(
+        functools.partial(score_kernel, len(turned), keys.shape[1] ** (-0.5)),
+        in_specs=[VMEM] * (1 + len(turned) + len(stats)),
         out_specs=[VMEM] * 2,
         out_shape=[
             jax.ShapeDtypeStruct((held, group), F32),
@@ -204,7 +210,7 @@
         ],
         compiler_params=PARAMS,
         name="passage_scores",
-    )(keys, all_q, *stats)
+    )(keys, *turned, *stats)
 
 
 def weight_kernel(far, tile, owners, scaling, score_ref, q_ref, part_ref, other_ref, *refs):
@@ -365,11 +371,11 @@
     far_tiles = [across(passages, "blk", blocks, 4 * z) for z in range(far - 1, 0, -1)][::-1]
 
     group_q = [shifted(queries, "shard", owners, d) for d in range(1, owners)]
-    my_tile, own_q, pool, marks, *found = own_scores(
+    my_tile, own_q, pool, marks, own_turned, *found = own_scores(
         hard_ids.T, positives.reshape(1, rows), passages, queries, neg_pool
     )
     group_marks = [marks] + [shifted(marks, "shard", owners, d) for d in range(1, owners)]
-    hard = [found]
+    hard, turned = [found], [own_turned]
     all_q = join_queries([own_q] + group_q)
 
     keys = jnp.concatenate([my_tile] + far_tiles, axis=0)
@@ -381,9 +387,11 @@
             jnp.concatenate([keys, across(keys, "blk", blocks, bit)], axis=0)
         )
     for d in range(1, owners):
-        hard.append(group_scores(d, group_marks[d], all_q, pool))
-
-    score, part = passage_scores(keys, all_q, [h[2] for h in hard])
+        other_turned, *found = group_scores(d, group_marks[d], all_q, pool)
+        turned.append(other_turned)
+        hard.append(found)
+
+    score, part = passage_scores(keys, turned, [h[2] for h in hard])
     if owners == 2:
         other = shifted(part, "shard", owners, 1)
     else:

time: 39.1 us -> 39 us (level)
  no operation moved by 1% of the time
where the time goes in v5:
time: 39 us; the launch traced here: 38.8 us
  starting transfers between devices  19.5 us (50%)
  Pallas kernels  11.1 us (28%)
  waiting for transfers between devices  6.66 us (17%)
  between operations  0.83 us (2%)
  other arithmetic  0.75 us (2%)
    ppermute x10, starting transfers between devices, across(): return lax.ppermute(x, axis, [(i, i ^ distance) for i in range(count)])  13.4 us
    ppermute x4, starting transfers between devices, shifted(): lax.ppermute(x, axis, [((i + distance) % count, i) for i in range(count)])  6.02 us
    pallas_call x2, Pallas kernels, pool_rows_grad(): pl.pallas_call(functools.partial(pool_kernel, first, chunk, features ** (...  3.96 us
    ppermute x4, waiting for transfers between devices, shifted(): lax.ppermute(x, axis, [((i + distance) % count, i) for i in range(count)])  3.91 us
    pallas_call x1, Pallas kernels, own_scores(): pl.pallas_call(functools.partial(own_kernel, chunk, features ** (-0.5)),...  2.94 us
    ppermute x10, waiting for transfers between devices, across(): return lax.ppermute(x, axis, [(i, i ^ distance) for i in range(count)])  2.75 us
    pallas_call x2, Pallas kernels, query_part(): pl.pallas_call(functools.partial(query_kernel, piece, features ** (-0.5))...  1.43 us
    pallas_call x1, Pallas kernels, group_scores(): pl.pallas_call(functools.partial(group_kernel, piece, min(pool_rows, 128)...  1.11 us
  transfers between devices with their start and end apart: 14, of which 7 were waited for; matrix products, arithmetic and copies ran while one was open for 0% of the time, Pallas kernels for 27%

profile of v5, /device:TPU:0, one launch (start us, length us, event | category | flops | bytes accessed | tf_op | source)
XLA Modules:
  0.0 38.8 jit_solution(1173546098621400757)
XLA Ops:
  0.6 3.1 %collective-permute-start = (bf16[8,1536]{1,0:T(8,128)(2,1)}, bf16[8,1536]{1,0:T(8,128)(2,1)S(1)}, u32[]{:S(2)}, u32[]{:S(2)}) collective-permute-start(bf16[8,1536]{1,0:T(8,128)(2,1)} %tile_ref.1), channel_id=1, source_target_pairs={{0,8},{2,10},{4,12},{6,14},{8,0},{10,2},{12,4},{14,6},{16,24},{18,... | collective-permute-start | bytes 73736 | tf_op jit(solution)/shard_map/ppermute | solution.py:25
  3.7 2.5 %collective-permute-start.2 = (bf16[8,1536]{1,0:T(8,128)(2,1)}, bf16[8,1536]{1,0:T(8,128)(2,1)S(1)}, u32[]{:S(2)}, u32[]{:S(2)}) collective-permute-start(bf16[8,1536]{1,0:T(8,128)(2,1)} %tile_ref.1), channel_id=1, source_target_pairs={{0,24},{2,26},{4,28},{6,30},{8,16},{10,18},{12,20},{14,22},{16,8},... | collective-permute-start | bytes 73736 | tf_op jit(solution)/shard_map/ppermute | solution.py:25
  6.2 0.1 collective-permute-start.1
  6.3 1.5 %collective-permute-start.4 = (bf16[128,1536]{1,0:T(8,128)(2,1)}, bf16[128,1536]{1,0:T(8,128)(2,1)S(1)}, u32[]{:S(2)}, u32[]{:S(2)}) collective-permute-start(bf16[128,1536]{1,0:T(8,128)(2,1)} %q_ref.1), channel_id=1, source_target_pairs={{1,0},{0,1},{3,2},{2,3},{5,4},{4,5},{7,6},{6,7},{9,8},{8,9},{11,10... | collective-permute-start | bytes 1179656 | tf_op jit(solution)/shard_map/ppermute | solution.py:29
  7.8 2.9 %own_scores.1 = (bf16[8,1536]{1,0:T(8,128)(2,1)S(1)}, bf16[128,1536]{1,0:T(8,128)(2,1)S(1)}, bf16[1024,1536]{1,0:T(8,128)(2,1)S(1)}, s32[8,128]{1,0:T(8,128)S(1)...) custom-call(s32[7,128]{1,0:T(8,128)} %bitcast.2, ...), custom_call_target="tpu_custom_call" | custom-call | bytes 73800000 | tf_op jit(solution)/shard_map/own_scores/pallas_call | solution.py:123
  10.8 0.6 %collective-permute-done.1 = bf16[8,1536]{1,0:T(8,128)(2,1)S(1)} collective-permute-done((bf16[8,1536]{1,0:T(8,128)(2,1)}, bf16[8,1536]{1,0:T(8,128)(2,1)S(1)}, u32[]{:S(2)}, u32[]{:S(2)}) %collective-permute-start.1) | collective-permute-done | bytes 24608 | tf_op jit(solution)/shard_map/ppermute | solution.py:25
  11.4 1.6 %collective-permute-start.3 = (bf16[32,1536]{1,0:T(8,128)(2,1)S(1)}, bf16[32,1536]{1,0:T(8,128)(2,1)S(1)}, u32[]{:S(2)}, u32[]{:S(2)}) collective-permute-start(bf16[32,1536]{1,0:T(8,128)(2,1)S(1)} %pad_maximum_fusion.2), channel_id=1, source_target_pairs={{0,4},{2,6},{4,0},{6,2},{8,12},{10,14},{12,8},{14,10},{16,20},{18,... | collective-permute-start | bytes 294920 | tf_op jit(solution)/shard_map/ppermute | solution.py:25
  13.0 1.5 %collective-permute-start.5 = (s32[8,128]{1,0:T(8,128)S(1)}, s32[8,128]{1,0:T(8,128)S(1)}, u32[]{:S(2)}, u32[]{:S(2)}) collective-permute-start(s32[8,128]{1,0:T(8,128)S(1)} %get-tuple-element.52.refs_0_), channel_id=1, source_target_pairs={{1,0},{0,1},{3,2},{2,3},{5,4},{4,5},{7,6},{6,7},{9,8},{8,9},{11,10... | collective-permute-start | bytes 12296 | tf_op jit(solution)/shard_map/ppermute | solution.py:29
  14.5 1.6 %collective-permute-done.3 = bf16[32,1536]{1,0:T(8,128)(2,1)S(1)} collective-permute-done((bf16[32,1536]{1,0:T(8,128)(2,1)S(1)}, bf16[32,1536]{1,0:T(8,128)(2,1)S(1)}, u32[]{:S(2)}, u32[]{:S(2)}) %collective-permute-start.3) | collective-permute-done | bytes 98336 | tf_op jit(solution)/shard_map/ppermute | solution.py:25
  16.1 0.8 %collective-permute-done.4.refs_1_ = bf16[128,1536]{1,0:T(8,128)(2,1)S(1)} collective-permute-done((bf16[128,1536]{1,0:T(8,128)(2,1)}, bf16[128,1536]{1,0:T(8,128)(2,1)S(1)}, u32[]{:S(2)}, u32[]{:S(2)}) %collective-permute-start.4) | collective-permute-done | bytes 393248 | tf_op jit(solution)/shard_map/ppermute | solution.py:29
  16.9 0.1 join_queries.1.all_q_ref.q_ref
  16.9 0.1 collective-permute-start.6
  17.0 1.1 %group_scores.1 = (bf16[1536,128]{1,0:T(8,128)(2,1)S(1)}, f32[1024,128]{1,0:T(8,128)S(1)}, f32[1024,128]{1,0:T(8,128)S(1)}, f32[2,128]{1,0:T(2,128)S(1)}) custom-call(s32[8,128]{1,0:T(8,128)S(1)} %collective-permute-done.5.marks_ref.refs_1_, bf16[256,1536]{1,0:T(8,128)(2,1)S(1)} %join_queries.1.all_q_ref.q_ref, bf16[1024,1536]{1,0:T(8,128)(2,1)S(1)} %get-tuple-element.46.pool_ref), custom_call_target="tpu_custom_call" | custom-call | bytes 73800000 | tf_op jit(solution)/shard_map/group_scores/pallas_call | solution.py:175
  18.1 0.3 collective-permute-done.6
  18.5 0.3 passage_scores.1
  18.8 1.6 %collective-permute-start.7 = (f32[2,256]{1,0:T(2,128)S(1)}, f32[2,256]{1,0:T(2,128)S(1)}, u32[]{:S(2)}, u32[]{:S(2)}) collective-permute-start(f32[2,256]{1,0:T(2,128)S(1)} %get-tuple-element.51.part_ref), channel_id=1, source_target_pairs={{1,0},{0,1},{3,2},{2,3},{5,4},{4,5},{7,6},{6,7},{9,8},{8,9},{11,10... | collective-permute-start | bytes 6152 | tf_op jit(solution)/shard_map/ppermute | solution.py:29
  20.4 2.1 %collective-permute-done.7.other_ref = f32[2,256]{1,0:T(2,128)S(1)} collective-permute-done((f32[2,256]{1,0:T(2,128)S(1)}, f32[2,256]{1,0:T(2,128)S(1)}, u32[]{:S(2)}, u32[]{:S(2)}) %collective-permute-start.7) | collective-permute-done | bytes 2080 | tf_op jit(solution)/shard_map/ppermute | solution.py:29
  22.5 0.3 passage_weights.1
  22.8 0.1 collective-permute-start.8
  22.9 0.7 %query_part.2 = (bf16[128,1536]{1,0:T(8,128)(2,1)S(1)}, bf16[1024,128]{1,0:T(8,128)(2,1)S(1)}) custom-call(f32[1024,128]{1,0:T(8,128)S(1)} %get-tuple-element.55.hard_ref, f32[1024,128]{1,0:T(8,128)S(1)} %get-tuple-element.56.times_ref, f32[1,256]{1,0:T(1,128)S(1)} %get-tuple-element.57.log_ref, bf16[128,256]{1,0:T(8,128)(2,1)S(1)} %get-tuple-element.58.w_ref, ...), custom_call_target="tpu_custom_call" | custom-call | bytes 36900000 | tf_op jit(solution)/shard_map/query_part/pallas_call | solution.py:278
  23.6 0.7 %query_part.3 = (f32[128,1536]{1,0:T(8,128)S(1)}, bf16[1024,128]{1,0:T(8,128)(2,1)S(1)}) custom-call(f32[1024,128]{1,0:T(8,128)S(1)} %get-tuple-element.61.hard_ref, f32[1024,128]{1,0:T(8,128)S(1)} %get-tuple-element.62.times_ref, f32[1,256]{1,0:T(1,128)S(1)} %get-tuple-element.57.log_ref, bf16[128,256]{1,0:T(8,128)(2,1)S(1)} %get-tuple-element.58.w_ref, ...), custom_call_target="tpu_custom_call" | custom-call | bytes 36900000 | tf_op jit(solution)/shard_map/query_part/pallas_call | solution.py:278
  24.4 1.6 %collective-permute-start.9 = (bf16[32,1536]{1,0:T(8,128)(2,1)S(1)}, bf16[32,1536]{1,0:T(8,128)(2,1)S(1)}, u32[]{:S(2)}, u32[]{:S(2)}) collective-permute-start(bf16[32,1536]{1,0:T(8,128)(2,1)S(1)} %slice.37), channel_id=1, source_target_pairs={{0,4},{2,6},{4,0},{6,2},{8,12},{10,14},{12,8},{14,10},{16,20},{18,... | collective-permute-start | bytes 294920 | tf_op jit(solution)/shard_map/ppermute | solution.py:25
  26.0 1.5 %collective-permute-start.10 = (bf16[128,1536]{1,0:T(8,128)(2,1)S(1)}, bf16[128,1536]{1,0:T(8,128)(2,1)S(1)}, u32[]{:S(2)}, u32[]{:S(2)}) collective-permute-start(bf16[128,1536]{1,0:T(8,128)(2,1)S(1)} %get-tuple-element.71), channel_id=1, source_target_pairs={{1,0},{0,1},{3,2},{2,3},{5,4},{4,5},{7,6},{6,7},{9,8},{8,9},{11,10... | collective-permute-start | bytes 1179656 | tf_op jit(solution)/shard_map/ppermute | solution.py:29
  27.5 2.0 %pool_grad.2.refs_2_ = f32[1024,1536]{1,0:T(8,128)} custom-call(bf16[256,1536]{1,0:T(8,128)(2,1)S(1)} %join_queries.1.all_q_ref.q_ref, bf16[1024,128]{1,0:T(8,128)(2,1)S(1)} %get-tuple-element.66.refs_0_, bf16[1024,128]{1,0:T(8,128)(2,1)S(1)} %get-tuple-element.67.refs_1_), custom_call_target="tpu_custom_call" | custom-call | bytes 73800000 | tf_op jit(solution)/shard_map/pool_grad/pallas_call | solution.py:314
  29.4 0.2 collective-permute-done.9
  29.7 2.7 %collective-permute-start.11 = (bf16[8,1536]{1,0:T(8,128)(2,1)S(1)}, bf16[8,1536]{1,0:T(8,128)(2,1)S(1)}, u32[]{:S(2)}, u32[]{:S(2)}) collective-permute-start(bf16[8,1536]{1,0:T(8,128)(2,1)S(1)} %get-tuple-element.75), channel_id=1, source_target_pairs={{0,24},{2,26},{4,28},{6,30},{8,16},{10,18},{12,20},{14,22},{16,8},... | collective-permute-start | bytes 73736 | tf_op jit(solution)/shard_map/ppermute | solution.py:25
  32.4 0.4 %collective-permute-start.13 = (bf16[8,1536]{1,0:T(8,128)(2,1)S(1)}, bf16[8,1536]{1,0:T(8,128)(2,1)S(1)}, u32[]{:S(2)}, u32[]{:S(2)}) collective-permute-start(bf16[8,1536]{1,0:T(8,128)(2,1)S(1)} %get-tuple-element.76), channel_id=1, source_target_pairs={{0,8},{2,10},{4,12},{6,14},{8,0},{10,2},{12,4},{14,6},{16,24},{18,... | collective-permute-start | bytes 73736 | tf_op jit(solution)/shard_map/ppermute | solution.py:25
  32.9 1.3 %collective-permute-start.12 = (bf16[8,1536]{1,0:T(8,128)(2,1)S(1)}, bf16[8,1536]{1,0:T(8,128)(2,1)S(1)}, u32[]{:S(2)}, u32[]{:S(2)}) collective-permute-start(bf16[8,1536]{1,0:T(8,128)(2,1)S(1)} %get-tuple-element.77), channel_id=1, source_target_pairs={{0,16},{2,18},{4,20},{6,22},{8,24},{10,26},{12,28},{14,30},{16,0},... | collective-permute-start | bytes 73736 | tf_op jit(solution)/shard_map/ppermute | solution.py:25
  34.2 2.0 %pool_grad.3 = f32[1024,1536]{1,0:T(8,128)} custom-call(bf16[256,1536]{1,0:T(8,128)(2,1)S(1)} %join_queries.1.all_q_ref.q_ref, bf16[1024,128]{1,0:T(8,128)(2,1)S(1)} %get-tuple-element.66.refs_0_, bf16[1024,128]{1,0:T(8,128)(2,1)S(1)} %get-tuple-element.67.refs_1_, f32[1024,1536]{1,0:T(8,128)} %pool_grad.2.refs_2_), custom_call_target="tpu_custom_call", output_to_operand_aliasing={{}: (3, {})} | custom-call | bytes 73800000 | tf_op jit(solution)/shard_map/pool_grad/pallas_call | solution.py:314
  36.2 1.1 %collective-permute-done.10.refs_1_ = bf16[128,1536]{1,0:T(8,128)(2,1)S(1)} collective-permute-done((bf16[128,1536]{1,0:T(8,128)(2,1)S(1)}, bf16[128,1536]{1,0:T(8,128)(2,1)S(1)}, u32[]{:S(2)}, u32[]{:S(2)}) %collective-permute-start.10) | collective-permute-done | bytes 393248 | tf_op jit(solution)/shard_map/ppermute | solution.py:29
  37.2 0.9 %query_grad.1 = f32[128,1536]{1,0:T(8,128)} custom-call(f32[128,1536]{1,0:T(8,128)S(1)} %get-tuple-element.70.refs_0_, bf16[128,1536]{1,0:T(8,128)(2,1)S(1)} %collective-permute-done.10.refs_1_), custom_call_target="tpu_custom_call" | custom-call | bytes 73800000 | tf_op jit(solution)/shard_map/query_grad/pallas_call | solution.py:348
  38.2 0.6 %add_add_fusion = f32[8,1536]{1,0:T(8,128)} fusion(bf16[8,1536]{1,0:T(8,128)(2,1)S(1)} %collective-permute-done.13, bf16[8,1536]{1,0:T(8,128)(2,1)S(1)} %collective-permute-done.12, bf16[8,1536]{1,0:T(8,128)(2,1)S(1)} %collective-permute-done.11, f32[32,1536]{1,0:T(8,128)S(1)} %convert_add_fusion.1), kind=kLoop, calls=%fused_computation.6 | loop fusion | flops 73728 | bytes 172032 | tf_op jit(solution)/shard_map/add | solution.py:431
  (16 shorter events, 0.2 us)
Async XLA Ops:
  0.6 10.1 %collective-permute-start = (bf16[8,1536]{1,0:T(8,128)(2,1)}, bf16[8,1536]{1,0:T(8,128)(2,1)S(1)}, u32[]{:S(2)}, u32[]{:S(2)}) collective-permute-start(bf16[8,1536]{1,0:T(8,128)(2,1)} %tile_ref.1), channel_id=1, source_target_pairs={{0,8},{2,10},{4,12},{6,14},{8,0},{10,2},{12,4},{14,6},{16,24},{18,... | collective-permute-start | bytes 73736 | tf_op jit(solution)/shard_map/ppermute | solution.py:25
  3.7 7.0 %collective-permute-start.2 = (bf16[8,1536]{1,0:T(8,128)(2,1)}, bf16[8,1536]{1,0:T(8,128)(2,1)S(1)}, u32[]{:S(2)}, u32[]{:S(2)}) collective-permute-start(bf16[8,1536]{1,0:T(8,128)(2,1)} %tile_ref.1), channel_id=1, source_target_pairs={{0,24},{2,26},{4,28},{6,30},{8,16},{10,18},{12,20},{14,22},{16,8},... | collective-permute-start | bytes 73736 | tf_op jit(solution)/shard_map/ppermute | solution.py:25
  6.2 5.2 %collective-permute-start.1 = (bf16[8,1536]{1,0:T(8,128)(2,1)}, bf16[8,1536]{1,0:T(8,128)(2,1)S(1)}, u32[]{:S(2)}, u32[]{:S(2)}) collective-permute-start(bf16[8,1536]{1,0:T(8,128)(2,1)} %tile_ref.1), channel_id=1, source_target_pairs={{0,16},{2,18},{4,20},{6,22},{8,24},{10,26},{12,28},{14,30},{16,0},... | collective-permute-start | bytes 73736 | tf_op jit(solution)/shard_map/ppermute | solution.py:25
  6.3 10.5 %collective-permute-start.4 = (bf16[128,1536]{1,0:T(8,128)(2,1)}, bf16[128,1536]{1,0:T(8,128)(2,1)S(1)}, u32[]{:S(2)}, u32[]{:S(2)}) collective-permute-start(bf16[128,1536]{1,0:T(8,128)(2,1)} %q_ref.1), channel_id=1, source_target_pairs={{1,0},{0,1},{3,2},{2,3},{5,4},{4,5},{7,6},{6,7},{9,8},{8,9},{11,10... | collective-permute-start | bytes 1179656 | tf_op jit(solution)/shard_map/ppermute | solution.py:29
  11.4 4.7 %collective-permute-start.3 = (bf16[32,1536]{1,0:T(8,128)(2,1)S(1)}, bf16[32,1536]{1,0:T(8,128)(2,1)S(1)}, u32[]{:S(2)}, u32[]{:S(2)}) collective-permute-start(bf16[32,1536]{1,0:T(8,128)(2,1)S(1)} %pad_maximum_fusion.2), channel_id=1, source_target_pairs={{0,4},{2,6},{4,0},{6,2},{8,12},{10,14},{12,8},{14,10},{16,20},{18,... | collective-permute-start | bytes 294920 | tf_op jit(solution)/shard_map/ppermute | solution.py:25
  13.0 3.9 %collective-permute-start.5 = (s32[8,128]{1,0:T(8,128)S(1)}, s32[8,128]{1,0:T(8,128)S(1)}, u32[]{:S(2)}, u32[]{:S(2)}) collective-permute-start(s32[8,128]{1,0:T(8,128)S(1)} %get-tuple-element.52.refs_0_), channel_id=1, source_target_pairs={{1,0},{0,1},{3,2},{2,3},{5,4},{4,5},{7,6},{6,7},{9,8},{8,9},{11,10... | collective-permute-start | bytes 12296 | tf_op jit(solution)/shard_map/ppermute | solution.py:29
  16.9 1.5 %collective-permute-start.6 = (bf16[64,1536]{1,0:T(8,128)(2,1)S(1)}, bf16[64,1536]{1,0:T(8,128)(2,1)S(1)}, u32[]{:S(2)}, u32[]{:S(2)}) collective-permute-start(bf16[64,1536]{1,0:T(8,128)(2,1)S(1)} %pad_maximum_fusion.1), channel_id=1, source_target_pairs={{0,2},{2,0},{4,6},{6,4},{8,10},{10,8},{12,14},{14,12},{16,18},{18,... | collective-permute-start | bytes 589832 | tf_op jit(solution)/shard_map/ppermute | solution.py:25
  18.8 3.6 %collective-permute-start.7 = (f32[2,256]{1,0:T(2,128)S(1)}, f32[2,256]{1,0:T(2,128)S(1)}, u32[]{:S(2)}, u32[]{:S(2)}) collective-permute-start(f32[2,256]{1,0:T(2,128)S(1)} %get-tuple-element.51.part_ref), channel_id=1, source_target_pairs={{1,0},{0,1},{3,2},{2,3},{5,4},{4,5},{7,6},{6,7},{9,8},{8,9},{11,10... | collective-permute-start | bytes 6152 | tf_op jit(solution)/shard_map/ppermute | solution.py:29
  22.8 1.5 %collective-permute-start.8 = (bf16[64,1536]{1,0:T(8,128)(2,1)S(1)}, bf16[64,1536]{1,0:T(8,128)(2,1)S(1)}, u32[]{:S(2)}, u32[]{:S(2)}) collective-permute-start(bf16[64,1536]{1,0:T(8,128)(2,1)S(1)} %get-tuple-element.54), channel_id=1, source_target_pairs={{0,2},{2,0},{4,6},{6,4},{8,10},{10,8},{12,14},{14,12},{16,18},{18,... | collective-permute-start | bytes 589832 | tf_op jit(solution)/shard_map/ppermute | solution.py:25
  24.4 5.3 %collective-permute-start.9 = (bf16[32,1536]{1,0:T(8,128)(2,1)S(1)}, bf16[32,1536]{1,0:T(8,128)(2,1)S(1)}, u32[]{:S(2)}, u32[]{:S(2)}) collective-permute-start(bf16[32,1536]{1,0:T(8,128)(2,1)S(1)} %slice.37), channel_id=1, source_target_pairs={{0,4},{2,6},{4,0},{6,2},{8,12},{10,14},{12,8},{14,10},{16,20},{18,... | collective-permute-start | bytes 294920 | tf_op jit(solution)/shard_map/ppermute | solution.py:25
  26.0 11.2 %collective-permute-start.10 = (bf16[128,1536]{1,0:T(8,128)(2,1)S(1)}, bf16[128,1536]{1,0:T(8,128)(2,1)S(1)}, u32[]{:S(2)}, u32[]{:S(2)}) collective-permute-start(bf16[128,1536]{1,0:T(8,128)(2,1)S(1)} %get-tuple-element.71), channel_id=1, source_target_pairs={{1,0},{0,1},{3,2},{2,3},{5,4},{4,5},{7,6},{6,7},{9,8},{8,9},{11,10... | collective-permute-start | bytes 1179656 | tf_op jit(solution)/shard_map/ppermute | solution.py:29
  29.7 8.4 %collective-permute-start.11 = (bf16[8,1536]{1,0:T(8,128)(2,1)S(1)}, bf16[8,1536]{1,0:T(8,128)(2,1)S(1)}, u32[]{:S(2)}, u32[]{:S(2)}) collective-permute-start(bf16[8,1536]{1,0:T(8,128)(2,1)S(1)} %get-tuple-element.75), channel_id=1, source_target_pairs={{0,24},{2,26},{4,28},{6,30},{8,16},{10,18},{12,20},{14,22},{16,8},... | collective-permute-start | bytes 73736 | tf_op jit(solution)/shard_map/ppermute | solution.py:25
  32.4 5.7 %collective-permute-start.13 = (bf16[8,1536]{1,0:T(8,128)(2,1)S(1)}, bf16[8,1536]{1,0:T(8,128)(2,1)S(1)}, u32[]{:S(2)}, u32[]{:S(2)}) collective-permute-start(bf16[8,1536]{1,0:T(8,128)(2,1)S(1)} %get-tuple-element.76), channel_id=1, source_target_pairs={{0,8},{2,10},{4,12},{6,14},{8,0},{10,2},{12,4},{14,6},{16,24},{18,... | collective-permute-start | bytes 73736 | tf_op jit(solution)/shard_map/ppermute | solution.py:25
  32.9 5.3 %collective-permute-start.12 = (bf16[8,1536]{1,0:T(8,128)(2,1)S(1)}, bf16[8,1536]{1,0:T(8,128)(2,1)S(1)}, u32[]{:S(2)}, u32[]{:S(2)}) collective-permute-start(bf16[8,1536]{1,0:T(8,128)(2,1)S(1)} %get-tuple-element.77), channel_id=1, source_target_pairs={{0,16},{2,18},{4,20},{6,22},{8,24},{10,26},{12,28},{14,30},{16,0},... | collective-permute-start | bytes 73736 | tf_op jit(solution)/shard_map/ppermute | solution.py:25

commit v6 on v5

--- a/solution.py
+++ b/solution.py
@@ -344,7 +344,7 @@
 
 def sum_terms(terms):
     rows = terms[0].shape[0]
-    chunk = min(rows, 32)
+    chunk = min(rows, 16)
     return pl.pallas_call(
         functools.partial(sum_kernel, chunk),
         in_specs=[VMEM] * len(terms),

time: 39 us -> 39 us (level)
  no operation moved by 1% of the time
where the time goes in v6:
time: 39 us; the launch traced here: 38.8 us
  starting transfers between devices  19.5 us (50%)
  Pallas kernels  11.1 us (28%)
  waiting for transfers between devices  6.66 us (17%)
  between operations  0.83 us (2%)
  other arithmetic  0.75 us (2%)
    ppermute x10, starting transfers between devices, across(): return lax.ppermute(x, axis, [(i, i ^ distance) for i in range(count)])  13.4 us
    ppermute x4, starting transfers between devices, shifted(): lax.ppermute(x, axis, [((i + distance) % count, i) for i in range(count)])  6.02 us
    pallas_call x2, Pallas kernels, pool_rows_grad(): pl.pallas_call(functools.partial(pool_kernel, first, chunk, features ** (...  3.96 us
    ppermute x4, waiting for transfers between devices, shifted(): lax.ppermute(x, axis, [((i + distance) % count, i) for i in range(count)])  3.91 us
    pallas_call x1, Pallas kernels, own_scores(): pl.pallas_call(functools.partial(own_kernel, chunk, features ** (-0.5)),...  2.94 us
    ppermute x10, waiting for transfers between devices, across(): return lax.ppermute(x, axis, [(i, i ^ distance) for i in range(count)])  2.75 us
    pallas_call x2, Pallas kernels, query_part(): pl.pallas_call(functools.partial(query_kernel, piece, features ** (-0.5))...  1.43 us
    pallas_call x1, Pallas kernels, group_scores(): pl.pallas_call(functools.partial(group_kernel, piece, min(pool_rows, 128)...  1.11 us
  transfers between devices with their start and end apart: 14, of which 7 were waited for; matrix products, arithmetic and copies ran while one was open for 0% of the time, Pallas kernels for 27%

profile of v6, /device:TPU:0, one launch (start us, length us, event | category | flops | bytes accessed | tf_op | source)
XLA Modules:
  0.0 38.8 jit_solution(10849907466027716059)
XLA Ops:
  0.6 3.1 %collective-permute-start = (bf16[8,1536]{1,0:T(8,128)(2,1)}, bf16[8,1536]{1,0:T(8,128)(2,1)S(1)}, u32[]{:S(2)}, u32[]{:S(2)}) collective-permute-start(bf16[8,1536]{1,0:T(8,128)(2,1)} %tile_ref.1), channel_id=1, source_target_pairs={{0,8},{2,10},{4,12},{6,14},{8,0},{10,2},{12,4},{14,6},{16,24},{18,... | collective-permute-start | bytes 73736 | tf_op jit(solution)/shard_map/ppermute | solution.py:25
  3.7 2.5 %collective-permute-start.2 = (bf16[8,1536]{1,0:T(8,128)(2,1)}, bf16[8,1536]{1,0:T(8,128)(2,1)S(1)}, u32[]{:S(2)}, u32[]{:S(2)}) collective-permute-start(bf16[8,1536]{1,0:T(8,128)(2,1)} %tile_ref.1), channel_id=1, source_target_pairs={{0,24},{2,26},{4,28},{6,30},{8,16},{10,18},{12,20},{14,22},{16,8},... | collective-permute-start | bytes 73736 | tf_op jit(solution)/shard_map/ppermute | solution.py:25
  6.2 0.1 collective-permute-start.1
  6.3 1.5 %collective-permute-start.4 = (bf16[128,1536]{1,0:T(8,128)(2,1)}, bf16[128,1536]{1,0:T(8,128)(2,1)S(1)}, u32[]{:S(2)}, u32[]{:S(2)}) collective-permute-start(bf16[128,1536]{1,0:T(8,128)(2,1)} %q_ref.1), channel_id=1, source_target_pairs={{1,0},{0,1},{3,2},{2,3},{5,4},{4,5},{7,6},{6,7},{9,8},{8,9},{11,10... | collective-permute-start | bytes 1179656 | tf_op jit(solution)/shard_map/ppermute | solution.py:29
  7.8 2.9 %own_scores.1 = (bf16[8,1536]{1,0:T(8,128)(2,1)S(1)}, bf16[128,1536]{1,0:T(8,128)(2,1)S(1)}, bf16[1024,1536]{1,0:T(8,128)(2,1)S(1)}, s32[8,128]{1,0:T(8,128)S(1)...) custom-call(s32[7,128]{1,0:T(8,128)} %bitcast.2, ...), custom_call_target="tpu_custom_call" | custom-call | bytes 73800000 | tf_op jit(solution)/shard_map/own_scores/pallas_call | solution.py:123
  10.8 0.6 %collective-permute-done.1 = bf16[8,1536]{1,0:T(8,128)(2,1)S(1)} collective-permute-done((bf16[8,1536]{1,0:T(8,128)(2,1)}, bf16[8,1536]{1,0:T(8,128)(2,1)S(1)}, u32[]{:S(2)}, u32[]{:S(2)}) %collective-permute-start.1) | collective-permute-done | bytes 24608 | tf_op jit(solution)/shard_map/ppermute | solution.py:25
  11.4 1.6 %collective-permute-start.3 = (bf16[32,1536]{1,0:T(8,128)(2,1)S(1)}, bf16[32,1536]{1,0:T(8,128)(2,1)S(1)}, u32[]{:S(2)}, u32[]{:S(2)}) collective-permute-start(bf16[32,1536]{1,0:T(8,128)(2,1)S(1)} %pad_maximum_fusion.2), channel_id=1, source_target_pairs={{0,4},{2,6},{4,0},{6,2},{8,12},{10,14},{12,8},{14,10},{16,20},{18,... | collective-permute-start | bytes 294920 | tf_op jit(solution)/shard_map/ppermute | solution.py:25
  13.0 1.5 %collective-permute-start.5 = (s32[8,128]{1,0:T(8,128)S(1)}, s32[8,128]{1,0:T(8,128)S(1)}, u32[]{:S(2)}, u32[]{:S(2)}) collective-permute-start(s32[8,128]{1,0:T(8,128)S(1)} %get-tuple-element.52.refs_0_), channel_id=1, source_target_pairs={{1,0},{0,1},{3,2},{2,3},{5,4},{4,5},{7,6},{6,7},{9,8},{8,9},{11,10... | collective-permute-start | bytes 12296 | tf_op jit(solution)/shard_map/ppermute | solution.py:29
  14.5 1.6 %collective-permute-done.3 = bf16[32,1536]{1,0:T(8,128)(2,1)S(1)} collective-permute-done((bf16[32,1536]{1,0:T(8,128)(2,1)S(1)}, bf16[32,1536]{1,0:T(8,128)(2,1)S(1)}, u32[]{:S(2)}, u32[]{:S(2)}) %collective-permute-start.3) | collective-permute-done | bytes 98336 | tf_op jit(solution)/shard_map/ppermute | solution.py:25
  16.1 0.8 %collective-permute-done.4.refs_1_ = bf16[128,1536]{1,0:T(8,128)(2,1)S(1)} collective-permute-done((bf16[128,1536]{1,0:T(8,128)(2,1)}, bf16[128,1536]{1,0:T(8,128)(2,1)S(1)}, u32[]{:S(2)}, u32[]{:S(2)}) %collective-permute-start.4) | collective-permute-done | bytes 393248 | tf_op jit(solution)/shard_map/ppermute | solution.py:29
  16.9 0.1 join_queries.1.all_q_ref.q_ref
  16.9 0.1 collective-permute-start.6
  17.0 1.1 %group_scores.1 = (bf16[1536,128]{1,0:T(8,128)(2,1)S(1)}, f32[1024,128]{1,0:T(8,128)S(1)}, f32[1024,128]{1,0:T(8,128)S(1)}, f32[2,128]{1,0:T(2,128)S(1)}) custom-call(s32[8,128]{1,0:T(8,128)S(1)} %collective-permute-done.5.marks_ref.refs_1_, bf16[256,1536]{1,0:T(8,128)(2,1)S(1)} %join_queries.1.all_q_ref.q_ref, bf16[1024,1536]{1,0:T(8,128)(2,1)S(1)} %get-tuple-element.46.pool_ref), custom_call_target="tpu_custom_call" | custom-call | bytes 73800000 | tf_op jit(solution)/shard_map/group_scores/pallas_call | solution.py:175
  18.1 0.3 collective-permute-done.6
  18.5 0.3 passage_scores.1
  18.8 1.6 %collective-permute-start.7 = (f32[2,256]{1,0:T(2,128)S(1)}, f32[2,256]{1,0:T(2,128)S(1)}, u32[]{:S(2)}, u32[]{:S(2)}) collective-permute-start(f32[2,256]{1,0:T(2,128)S(1)} %get-tuple-element.51.part_ref), channel_id=1, source_target_pairs={{1,0},{0,1},{3,2},{2,3},{5,4},{4,5},{7,6},{6,7},{9,8},{8,9},{11,10... | collective-permute-start | bytes 6152 | tf_op jit(solution)/shard_map/ppermute | solution.py:29
  20.4 2.1 %collective-permute-done.7.other_ref = f32[2,256]{1,0:T(2,128)S(1)} collective-permute-done((f32[2,256]{1,0:T(2,128)S(1)}, f32[2,256]{1,0:T(2,128)S(1)}, u32[]{:S(2)}, u32[]{:S(2)}) %collective-permute-start.7) | collective-permute-done | bytes 2080 | tf_op jit(solution)/shard_map/ppermute | solution.py:29
  22.5 0.3 passage_weights.1
  22.8 0.1 collective-permute-start.8
  22.9 0.7 %query_part.2 = (bf16[128,1536]{1,0:T(8,128)(2,1)S(1)}, bf16[1024,128]{1,0:T(8,128)(2,1)S(1)}) custom-call(f32[1024,128]{1,0:T(8,128)S(1)} %get-tuple-element.55.hard_ref, f32[1024,128]{1,0:T(8,128)S(1)} %get-tuple-element.56.times_ref, f32[1,256]{1,0:T(1,128)S(1)} %get-tuple-element.57.log_ref, bf16[128,256]{1,0:T(8,128)(2,1)S(1)} %get-tuple-element.58.w_ref, ...), custom_call_target="tpu_custom_call" | custom-call | bytes 36900000 | tf_op jit(solution)/shard_map/query_part/pallas_call | solution.py:278
  23.6 0.7 %query_part.3 = (f32[128,1536]{1,0:T(8,128)S(1)}, bf16[1024,128]{1,0:T(8,128)(2,1)S(1)}) custom-call(f32[1024,128]{1,0:T(8,128)S(1)} %get-tuple-element.61.hard_ref, f32[1024,128]{1,0:T(8,128)S(1)} %get-tuple-element.62.times_ref, f32[1,256]{1,0:T(1,128)S(1)} %get-tuple-element.57.log_ref, bf16[128,256]{1,0:T(8,128)(2,1)S(1)} %get-tuple-element.58.w_ref, ...), custom_call_target="tpu_custom_call" | custom-call | bytes 36900000 | tf_op jit(solution)/shard_map/query_part/pallas_call | solution.py:278
  24.4 1.6 %collective-permute-start.9 = (bf16[32,1536]{1,0:T(8,128)(2,1)S(1)}, bf16[32,1536]{1,0:T(8,128)(2,1)S(1)}, u32[]{:S(2)}, u32[]{:S(2)}) collective-permute-start(bf16[32,1536]{1,0:T(8,128)(2,1)S(1)} %slice.37), channel_id=1, source_target_pairs={{0,4},{2,6},{4,0},{6,2},{8,12},{10,14},{12,8},{14,10},{16,20},{18,... | collective-permute-start | bytes 294920 | tf_op jit(solution)/shard_map/ppermute | solution.py:25
  26.0 1.5 %collective-permute-start.10 = (bf16[128,1536]{1,0:T(8,128)(2,1)S(1)}, bf16[128,1536]{1,0:T(8,128)(2,1)S(1)}, u32[]{:S(2)}, u32[]{:S(2)}) collective-permute-start(bf16[128,1536]{1,0:T(8,128)(2,1)S(1)} %get-tuple-element.71), channel_id=1, source_target_pairs={{1,0},{0,1},{3,2},{2,3},{5,4},{4,5},{7,6},{6,7},{9,8},{8,9},{11,10... | collective-permute-start | bytes 1179656 | tf_op jit(solution)/shard_map/ppermute | solution.py:29
  27.5 2.0 %pool_grad.2.refs_2_ = f32[1024,1536]{1,0:T(8,128)} custom-call(bf16[256,1536]{1,0:T(8,128)(2,1)S(1)} %join_queries.1.all_q_ref.q_ref, bf16[1024,128]{1,0:T(8,128)(2,1)S(1)} %get-tuple-element.66.refs_0_, bf16[1024,128]{1,0:T(8,128)(2,1)S(1)} %get-tuple-element.67.refs_1_), custom_call_target="tpu_custom_call" | custom-call | bytes 73800000 | tf_op jit(solution)/shard_map/pool_grad/pallas_call | solution.py:314
  29.4 0.2 collective-permute-done.9
  29.7 2.7 %collective-permute-start.11 = (bf16[8,1536]{1,0:T(8,128)(2,1)S(1)}, bf16[8,1536]{1,0:T(8,128)(2,1)S(1)}, u32[]{:S(2)}, u32[]{:S(2)}) collective-permute-start(bf16[8,1536]{1,0:T(8,128)(2,1)S(1)} %get-tuple-element.75), channel_id=1, source_target_pairs={{0,24},{2,26},{4,28},{6,30},{8,16},{10,18},{12,20},{14,22},{16,8},... | collective-permute-start | bytes 73736 | tf_op jit(solution)/shard_map/ppermute | solution.py:25
  32.4 0.4 %collective-permute-start.13 = (bf16[8,1536]{1,0:T(8,128)(2,1)S(1)}, bf16[8,1536]{1,0:T(8,128)(2,1)S(1)}, u32[]{:S(2)}, u32[]{:S(2)}) collective-permute-start(bf16[8,1536]{1,0:T(8,128)(2,1)S(1)} %get-tuple-element.76), channel_id=1, source_target_pairs={{0,8},{2,10},{4,12},{6,14},{8,0},{10,2},{12,4},{14,6},{16,24},{18,... | collective-permute-start | bytes 73736 | tf_op jit(solution)/shard_map/ppermute | solution.py:25
  32.9 1.3 %collective-permute-start.12 = (bf16[8,1536]{1,0:T(8,128)(2,1)S(1)}, bf16[8,1536]{1,0:T(8,128)(2,1)S(1)}, u32[]{:S(2)}, u32[]{:S(2)}) collective-permute-start(bf16[8,1536]{1,0:T(8,128)(2,1)S(1)} %get-tuple-element.77), channel_id=1, source_target_pairs={{0,16},{2,18},{4,20},{6,22},{8,24},{10,26},{12,28},{14,30},{16,0},... | collective-permute-start | bytes 73736 | tf_op jit(solution)/shard_map/ppermute | solution.py:25
  34.2 2.0 %pool_grad.3 = f32[1024,1536]{1,0:T(8,128)} custom-call(bf16[256,1536]{1,0:T(8,128)(2,1)S(1)} %join_queries.1.all_q_ref.q_ref, bf16[1024,128]{1,0:T(8,128)(2,1)S(1)} %get-tuple-element.66.refs_0_, bf16[1024,128]{1,0:T(8,128)(2,1)S(1)} %get-tuple-element.67.refs_1_, f32[1024,1536]{1,0:T(8,128)} %pool_grad.2.refs_2_), custom_call_target="tpu_custom_call", output_to_operand_aliasing={{}: (3, {})} | custom-call | bytes 73800000 | tf_op jit(solution)/shard_map/pool_grad/pallas_call | solution.py:314
  36.2 1.1 %collective-permute-done.10.refs_1_ = bf16[128,1536]{1,0:T(8,128)(2,1)S(1)} collective-permute-done((bf16[128,1536]{1,0:T(8,128)(2,1)S(1)}, bf16[128,1536]{1,0:T(8,128)(2,1)S(1)}, u32[]{:S(2)}, u32[]{:S(2)}) %collective-permute-start.10) | collective-permute-done | bytes 393248 | tf_op jit(solution)/shard_map/ppermute | solution.py:29
  37.2 0.9 %query_grad.1 = f32[128,1536]{1,0:T(8,128)} custom-call(f32[128,1536]{1,0:T(8,128)S(1)} %get-tuple-element.70.refs_0_, bf16[128,1536]{1,0:T(8,128)(2,1)S(1)} %collective-permute-done.10.refs_1_), custom_call_target="tpu_custom_call" | custom-call | bytes 73800000 | tf_op jit(solution)/shard_map/query_grad/pallas_call | solution.py:348
  38.2 0.6 %add_add_fusion = f32[8,1536]{1,0:T(8,128)} fusion(bf16[8,1536]{1,0:T(8,128)(2,1)S(1)} %collective-permute-done.13, bf16[8,1536]{1,0:T(8,128)(2,1)S(1)} %collective-permute-done.12, bf16[8,1536]{1,0:T(8,128)(2,1)S(1)} %collective-permute-done.11, f32[32,1536]{1,0:T(8,128)S(1)} %convert_add_fusion.1), kind=kLoop, calls=%fused_computation.6 | loop fusion | flops 73728 | bytes 172032 | tf_op jit(solution)/shard_map/add | solution.py:431
  (16 shorter events, 0.2 us)
Async XLA Ops:
  0.6 10.1 %collective-permute-start = (bf16[8,1536]{1,0:T(8,128)(2,1)}, bf16[8,1536]{1,0:T(8,128)(2,1)S(1)}, u32[]{:S(2)}, u32[]{:S(2)}) collective-permute-start(bf16[8,1536]{1,0:T(8,128)(2,1)} %tile_ref.1), channel_id=1, source_target_pairs={{0,8},{2,10},{4,12},{6,14},{8,0},{10,2},{12,4},{14,6},{16,24},{18,... | collective-permute-start | bytes 73736 | tf_op jit(solution)/shard_map/ppermute | solution.py:25
  3.7 7.0 %collective-permute-start.2 = (bf16[8,1536]{1,0:T(8,128)(2,1)}, bf16[8,1536]{1,0:T(8,128)(2,1)S(1)}, u32[]{:S(2)}, u32[]{:S(2)}) collective-permute-start(bf16[8,1536]{1,0:T(8,128)(2,1)} %tile_ref.1), channel_id=1, source_target_pairs={{0,24},{2,26},{4,28},{6,30},{8,16},{10,18},{12,20},{14,22},{16,8},... | collective-permute-start | bytes 73736 | tf_op jit(solution)/shard_map/ppermute | solution.py:25
  6.2 5.2 %collective-permute-start.1 = (bf16[8,1536]{1,0:T(8,128)(2,1)}, bf16[8,1536]{1,0:T(8,128)(2,1)S(1)}, u32[]{:S(2)}, u32[]{:S(2)}) collective-permute-start(bf16[8,1536]{1,0:T(8,128)(2,1)} %tile_ref.1), channel_id=1, source_target_pairs={{0,16},{2,18},{4,20},{6,22},{8,24},{10,26},{12,28},{14,30},{16,0},... | collective-permute-start | bytes 73736 | tf_op jit(solution)/shard_map/ppermute | solution.py:25
  6.3 10.5 %collective-permute-start.4 = (bf16[128,1536]{1,0:T(8,128)(2,1)}, bf16[128,1536]{1,0:T(8,128)(2,1)S(1)}, u32[]{:S(2)}, u32[]{:S(2)}) collective-permute-start(bf16[128,1536]{1,0:T(8,128)(2,1)} %q_ref.1), channel_id=1, source_target_pairs={{1,0},{0,1},{3,2},{2,3},{5,4},{4,5},{7,6},{6,7},{9,8},{8,9},{11,10... | collective-permute-start | bytes 1179656 | tf_op jit(solution)/shard_map/ppermute | solution.py:29
  11.4 4.7 %collective-permute-start.3 = (bf16[32,1536]{1,0:T(8,128)(2,1)S(1)}, bf16[32,1536]{1,0:T(8,128)(2,1)S(1)}, u32[]{:S(2)}, u32[]{:S(2)}) collective-permute-start(bf16[32,1536]{1,0:T(8,128)(2,1)S(1)} %pad_maximum_fusion.2), channel_id=1, source_target_pairs={{0,4},{2,6},{4,0},{6,2},{8,12},{10,14},{12,8},{14,10},{16,20},{18,... | collective-permute-start | bytes 294920 | tf_op jit(solution)/shard_map/ppermute | solution.py:25
  13.0 3.9 %collective-permute-start.5 = (s32[8,128]{1,0:T(8,128)S(1)}, s32[8,128]{1,0:T(8,128)S(1)}, u32[]{:S(2)}, u32[]{:S(2)}) collective-permute-start(s32[8,128]{1,0:T(8,128)S(1)} %get-tuple-element.52.refs_0_), channel_id=1, source_target_pairs={{1,0},{0,1},{3,2},{2,3},{5,4},{4,5},{7,6},{6,7},{9,8},{8,9},{11,10... | collective-permute-start | bytes 12296 | tf_op jit(solution)/shard_map/ppermute | solution.py:29
  16.9 1.5 %collective-permute-start.6 = (bf16[64,1536]{1,0:T(8,128)(2,1)S(1)}, bf16[64,1536]{1,0:T(8,128)(2,1)S(1)}, u32[]{:S(2)}, u32[]{:S(2)}) collective-permute-start(bf16[64,1536]{1,0:T(8,128)(2,1)S(1)} %pad_maximum_fusion.1), channel_id=1, source_target_pairs={{0,2},{2,0},{4,6},{6,4},{8,10},{10,8},{12,14},{14,12},{16,18},{18,... | collective-permute-start | bytes 589832 | tf_op jit(solution)/shard_map/ppermute | solution.py:25
  18.8 3.6 %collective-permute-start.7 = (f32[2,256]{1,0:T(2,128)S(1)}, f32[2,256]{1,0:T(2,128)S(1)}, u32[]{:S(2)}, u32[]{:S(2)}) collective-permute-start(f32[2,256]{1,0:T(2,128)S(1)} %get-tuple-element.51.part_ref), channel_id=1, source_target_pairs={{1,0},{0,1},{3,2},{2,3},{5,4},{4,5},{7,6},{6,7},{9,8},{8,9},{11,10... | collective-permute-start | bytes 6152 | tf_op jit(solution)/shard_map/ppermute | solution.py:29
  22.8 1.5 %collective-permute-start.8 = (bf16[64,1536]{1,0:T(8,128)(2,1)S(1)}, bf16[64,1536]{1,0:T(8,128)(2,1)S(1)}, u32[]{:S(2)}, u32[]{:S(2)}) collective-permute-start(bf16[64,1536]{1,0:T(8,128)(2,1)S(1)} %get-tuple-element.54), channel_id=1, source_target_pairs={{0,2},{2,0},{4,6},{6,4},{8,10},{10,8},{12,14},{14,12},{16,18},{18,... | collective-permute-start | bytes 589832 | tf_op jit(solution)/shard_map/ppermute | solution.py:25
  24.4 5.3 %collective-permute-start.9 = (bf16[32,1536]{1,0:T(8,128)(2,1)S(1)}, bf16[32,1536]{1,0:T(8,128)(2,1)S(1)}, u32[]{:S(2)}, u32[]{:S(2)}) collective-permute-start(bf16[32,1536]{1,0:T(8,128)(2,1)S(1)} %slice.37), channel_id=1, source_target_pairs={{0,4},{2,6},{4,0},{6,2},{8,12},{10,14},{12,8},{14,10},{16,20},{18,... | collective-permute-start | bytes 294920 | tf_op jit(solution)/shard_map/ppermute | solution.py:25
  26.0 11.2 %collective-permute-start.10 = (bf16[128,1536]{1,0:T(8,128)(2,1)S(1)}, bf16[128,1536]{1,0:T(8,128)(2,1)S(1)}, u32[]{:S(2)}, u32[]{:S(2)}) collective-permute-start(bf16[128,1536]{1,0:T(8,128)(2,1)S(1)} %get-tuple-element.71), channel_id=1, source_target_pairs={{1,0},{0,1},{3,2},{2,3},{5,4},{4,5},{7,6},{6,7},{9,8},{8,9},{11,10... | collective-permute-start | bytes 1179656 | tf_op jit(solution)/shard_map/ppermute | solution.py:29
  29.7 8.5 %collective-permute-start.11 = (bf16[8,1536]{1,0:T(8,128)(2,1)S(1)}, bf16[8,1536]{1,0:T(8,128)(2,1)S(1)}, u32[]{:S(2)}, u32[]{:S(2)}) collective-permute-start(bf16[8,1536]{1,0:T(8,128)(2,1)S(1)} %get-tuple-element.75), channel_id=1, source_target_pairs={{0,24},{2,26},{4,28},{6,30},{8,16},{10,18},{12,20},{14,22},{16,8},... | collective-permute-start | bytes 73736 | tf_op jit(solution)/shard_map/ppermute | solution.py:25
  32.4 5.8 %collective-permute-start.13 = (bf16[8,1536]{1,0:T(8,128)(2,1)S(1)}, bf16[8,1536]{1,0:T(8,128)(2,1)S(1)}, u32[]{:S(2)}, u32[]{:S(2)}) collective-permute-start(bf16[8,1536]{1,0:T(8,128)(2,1)S(1)} %get-tuple-element.76), channel_id=1, source_target_pairs={{0,8},{2,10},{4,12},{6,14},{8,0},{10,2},{12,4},{14,6},{16,24},{18,... | collective-permute-start | bytes 73736 | tf_op jit(solution)/shard_map/ppermute | solution.py:25
  32.9 5.3 %collective-permute-start.12 = (bf16[8,1536]{1,0:T(8,128)(2,1)S(1)}, bf16[8,1536]{1,0:T(8,128)(2,1)S(1)}, u32[]{:S(2)}, u32[]{:S(2)}) collective-permute-start(bf16[8,1536]{1,0:T(8,128)(2,1)S(1)} %get-tuple-element.77), channel_id=1, source_target_pairs={{0,16},{2,18},{4,20},{6,22},{8,24},{10,26},{12,28},{14,30},{16,0},... | collective-permute-start | bytes 73736 | tf_op jit(solution)/shard_map/ppermute | solution.py:25

commit v7 on v6

--- a/solution.py
+++ b/solution.py
@@ -417,7 +417,7 @@
                 shifted(grad, "shard", owners, owners - d) for d, (grad, _) in enumerate(made, 1)
             ]
             hard_w = [own_w] + [hw for _, hw in made]
-    part = neg_pool.shape[0] // 2
+    part = 3 * neg_pool.shape[0] // 8
     pool_grad = pool_rows_grad(0, part, all_q, hard_w, None, 20)
     passage_grad, pool_grad = after(passage_grad, pool_grad)
     sent = passage_grad[tile:].astype(BF16)

time: 39 us -> 39 us (level)
  no operation moved by 1% of the time
where the time goes in v7:
time: 39 us; the launch traced here: 38.8 us
  starting transfers between devices  19.5 us (50%)
  Pallas kernels  11.1 us (28%)
  waiting for transfers between devices  6.66 us (17%)
  between operations  0.83 us (2%)
  other arithmetic  0.75 us (2%)
    ppermute x10, starting transfers between devices, across(): return lax.ppermute(x, axis, [(i, i ^ distance) for i in range(count)])  13.4 us
    ppermute x4, starting transfers between devices, shifted(): lax.ppermute(x, axis, [((i + distance) % count, i) for i in range(count)])  6.02 us
    pallas_call x2, Pallas kernels, pool_rows_grad(): pl.pallas_call(functools.partial(pool_kernel, first, chunk, features ** (...  3.96 us
    ppermute x4, waiting for transfers between devices, shifted(): lax.ppermute(x, axis, [((i + distance) % count, i) for i in range(count)])  3.65 us
    ppermute x10, waiting for transfers between devices, across(): return lax.ppermute(x, axis, [(i, i ^ distance) for i in range(count)])  3.02 us
    pallas_call x1, Pallas kernels, own_scores(): pl.pallas_call(functools.partial(own_kernel, chunk, features ** (-0.5)),...  2.94 us
    pallas_call x2, Pallas kernels, query_part(): pl.pallas_call(functools.partial(query_kernel, piece, features ** (-0.5))...  1.43 us
    pallas_call x1, Pallas kernels, group_scores(): pl.pallas_call(functools.partial(group_kernel, piece, min(pool_rows, 128)...  1.11 us
  transfers between devices with their start and end apart: 14, of which 7 were waited for; matrix products, arithmetic and copies ran while one was open for 0% of the time, Pallas kernels for 27%

profile of v7, /device:TPU:0, one launch (start us, length us, event | category | flops | bytes accessed | tf_op | source)
XLA Modules:
  0.0 38.8 jit_solution(9566309120244626682)
XLA Ops:
  0.6 3.1 %collective-permute-start = (bf16[8,1536]{1,0:T(8,128)(2,1)}, bf16[8,1536]{1,0:T(8,128)(2,1)S(1)}, u32[]{:S(2)}, u32[]{:S(2)}) collective-permute-start(bf16[8,1536]{1,0:T(8,128)(2,1)} %tile_ref.1), channel_id=1, source_target_pairs={{0,8},{2,10},{4,12},{6,14},{8,0},{10,2},{12,4},{14,6},{16,24},{18,... | collective-permute-start | bytes 73736 | tf_op jit(solution)/shard_map/ppermute | solution.py:25
  3.7 2.5 %collective-permute-start.2 = (bf16[8,1536]{1,0:T(8,128)(2,1)}, bf16[8,1536]{1,0:T(8,128)(2,1)S(1)}, u32[]{:S(2)}, u32[]{:S(2)}) collective-permute-start(bf16[8,1536]{1,0:T(8,128)(2,1)} %tile_ref.1), channel_id=1, source_target_pairs={{0,24},{2,26},{4,28},{6,30},{8,16},{10,18},{12,20},{14,22},{16,8},... | collective-permute-start | bytes 73736 | tf_op jit(solution)/shard_map/ppermute | solution.py:25
  6.2 0.1 collective-permute-start.1
  6.3 1.5 %collective-permute-start.4 = (bf16[128,1536]{1,0:T(8,128)(2,1)}, bf16[128,1536]{1,0:T(8,128)(2,1)S(1)}, u32[]{:S(2)}, u32[]{:S(2)}) collective-permute-start(bf16[128,1536]{1,0:T(8,128)(2,1)} %q_ref.1), channel_id=1, source_target_pairs={{1,0},{0,1},{3,2},{2,3},{5,4},{4,5},{7,6},{6,7},{9,8},{8,9},{11,10... | collective-permute-start | bytes 1179656 | tf_op jit(solution)/shard_map/ppermute | solution.py:29
  7.8 2.9 %own_scores.1 = (bf16[8,1536]{1,0:T(8,128)(2,1)S(1)}, bf16[128,1536]{1,0:T(8,128)(2,1)S(1)}, bf16[1024,1536]{1,0:T(8,128)(2,1)S(1)}, s32[8,128]{1,0:T(8,128)S(1)...) custom-call(s32[7,128]{1,0:T(8,128)} %bitcast.2, ...), custom_call_target="tpu_custom_call" | custom-call | bytes 73800000 | tf_op jit(solution)/shard_map/own_scores/pallas_call | solution.py:123
  10.8 0.6 %collective-permute-done.1 = bf16[8,1536]{1,0:T(8,128)(2,1)S(1)} collective-permute-done((bf16[8,1536]{1,0:T(8,128)(2,1)}, bf16[8,1536]{1,0:T(8,128)(2,1)S(1)}, u32[]{:S(2)}, u32[]{:S(2)}) %collective-permute-start.1) | collective-permute-done | bytes 24608 | tf_op jit(solution)/shard_map/ppermute | solution.py:25
  11.4 1.6 %collective-permute-start.3 = (bf16[32,1536]{1,0:T(8,128)(2,1)S(1)}, bf16[32,1536]{1,0:T(8,128)(2,1)S(1)}, u32[]{:S(2)}, u32[]{:S(2)}) collective-permute-start(bf16[32,1536]{1,0:T(8,128)(2,1)S(1)} %pad_maximum_fusion.2), channel_id=1, source_target_pairs={{0,4},{2,6},{4,0},{6,2},{8,12},{10,14},{12,8},{14,10},{16,20},{18,... | collective-permute-start | bytes 294920 | tf_op jit(solution)/shard_map/ppermute | solution.py:25
  13.0 1.5 %collective-permute-start.5 = (s32[8,128]{1,0:T(8,128)S(1)}, s32[8,128]{1,0:T(8,128)S(1)}, u32[]{:S(2)}, u32[]{:S(2)}) collective-permute-start(s32[8,128]{1,0:T(8,128)S(1)} %get-tuple-element.52.refs_0_), channel_id=1, source_target_pairs={{1,0},{0,1},{3,2},{2,3},{5,4},{4,5},{7,6},{6,7},{9,8},{8,9},{11,10... | collective-permute-start | bytes 12296 | tf_op jit(solution)/shard_map/ppermute | solution.py:29
  14.5 1.6 %collective-permute-done.3 = bf16[32,1536]{1,0:T(8,128)(2,1)S(1)} collective-permute-done((bf16[32,1536]{1,0:T(8,128)(2,1)S(1)}, bf16[32,1536]{1,0:T(8,128)(2,1)S(1)}, u32[]{:S(2)}, u32[]{:S(2)}) %collective-permute-start.3) | collective-permute-done | bytes 98336 | tf_op jit(solution)/shard_map/ppermute | solution.py:25
  16.1 0.8 %collective-permute-done.4.refs_1_ = bf16[128,1536]{1,0:T(8,128)(2,1)S(1)} collective-permute-done((bf16[128,1536]{1,0:T(8,128)(2,1)}, bf16[128,1536]{1,0:T(8,128)(2,1)S(1)}, u32[]{:S(2)}, u32[]{:S(2)}) %collective-permute-start.4) | collective-permute-done | bytes 393248 | tf_op jit(solution)/shard_map/ppermute | solution.py:29
  16.9 0.1 join_queries.1.all_q_ref.q_ref
  16.9 0.1 collective-permute-start.6
  17.0 1.1 %group_scores.1 = (bf16[1536,128]{1,0:T(8,128)(2,1)S(1)}, f32[1024,128]{1,0:T(8,128)S(1)}, f32[1024,128]{1,0:T(8,128)S(1)}, f32[2,128]{1,0:T(2,128)S(1)}) custom-call(s32[8,128]{1,0:T(8,128)S(1)} %collective-permute-done.5.marks_ref.refs_1_, bf16[256,1536]{1,0:T(8,128)(2,1)S(1)} %join_queries.1.all_q_ref.q_ref, bf16[1024,1536]{1,0:T(8,128)(2,1)S(1)} %get-tuple-element.46.pool_ref), custom_call_target="tpu_custom_call" | custom-call | bytes 73800000 | tf_op jit(solution)/shard_map/group_scores/pallas_call | solution.py:175
  18.1 0.3 collective-permute-done.6
  18.5 0.3 passage_scores.1
  18.8 1.6 %collective-permute-start.7 = (f32[2,256]{1,0:T(2,128)S(1)}, f32[2,256]{1,0:T(2,128)S(1)}, u32[]{:S(2)}, u32[]{:S(2)}) collective-permute-start(f32[2,256]{1,0:T(2,128)S(1)} %get-tuple-element.51.part_ref), channel_id=1, source_target_pairs={{1,0},{0,1},{3,2},{2,3},{5,4},{4,5},{7,6},{6,7},{9,8},{8,9},{11,10... | collective-permute-start | bytes 6152 | tf_op jit(solution)/shard_map/ppermute | solution.py:29
  20.4 2.1 %collective-permute-done.7.other_ref = f32[2,256]{1,0:T(2,128)S(1)} collective-permute-done((f32[2,256]{1,0:T(2,128)S(1)}, f32[2,256]{1,0:T(2,128)S(1)}, u32[]{:S(2)}, u32[]{:S(2)}) %collective-permute-start.7) | collective-permute-done | bytes 2080 | tf_op jit(solution)/shard_map/ppermute | solution.py:29
  22.5 0.3 passage_weights.1
  22.8 0.1 collective-permute-start.8
  22.9 0.7 %query_part.2 = (bf16[128,1536]{1,0:T(8,128)(2,1)S(1)}, bf16[1024,128]{1,0:T(8,128)(2,1)S(1)}) custom-call(f32[1024,128]{1,0:T(8,128)S(1)} %get-tuple-element.55.hard_ref, f32[1024,128]{1,0:T(8,128)S(1)} %get-tuple-element.56.times_ref, f32[1,256]{1,0:T(1,128)S(1)} %get-tuple-element.57.log_ref, bf16[128,256]{1,0:T(8,128)(2,1)S(1)} %get-tuple-element.58.w_ref, ...), custom_call_target="tpu_custom_call" | custom-call | bytes 36900000 | tf_op jit(solution)/shard_map/query_part/pallas_call | solution.py:278
  23.6 0.7 %query_part.3 = (f32[128,1536]{1,0:T(8,128)S(1)}, bf16[1024,128]{1,0:T(8,128)(2,1)S(1)}) custom-call(f32[1024,128]{1,0:T(8,128)S(1)} %get-tuple-element.61.hard_ref, f32[1024,128]{1,0:T(8,128)S(1)} %get-tuple-element.62.times_ref, f32[1,256]{1,0:T(1,128)S(1)} %get-tuple-element.57.log_ref, bf16[128,256]{1,0:T(8,128)(2,1)S(1)} %get-tuple-element.58.w_ref, ...), custom_call_target="tpu_custom_call" | custom-call | bytes 36900000 | tf_op jit(solution)/shard_map/query_part/pallas_call | solution.py:278
  24.4 1.6 %collective-permute-start.9 = (bf16[32,1536]{1,0:T(8,128)(2,1)S(1)}, bf16[32,1536]{1,0:T(8,128)(2,1)S(1)}, u32[]{:S(2)}, u32[]{:S(2)}) collective-permute-start(bf16[32,1536]{1,0:T(8,128)(2,1)S(1)} %slice.37), channel_id=1, source_target_pairs={{0,4},{2,6},{4,0},{6,2},{8,12},{10,14},{12,8},{14,10},{16,20},{18,... | collective-permute-start | bytes 294920 | tf_op jit(solution)/shard_map/ppermute | solution.py:25
  26.0 1.5 %collective-permute-start.10 = (bf16[128,1536]{1,0:T(8,128)(2,1)S(1)}, bf16[128,1536]{1,0:T(8,128)(2,1)S(1)}, u32[]{:S(2)}, u32[]{:S(2)}) collective-permute-start(bf16[128,1536]{1,0:T(8,128)(2,1)S(1)} %get-tuple-element.71), channel_id=1, source_target_pairs={{1,0},{0,1},{3,2},{2,3},{5,4},{4,5},{7,6},{6,7},{9,8},{8,9},{11,10... | collective-permute-start | bytes 1179656 | tf_op jit(solution)/shard_map/ppermute | solution.py:29
  27.5 1.7 %pool_grad.2.refs_2_ = f32[1024,1536]{1,0:T(8,128)} custom-call(bf16[256,1536]{1,0:T(8,128)(2,1)S(1)} %join_queries.1.all_q_ref.q_ref, bf16[1024,128]{1,0:T(8,128)(2,1)S(1)} %get-tuple-element.66.refs_0_, bf16[1024,128]{1,0:T(8,128)(2,1)S(1)} %get-tuple-element.67.refs_1_), custom_call_target="tpu_custom_call" | custom-call | bytes 73800000 | tf_op jit(solution)/shard_map/pool_grad/pallas_call | solution.py:314
  29.2 0.5 %collective-permute-done.9 = bf16[32,1536]{1,0:T(8,128)(2,1)S(1)} collective-permute-done((bf16[32,1536]{1,0:T(8,128)(2,1)S(1)}, bf16[32,1536]{1,0:T(8,128)(2,1)S(1)}, u32[]{:S(2)}, u32[]{:S(2)}) %collective-permute-start.9) | collective-permute-done | bytes 98336 | tf_op jit(solution)/shard_map/ppermute | solution.py:25
  29.7 2.7 %collective-permute-start.11 = (bf16[8,1536]{1,0:T(8,128)(2,1)S(1)}, bf16[8,1536]{1,0:T(8,128)(2,1)S(1)}, u32[]{:S(2)}, u32[]{:S(2)}) collective-permute-start(bf16[8,1536]{1,0:T(8,128)(2,1)S(1)} %get-tuple-element.75), channel_id=1, source_target_pairs={{0,24},{2,26},{4,28},{6,30},{8,16},{10,18},{12,20},{14,22},{16,8},... | collective-permute-start | bytes 73736 | tf_op jit(solution)/shard_map/ppermute | solution.py:25
  32.4 0.4 %collective-permute-start.13 = (bf16[8,1536]{1,0:T(8,128)(2,1)S(1)}, bf16[8,1536]{1,0:T(8,128)(2,1)S(1)}, u32[]{:S(2)}, u32[]{:S(2)}) collective-permute-start(bf16[8,1536]{1,0:T(8,128)(2,1)S(1)} %get-tuple-element.76), channel_id=1, source_target_pairs={{0,8},{2,10},{4,12},{6,14},{8,0},{10,2},{12,4},{14,6},{16,24},{18,... | collective-permute-start | bytes 73736 | tf_op jit(solution)/shard_map/ppermute | solution.py:25
  32.9 1.3 %collective-permute-start.12 = (bf16[8,1536]{1,0:T(8,128)(2,1)S(1)}, bf16[8,1536]{1,0:T(8,128)(2,1)S(1)}, u32[]{:S(2)}, u32[]{:S(2)}) collective-permute-start(bf16[8,1536]{1,0:T(8,128)(2,1)S(1)} %get-tuple-element.77), channel_id=1, source_target_pairs={{0,16},{2,18},{4,20},{6,22},{8,24},{10,26},{12,28},{14,30},{16,0},... | collective-permute-start | bytes 73736 | tf_op jit(solution)/shard_map/ppermute | solution.py:25
  34.2 2.2 %pool_grad.3 = f32[1024,1536]{1,0:T(8,128)} custom-call(bf16[256,1536]{1,0:T(8,128)(2,1)S(1)} %join_queries.1.all_q_ref.q_ref, bf16[1024,128]{1,0:T(8,128)(2,1)S(1)} %get-tuple-element.66.refs_0_, bf16[1024,128]{1,0:T(8,128)(2,1)S(1)} %get-tuple-element.67.refs_1_, f32[1024,1536]{1,0:T(8,128)} %pool_grad.2.refs_2_), custom_call_target="tpu_custom_call", output_to_operand_aliasing={{}: (3, {})} | custom-call | bytes 73800000 | tf_op jit(solution)/shard_map/pool_grad/pallas_call | solution.py:314
  36.4 0.8 %collective-permute-done.10.refs_1_ = bf16[128,1536]{1,0:T(8,128)(2,1)S(1)} collective-permute-done((bf16[128,1536]{1,0:T(8,128)(2,1)S(1)}, bf16[128,1536]{1,0:T(8,128)(2,1)S(1)}, u32[]{:S(2)}, u32[]{:S(2)}) %collective-permute-start.10) | collective-permute-done | bytes 393248 | tf_op jit(solution)/shard_map/ppermute | solution.py:29
  37.2 0.9 %query_grad.1 = f32[128,1536]{1,0:T(8,128)} custom-call(f32[128,1536]{1,0:T(8,128)S(1)} %get-tuple-element.70.refs_0_, bf16[128,1536]{1,0:T(8,128)(2,1)S(1)} %collective-permute-done.10.refs_1_), custom_call_target="tpu_custom_call" | custom-call | bytes 73800000 | tf_op jit(solution)/shard_map/query_grad/pallas_call | solution.py:348
  38.2 0.6 %add_add_fusion = f32[8,1536]{1,0:T(8,128)} fusion(bf16[8,1536]{1,0:T(8,128)(2,1)S(1)} %collective-permute-done.13, bf16[8,1536]{1,0:T(8,128)(2,1)S(1)} %collective-permute-done.12, bf16[8,1536]{1,0:T(8,128)(2,1)S(1)} %collective-permute-done.11, f32[32,1536]{1,0:T(8,128)S(1)} %convert_add_fusion.1), kind=kLoop, calls=%fused_computation.6 | loop fusion | flops 73728 | bytes 172032 | tf_op jit(solution)/shard_map/add | solution.py:431
  (16 shorter events, 0.2 us)
Async XLA Ops:
  0.6 10.1 %collective-permute-start = (bf16[8,1536]{1,0:T(8,128)(2,1)}, bf16[8,1536]{1,0:T(8,128)(2,1)S(1)}, u32[]{:S(2)}, u32[]{:S(2)}) collective-permute-start(bf16[8,1536]{1,0:T(8,128)(2,1)} %tile_ref.1), channel_id=1, source_target_pairs={{0,8},{2,10},{4,12},{6,14},{8,0},{10,2},{12,4},{14,6},{16,24},{18,... | collective-permute-start | bytes 73736 | tf_op jit(solution)/shard_map/ppermute | solution.py:25
  3.7 7.0 %collective-permute-start.2 = (bf16[8,1536]{1,0:T(8,128)(2,1)}, bf16[8,1536]{1,0:T(8,128)(2,1)S(1)}, u32[]{:S(2)}, u32[]{:S(2)}) collective-permute-start(bf16[8,1536]{1,0:T(8,128)(2,1)} %tile_ref.1), channel_id=1, source_target_pairs={{0,24},{2,26},{4,28},{6,30},{8,16},{10,18},{12,20},{14,22},{16,8},... | collective-permute-start | bytes 73736 | tf_op jit(solution)/shard_map/ppermute | solution.py:25
  6.2 5.2 %collective-permute-start.1 = (bf16[8,1536]{1,0:T(8,128)(2,1)}, bf16[8,1536]{1,0:T(8,128)(2,1)S(1)}, u32[]{:S(2)}, u32[]{:S(2)}) collective-permute-start(bf16[8,1536]{1,0:T(8,128)(2,1)} %tile_ref.1), channel_id=1, source_target_pairs={{0,16},{2,18},{4,20},{6,22},{8,24},{10,26},{12,28},{14,30},{16,0},... | collective-permute-start | bytes 73736 | tf_op jit(solution)/shard_map/ppermute | solution.py:25
  6.3 10.5 %collective-permute-start.4 = (bf16[128,1536]{1,0:T(8,128)(2,1)}, bf16[128,1536]{1,0:T(8,128)(2,1)S(1)}, u32[]{:S(2)}, u32[]{:S(2)}) collective-permute-start(bf16[128,1536]{1,0:T(8,128)(2,1)} %q_ref.1), channel_id=1, source_target_pairs={{1,0},{0,1},{3,2},{2,3},{5,4},{4,5},{7,6},{6,7},{9,8},{8,9},{11,10... | collective-permute-start | bytes 1179656 | tf_op jit(solution)/shard_map/ppermute | solution.py:29
  11.4 4.7 %collective-permute-start.3 = (bf16[32,1536]{1,0:T(8,128)(2,1)S(1)}, bf16[32,1536]{1,0:T(8,128)(2,1)S(1)}, u32[]{:S(2)}, u32[]{:S(2)}) collective-permute-start(bf16[32,1536]{1,0:T(8,128)(2,1)S(1)} %pad_maximum_fusion.2), channel_id=1, source_target_pairs={{0,4},{2,6},{4,0},{6,2},{8,12},{10,14},{12,8},{14,10},{16,20},{18,... | collective-permute-start | bytes 294920 | tf_op jit(solution)/shard_map/ppermute | solution.py:25
  13.0 3.9 %collective-permute-start.5 = (s32[8,128]{1,0:T(8,128)S(1)}, s32[8,128]{1,0:T(8,128)S(1)}, u32[]{:S(2)}, u32[]{:S(2)}) collective-permute-start(s32[8,128]{1,0:T(8,128)S(1)} %get-tuple-element.52.refs_0_), channel_id=1, source_target_pairs={{1,0},{0,1},{3,2},{2,3},{5,4},{4,5},{7,6},{6,7},{9,8},{8,9},{11,10... | collective-permute-start | bytes 12296 | tf_op jit(solution)/shard_map/ppermute | solution.py:29
  16.9 1.5 %collective-permute-start.6 = (bf16[64,1536]{1,0:T(8,128)(2,1)S(1)}, bf16[64,1536]{1,0:T(8,128)(2,1)S(1)}, u32[]{:S(2)}, u32[]{:S(2)}) collective-permute-start(bf16[64,1536]{1,0:T(8,128)(2,1)S(1)} %pad_maximum_fusion.1), channel_id=1, source_target_pairs={{0,2},{2,0},{4,6},{6,4},{8,10},{10,8},{12,14},{14,12},{16,18},{18,... | collective-permute-start | bytes 589832 | tf_op jit(solution)/shard_map/ppermute | solution.py:25
  18.8 3.6 %collective-permute-start.7 = (f32[2,256]{1,0:T(2,128)S(1)}, f32[2,256]{1,0:T(2,128)S(1)}, u32[]{:S(2)}, u32[]{:S(2)}) collective-permute-start(f32[2,256]{1,0:T(2,128)S(1)} %get-tuple-element.51.part_ref), channel_id=1, source_target_pairs={{1,0},{0,1},{3,2},{2,3},{5,4},{4,5},{7,6},{6,7},{9,8},{8,9},{11,10... | collective-permute-start | bytes 6152 | tf_op jit(solution)/shard_map/ppermute | solution.py:29
  22.8 1.5 %collective-permute-start.8 = (bf16[64,1536]{1,0:T(8,128)(2,1)S(1)}, bf16[64,1536]{1,0:T(8,128)(2,1)S(1)}, u32[]{:S(2)}, u32[]{:S(2)}) collective-permute-start(bf16[64,1536]{1,0:T(8,128)(2,1)S(1)} %get-tuple-element.54), channel_id=1, source_target_pairs={{0,2},{2,0},{4,6},{6,4},{8,10},{10,8},{12,14},{14,12},{16,18},{18,... | collective-permute-start | bytes 589832 | tf_op jit(solution)/shard_map/ppermute | solution.py:25
  24.4 5.3 %collective-permute-start.9 = (bf16[32,1536]{1,0:T(8,128)(2,1)S(1)}, bf16[32,1536]{1,0:T(8,128)(2,1)S(1)}, u32[]{:S(2)}, u32[]{:S(2)}) collective-permute-start(bf16[32,1536]{1,0:T(8,128)(2,1)S(1)} %slice.37), channel_id=1, source_target_pairs={{0,4},{2,6},{4,0},{6,2},{8,12},{10,14},{12,8},{14,10},{16,20},{18,... | collective-permute-start | bytes 294920 | tf_op jit(solution)/shard_map/ppermute | solution.py:25
  26.0 11.2 %collective-permute-start.10 = (bf16[128,1536]{1,0:T(8,128)(2,1)S(1)}, bf16[128,1536]{1,0:T(8,128)(2,1)S(1)}, u32[]{:S(2)}, u32[]{:S(2)}) collective-permute-start(bf16[128,1536]{1,0:T(8,128)(2,1)S(1)} %get-tuple-element.71), channel_id=1, source_target_pairs={{1,0},{0,1},{3,2},{2,3},{5,4},{4,5},{7,6},{6,7},{9,8},{8,9},{11,10... | collective-permute-start | bytes 1179656 | tf_op jit(solution)/shard_map/ppermute | solution.py:29
  29.7 8.5 %collective-permute-start.11 = (bf16[8,1536]{1,0:T(8,128)(2,1)S(1)}, bf16[8,1536]{1,0:T(8,128)(2,1)S(1)}, u32[]{:S(2)}, u32[]{:S(2)}) collective-permute-start(bf16[8,1536]{1,0:T(8,128)(2,1)S(1)} %get-tuple-element.75), channel_id=1, source_target_pairs={{0,24},{2,26},{4,28},{6,30},{8,16},{10,18},{12,20},{14,22},{16,8},... | collective-permute-start | bytes 73736 | tf_op jit(solution)/shard_map/ppermute | solution.py:25
  32.4 5.8 %collective-permute-start.13 = (bf16[8,1536]{1,0:T(8,128)(2,1)S(1)}, bf16[8,1536]{1,0:T(8,128)(2,1)S(1)}, u32[]{:S(2)}, u32[]{:S(2)}) collective-permute-start(bf16[8,1536]{1,0:T(8,128)(2,1)S(1)} %get-tuple-element.76), channel_id=1, source_target_pairs={{0,8},{2,10},{4,12},{6,14},{8,0},{10,2},{12,4},{14,6},{16,24},{18,... | collective-permute-start | bytes 73736 | tf_op jit(solution)/shard_map/ppermute | solution.py:25
  32.9 5.3 %collective-permute-start.12 = (bf16[8,1536]{1,0:T(8,128)(2,1)S(1)}, bf16[8,1536]{1,0:T(8,128)(2,1)S(1)}, u32[]{:S(2)}, u32[]{:S(2)}) collective-permute-start(bf16[8,1536]{1,0:T(8,128)(2,1)S(1)} %get-tuple-element.77), channel_id=1, source_target_pairs={{0,16},{2,18},{4,20},{6,22},{8,24},{10,26},{12,28},{14,30},{16,0},... | collective-permute-start | bytes 73736 | tf_op jit(solution)/shard_map/ppermute | solution.py:25
